TPU v7x, 256 devices: a whole 4x4x8 slice. The times are simulated.
256 devices in a mesh: energy: 64 (over x, z_hi, y, core), elem: 4 (over z_lo).
Axes of the slice: x: 4, y: 4, z: 8 (z_hi: 2, z_lo: 4; z = z_hi * 4 + z_lo), core: 2. Of those that a mesh axis runs over, the one named last changes fastest.
Arguments:
- green_lesser: float32 [2, 8192, 8192], P(None, 'elem', 'energy'), may hold values from -5 to 5
- green_greater: float32 [2, 8192, 8192], P(None, 'elem', 'energy'), may hold values from -5 to 5
- screen: float32 [8192], P('elem'), may hold values from 0.5 to 2
- couple: float32 [8192], P('elem'), may hold values from 0.2 to 1
Outputs:
- polarization: float32 [2, 8192, 8192], P(None, 'elem', 'energy')
- self_energy: float32 [2, 8192, 8192], P(None, 'elem', 'energy')
All inputs are finite; a program needn't handle non-finite values.
Results may differ from a plain program's by a relative error of at most 0.00013.
Values sent between devices are 32-bit elements; how exact they have to be, the bound alone decides.
No kernel may reach another device: no remote copies, remote signals or barrier semaphores. Data moves between devices by JAX's collectives and lax.ppermute only.
A program may use at most 128 MiB of HBM per device.

v0:
```python
import math

import jax
import jax.numpy as jnp
from jax import lax
from jax.sharding import PartitionSpec as P


def with_halo(x, sides, width):
    for axis, dim in sides:
        devices, length = (lax.axis_size(axis), x.shape[dim])
        up = [(i, (i + 1) % devices) for i in range(devices - 1)]
        down = [(j, i) for i, j in up]
        last = lax.slice_in_dim(x, length - width, length, axis=dim)
        initial = lax.slice_in_dim(x, 0, width, axis=dim)
        before = lax.ppermute(last, axis, up)
        after = lax.ppermute(initial, axis, down)
        x = jnp.concatenate([before, x, after], axis=dim)
    return x


def angle_table(row_count, col_count, modulus):
    first_axis = jnp.arange(row_count, dtype=jnp.int32)[:, None]
    second_axis = jnp.arange(col_count, dtype=jnp.int32)[None, :]
    phase_index = first_axis * second_axis % modulus
    angles = phase_index.astype(jnp.float32) * (2.0 * math.pi / modulus)
    return (jnp.cos(angles), jnp.sin(angles))


def product(pattern, left_side, right_side):
    return jnp.einsum(pattern, left_side, right_side, precision=lax.Precision.HIGHEST)


def all_tables(length):
    inner_len = min(128, length)
    outer_len = length // inner_len
    cos_outer, sin_outer = angle_table(outer_len, outer_len, outer_len)
    cos_twist, sin_twist = angle_table(outer_len, inner_len, length)
    cos_inner, sin_inner = angle_table(inner_len, inner_len, inner_len)
    return (outer_len, inner_len, cos_outer, sin_outer, cos_twist, sin_twist, cos_inner, sin_inner)


def forward(signal):
    length = signal.shape[2]
    outer_len, inner_len, cos_outer, sin_outer, cos_twist, sin_twist, cos_inner, sin_inner = (
        all_tables(length)
    )
    grid_form = signal.reshape(2, signal.shape[1], outer_len, inner_len)
    real_in = grid_form[0]
    imag_in = grid_form[1]
    first_real = product("ka,iab->ikb", cos_outer, real_in) + product(
        "ka,iab->ikb", sin_outer, imag_in
    )
    first_imag = product("ka,iab->ikb", cos_outer, imag_in) - product(
        "ka,iab->ikb", sin_outer, real_in
    )
    twist_real = first_real * cos_twist + first_imag * sin_twist
    twist_imag = first_imag * cos_twist - first_real * sin_twist
    out_real = product("ikb,bl->ikl", twist_real, cos_inner) + product(
        "ikb,bl->ikl", twist_imag, sin_inner
    )
    out_imag = product("ikb,bl->ikl", twist_imag, cos_inner) - product(
        "ikb,bl->ikl", twist_real, sin_inner
    )
    return jnp.stack([out_real, out_imag]).reshape(signal.shape)


def inverse(spectrum):
    length = spectrum.shape[2]
    outer_len, inner_len, cos_outer, sin_outer, cos_twist, sin_twist, cos_inner, sin_inner = (
        all_tables(length)
    )
    grid_form = spectrum.reshape(2, spectrum.shape[1], outer_len, inner_len)
    spec_real = grid_form[0]
    spec_imag = grid_form[1]
    step_real = product("ikl,bl->ikb", spec_real, cos_inner) - product(
        "ikl,bl->ikb", spec_imag, sin_inner
    )
    step_imag = product("ikl,bl->ikb", spec_imag, cos_inner) + product(
        "ikl,bl->ikb", spec_real, sin_inner
    )
    turn_real = step_real * cos_twist - step_imag * sin_twist
    turn_imag = step_imag * cos_twist + step_real * sin_twist
    back_real = product("ak,ikb->iab", cos_outer, turn_real) - product(
        "ak,ikb->iab", sin_outer, turn_imag
    )
    back_imag = product("ak,ikb->iab", cos_outer, turn_imag) + product(
        "ak,ikb->iab", sin_outer, turn_real
    )
    return jnp.stack([back_real, back_imag]).reshape(spectrum.shape) * (1.0 / length)


def times_unit(summed):
    norm_factor = summed.shape[2] ** (-0.5)
    return jnp.stack([-norm_factor * summed[1], norm_factor * summed[0]])


def polarization_items(green_pair):
    lesser, greater = green_pair
    spec_lesser = forward(lesser)
    spec_greater = forward(greater)
    corr_real = spec_lesser[0] * spec_greater[0] + spec_lesser[1] * spec_greater[1]
    corr_imag = spec_lesser[1] * spec_greater[0] - spec_lesser[0] * spec_greater[1]
    summed = inverse(jnp.stack([corr_real, corr_imag]))
    return (times_unit(summed), spec_lesser)


def polarization_blocks(green_pair):
    lesser, greater = green_pair
    item_count = lesser.shape[2]
    length = lesser.shape[3]
    polar, spec_lesser = polarization_items(
        (lesser.reshape(2, item_count, length), greater.reshape(2, item_count, length))
    )
    return (polar.reshape(2, 1, item_count, length), spec_lesser.reshape(2, 1, item_count, length))


def self_energy_items(screened, spec_lesser):
    spec_weights = forward(screened)
    conv_real = spec_lesser[0] * spec_weights[0] - spec_lesser[1] * spec_weights[1]
    conv_imag = spec_lesser[0] * spec_weights[1] + spec_lesser[1] * spec_weights[0]
    summed = inverse(jnp.stack([conv_real, conv_imag]))
    return times_unit(summed)


def couple_rows(beside_all, screen_part, couple_part):
    return screen_part[:, None] * beside_all[1] + couple_part[:, None] * (
        beside_all[0] + beside_all[2]
    )


def shards(green_lesser, green_greater, screen, couple):
    group_count = lax.axis_size("energy")
    local_rows = green_lesser.shape[1]
    local_energies = green_lesser.shape[2]
    per_device = local_rows // group_count
    lesser_grouped = green_lesser.reshape(2, group_count, per_device, local_energies)
    greater_grouped = green_greater.reshape(2, group_count, per_device, local_energies)
    polar_blocks, spec_blocks = polarization_blocks(
        (
            lax.all_to_all(lesser_grouped, "energy", split_axis=1, concat_axis=3, tiled=True),
            lax.all_to_all(greater_grouped, "energy", split_axis=1, concat_axis=3, tiled=True),
        )
    )
    full_length = polar_blocks.shape[3]
    polar_el = polar_blocks.reshape(2, per_device, full_length)
    spec_lesser = spec_blocks.reshape(2, per_device, full_length)
    polar_en = lax.all_to_all(polar_el, "energy", split_axis=2, concat_axis=1, tiled=True)
    beside_all = with_halo(polar_en[None], (("elem", 0),), 1)
    screened_en = couple_rows(beside_all, screen, couple)
    screened_el = lax.all_to_all(screened_en, "energy", split_axis=1, concat_axis=2, tiled=True)
    sigma_el = self_energy_items(screened_el, spec_lesser)
    sigma_en = lax.all_to_all(sigma_el, "energy", split_axis=2, concat_axis=1, tiled=True)
    return (polar_en, sigma_en)


def solution(mesh):
    placed = (P(None, "elem", "energy"), P(None, "elem", "energy"), P("elem"), P("elem"))
    return jax.shard_map(
        shards,
        mesh=mesh,
        in_specs=placed,
        out_specs=(P(None, "elem", "energy"), P(None, "elem", "energy")),
        check_vma=False,
    )
```

profile of v0, /device:TPU:33, one launch (start us, length us, event | category | flops | bytes accessed | tf_op | source)
XLA Modules:
  0.0 517.3 jit_solution(7944901628702181092)
XLA Ops:
  0.6 3.2 copy.27
  3.8 13.9 %all-to-all-start = ((f32[2,64,32,128]{3,2,0,1:T(8,128)}), f32[2,64,32,128]{3,2,0,1:T(8,128)S(1)}, u32[]{:S(2)}, u32[]{:S(2)}) async-start(f32[2,64,32,128]{3,2,0,1:T(8,128)} %copy.27), calls=%async_computation | async-start | bytes 4194304 | tf_op jit(solution)/shard_map/all_to_all | solution.py:141
  17.7 3.2 copy.29
  20.8 52.1 %all-to-all-done = f32[2,64,32,128]{3,2,0,1:T(8,128)S(1)} async-done(((f32[2,64,32,128]{3,2,0,1:T(8,128)}), f32[2,64,32,128]{3,2,0,1:T(8,128)S(1)}, u32[]{:S(2)}, u32[]{:S(2)}) %all-to-all-start) | async-done | bytes 2097184 | tf_op jit(solution)/shard_map/all_to_all | solution.py:141
  72.9 5.3 %all-to-all-start.1 = ((f32[2,64,32,128]{3,2,0,1:T(8,128)}), f32[2,64,32,128]{3,2,0,1:T(8,128)}, u32[]{:S(2)}, u32[]{:S(2)}) async-start(f32[2,64,32,128]{3,2,0,1:T(8,128)} %copy.29), calls=%async_computation.1 | async-start | bytes 4194304 | tf_op jit(solution)/shard_map/all_to_all | solution.py:142
  88.7 43.3 %all-to-all-done.1 = f32[2,64,32,128]{3,2,0,1:T(8,128)} async-done(((f32[2,64,32,128]{3,2,0,1:T(8,128)}), f32[2,64,32,128]{3,2,0,1:T(8,128)}, u32[]{:S(2)}, u32[]{:S(2)}) %all-to-all-start.1) | async-done | bytes 2097184 | tf_op jit(solution)/shard_map/all_to_all | solution.py:142
  132.0 2.8 copy.45
  145.9 2.4 multiply_subtract_fusion.4
  155.0 2.3 fusion.25
  157.3 2.3 fusion.5
  159.6 2.4 stack.17
  162.0 3.5 fusion.6
  167.6 7.9 %copy.31 = f32[2,32,8192]{1,0,2:T(2,128)} copy(f32[2,32,8192]{2,1,0:T(8,128)S(1)} %pad_maximum_fusion) | data formatting | bytes 4194304 | tf_op jit(solution)/shard_map/stack | solution.py:95
  175.5 10.2 %reshape.115 = f32[64,1,8192]{2,1,0:T(1,128)S(1)} reshape(f32[8192,2,32]{2,1,0:T(2,128)} %bitcast.188) | data formatting | bytes 4194304
  185.7 53.3 %all_to_all.81 = f32[64,1,8192]{2,1,0:T(1,128)} all-to-all(f32[64,1,8192]{2,1,0:T(1,128)S(1)} %reshape.115), channel_id=1, replica_groups=mesh['energy'=64,'elem'=4] {'energy'}, dimensions={0} | all-to-all | bytes 4194304 | tf_op jit(solution)/shard_map/all_to_all | solution.py:148
  239.6 7.6 %reduce = f32[64,8192]{1,0:T(8,128)S(1)} reduce(f32[64,1,8192]{2,1,0:T(1,128)} %all_to_all.81, f32[]{:T(128)} %broadcast.405), dimensions={1}, to_apply=%all_to_all.65.reduce_sub_computation | reduce | bytes 4194308 | tf_op jit(solution)/shard_map/all_to_all | solution.py:148
  247.2 8.5 %reshape.116 = f32[8192,2,32]{2,1,0:T(2,128)} reshape(f32[64,8192]{1,0:T(8,128)S(1)} %reduce) | data formatting | bytes 4194304
  255.6 10.3 %copy.32 = f32[2,64,32,128]{3,0,2,1:T(2,128)S(1)} copy(f32[2,64,32,128]{2,0,3,1:T(2,128)} %bitcast.189) | data formatting | bytes 4194304 | tf_op jit(solution)/shard_map/all_to_all | solution.py:148
  267.9 3.4 collective-permute-start
  271.3 43.3 %collective-permute-done.1 = f32[1,2,2048,128]{3,1,2,0:T(2,128)S(1)} collective-permute-done((f32[1,2,2048,128]{3,1,2,0:T(2,128)S(1)}, f32[1,2,2048,128]{3,1,2,0:T(2,128)S(1)}, u32[]{:S(2)}, u32[]{:S(2)}) %collective-permute-start.1) | collective-permute-done | bytes 2097184 | tf_op jit(solution)/shard_map/ppermute | solution.py:17
  316.5 7.4 %fusion = f32[2,2048,128]{2,0,1:T(2,128)S(1)} fusion(f32[1,2,2048,128]{3,1,2,0:T(2,128)S(1)} %collective-permute-done, f32[1,2,2048,128]{3,1,2,0:T(2,128)S(1)} %collective-permute-done.1, f32[2048]{0:T(1024)S(1)} %copy-done.7, f32[2048]{0:T(1024)S(1)} %copy-done.8, f32[2,64,32,128]{3,0,2,1:T(2,128)S(1)} %copy.32), kind=kLoop, calls=%fused_computation.6 | loop fusion | flops 2097152 | bytes 8404992 | tf_op jit(solution)/shard_map/add | solution.py:127
  323.9 60.4 %all_to_all.82 = f32[2,2048,128]{2,0,1:T(2,128)S(1)} all-to-all(f32[2,2048,128]{2,0,1:T(2,128)S(1)} %fusion), channel_id=1, replica_groups=mesh['energy'=64,'elem'=4] {'energy'}, dimensions={1} | all-to-all | bytes 4194304 | tf_op jit(solution)/shard_map/all_to_all | solution.py:151
  403.5 2.3 fusion.1
  405.8 2.4 stack.21
  408.2 2.3 fusion.2
  412.6 7.9 %copy.36 = f32[2,32,8192]{1,0,2:T(2,128)} copy(f32[2,32,8192]{2,1,0:T(8,128)S(1)} %pad_maximum_fusion.1) | data formatting | bytes 4194304 | tf_op jit(solution)/shard_map/stack | solution.py:95
  420.5 11.0 %reshape.117 = f32[64,1,8192]{2,1,0:T(1,128)} reshape(f32[8192,2,32]{2,1,0:T(2,128)} %bitcast.190) | data formatting | bytes 4194304
  431.5 5.3 %all-to-all-start.4 = ((f32[64,1,8192]{2,1,0:T(1,128)}), f32[64,1,8192]{2,1,0:T(1,128)}, u32[]{:S(2)}, u32[]{:S(2)}) async-start(f32[64,1,8192]{2,1,0:T(1,128)} %reshape.117), calls=%async_computation.4 | async-start | bytes 4194304 | tf_op jit(solution)/shard_map/all_to_all | solution.py:153
  438.3 52.5 %all-to-all-done.4 = f32[64,1,8192]{2,1,0:T(1,128)} async-done(((f32[64,1,8192]{2,1,0:T(1,128)}), f32[64,1,8192]{2,1,0:T(1,128)}, u32[]{:S(2)}, u32[]{:S(2)}) %all-to-all-start.4) | async-done | bytes 2097184 | tf_op jit(solution)/shard_map/all_to_all | solution.py:153
  490.7 7.6 %reduce.1 = f32[64,8192]{1,0:T(8,128)S(1)} reduce(f32[64,1,8192]{2,1,0:T(1,128)} %all-to-all-done.4, f32[]{:T(128)} %broadcast.405), dimensions={1}, to_apply=%all_to_all.72.reduce_sub_computation | reduce | bytes 4194308 | tf_op jit(solution)/shard_map/all_to_all | solution.py:153
  498.3 8.5 %reshape.118 = f32[8192,2,32]{2,1,0:T(2,128)} reshape(f32[64,8192]{1,0:T(8,128)S(1)} %reduce.1) | data formatting | bytes 4194304
  506.8 10.4 %copy.37 = f32[2,64,32,128]{3,2,1,0:T(8,128)} copy(f32[2,64,32,128]{2,0,3,1:T(2,128)} %bitcast.191) | data formatting | bytes 4194304 | tf_op jit(solution)/shard_map/all_to_all | solution.py:153
  (67 shorter events, 57.2 us)
Async XLA Ops:
  3.8 69.2 %all-to-all-start = ((f32[2,64,32,128]{3,2,0,1:T(8,128)}), f32[2,64,32,128]{3,2,0,1:T(8,128)S(1)}, u32[]{:S(2)}, u32[]{:S(2)}) async-start(f32[2,64,32,128]{3,2,0,1:T(8,128)} %copy.27), calls=%async_computation | async-start | bytes 4194304 | tf_op jit(solution)/shard_map/all_to_all | solution.py:141
  72.9 59.0 %all-to-all-start.1 = ((f32[2,64,32,128]{3,2,0,1:T(8,128)}), f32[2,64,32,128]{3,2,0,1:T(8,128)}, u32[]{:S(2)}, u32[]{:S(2)}) async-start(f32[2,64,32,128]{3,2,0,1:T(8,128)} %copy.29), calls=%async_computation.1 | async-start | bytes 4194304 | tf_op jit(solution)/shard_map/all_to_all | solution.py:142
  140.9 1.2 copy-start.3
  144.6 1.3 copy-start.2
  165.5 1.5 copy-start.5
  255.6 60.9 %copy-start.7 = (f32[2048]{0:T(1024)S(1)}, f32[2048]{0:T(1024)}, u32[]{:S(2)}) copy-start(f32[2048]{0:T(1024)} %param.7) | copy-start | bytes 24580
  255.6 60.9 %copy-start.8 = (f32[2048]{0:T(1024)S(1)}, f32[2048]{0:T(1024)}, u32[]{:S(2)}) copy-start(f32[2048]{0:T(1024)} %param.6) | copy-start | bytes 24580
  266.0 58.0 %copy-start = (f32[2,64,32,128]{3,0,2,1:T(2,128)}, f32[2,64,32,128]{3,0,2,1:T(2,128)S(1)}, u32[]{:S(2)}) copy-start(f32[2,64,32,128]{3,0,2,1:T(2,128)S(1)} %copy.32) | copy-start | bytes 6291460
  266.0 48.6 %collective-permute-start.1 = (f32[1,2,2048,128]{3,1,2,0:T(2,128)S(1)}, f32[1,2,2048,128]{3,1,2,0:T(2,128)S(1)}, u32[]{:S(2)}, u32[]{:S(2)}) collective-permute-start(f32[1,2,2048,128]{3,1,2,0:T(2,128)S(1)} %bitcast.204), channel_id=1, source_target_pairs={{1,0},{2,1},{3,2},{5,4},{6,5},{7,6},{9,8},{10,9},{11,10},{13,12},{... | collective-permute-start | bytes 6291464 | tf_op jit(solution)/shard_map/ppermute | solution.py:17
  267.9 48.6 %collective-permute-start = (f32[1,2,2048,128]{3,1,2,0:T(2,128)S(1)}, f32[1,2,2048,128]{3,1,2,0:T(2,128)S(1)}, u32[]{:S(2)}, u32[]{:S(2)}) collective-permute-start(f32[1,2,2048,128]{3,1,2,0:T(2,128)S(1)} %bitcast.205), channel_id=1, source_target_pairs={{0,1},{1,2},{2,3},{4,5},{5,6},{6,7},{8,9},{9,10},{10,11},{12,13},{... | collective-permute-start | bytes 6291464 | tf_op jit(solution)/shard_map/ppermute | solution.py:16
  392.8 1.3 copy-start.6
  410.5 1.5 copy-start.4
  431.5 5.3 %copy-start.1 = (f32[2,64,32,128]{3,0,2,1:T(2,128)S(1)}, f32[2,64,32,128]{3,0,2,1:T(2,128)}, u32[]{:S(2)}) copy-start(f32[2,64,32,128]{3,0,2,1:T(2,128)} %copy-done) | copy-start | bytes 6291460
  431.5 59.2 %all-to-all-start.4 = ((f32[64,1,8192]{2,1,0:T(1,128)}), f32[64,1,8192]{2,1,0:T(1,128)}, u32[]{:S(2)}, u32[]{:S(2)}) async-start(f32[64,1,8192]{2,1,0:T(1,128)} %reshape.117), calls=%async_computation.4 | async-start | bytes 4194304 | tf_op jit(solution)/shard_map/all_to_all | solution.py:153
where the time goes:
time: 521 us; the launch traced here: 517 us
  waiting for transfers between devices  193 us (37%)
  blocking collectives  114 us (22%)
  local copies, waits for them, and re-layouts  96.1 us (18%)
  matrix products  59.7 us (11%)
  starting transfers between devices  29.8 us (6%)
  other arithmetic  23.7 us (5%)
    all_to_all x1, blocking collectives, shards(): lax.all_to_all(screened_en, 'energy', split_axis=1, concat_axis=2, tiled=...  60.4 us
    dot_general x40, matrix products, product(): jnp.einsum(pattern, left_side, right_side, precision=lax.Precision.HIGHEST)  59.7 us
    all_to_all x1, blocking collectives, shards(): lax.all_to_all(polar_el, 'energy', split_axis=2, concat_axis=1, tiled=True)  53.3 us
    all_to_all x1, waiting for transfers between devices, shards(): lax.all_to_all(sigma_el, 'energy', split_axis=2, concat_axis=1, tiled=True)  52.5 us
    all_to_all x1, waiting for transfers between devices, shards(): lax.all_to_all(lesser_grouped, 'energy', split_axis=1, concat_axis=3, til...  52.1 us
    ppermute x1, waiting for transfers between devices, with_halo(): after = lax.ppermute(initial, axis, down)  43.3 us
    all_to_all x1, waiting for transfers between devices, shards(): lax.all_to_all(greater_grouped, 'energy', split_axis=1, concat_axis=3, ti...  43.3 us
    unnamed x23, local copies, waits for them, and re-layouts  39.6 us
  transfers between devices with their start and end apart: 5, of which 5 were waited for; matrix products, arithmetic and copies ran while one was open for 3% of the time, Pallas kernels for 0%

commit v1 on v0

v1 whole, which is shorter than its diff:
```python
import functools
import math

import jax
import jax.numpy as jnp
import ml_dtypes
import numpy as np
from jax import lax
from jax.experimental import pallas as pl
from jax.experimental.pallas import tpu as pltpu
from jax.sharding import Mesh
from jax.sharding import PartitionSpec as P

SIZES = (4, 2, 4, 2, 4)
AXES = ("x", "zh", "y", "c", "zl")
RING = ("zh", "zl")
PLANE = ("x", "y", "c")
NZ, NU = 8, 32
NJ, NB = 64, 128
NE = NJ * NB
KK = 4
F32, BF16 = jnp.float32, jnp.bfloat16
HBM = pl.BlockSpec(memory_space=pl.ANY)
VMEM = pl.BlockSpec(memory_space=pltpu.VMEM)
SMEM = pl.BlockSpec(memory_space=pltpu.SMEM)
LIMIT = 40 * 1024 * 1024


def halves(table):
    high = table.astype(np.float32).astype(ml_dtypes.bfloat16)
    low = (table - high.astype(np.float64)).astype(np.float32).astype(ml_dtypes.bfloat16)
    return high, low


@functools.lru_cache(maxsize=1)
def tables():
    zh, u = np.meshgrid(np.arange(2), np.arange(NU), indexing="ij")
    j = ((u // 8) * 16 + zh * 8 + u % 8).reshape(-1)
    outer = 2 * math.pi * (j[:, None] * np.arange(NJ)[None, :] % NJ) / NJ
    inner = 2 * math.pi * (np.arange(NB)[:, None] * np.arange(NB)[None, :] % NB) / NB
    twist = 2 * math.pi * (np.arange(NJ)[:, None] * np.arange(NB)[None, :]) / NE
    co, so, ci, si = np.cos(outer), np.sin(outer), np.cos(inner), np.sin(inner)
    d1 = np.block([[co.T, so.T], [-so.T, co.T]])
    d2 = np.block([[ci, -si], [si, ci]])
    e2 = np.block([[ci, si], [-si, ci]])
    polar_scale, sigma_scale = NE**-1.5, -(float(NE) ** -2)
    e1p = polar_scale * np.block([[-so, -co], [co, -so]])
    e1s = sigma_scale * np.block([[co, -so], [so, co]])
    out = []
    for table in (d1, d2, e2, e1p, e1s):
        out.extend(halves(table))
    out.append(np.cos(twist).astype(np.float32))
    out.append(np.sin(twist).astype(np.float32))
    return tuple(out)


def split(x):
    high = x.astype(BF16)
    return high, (x - high.astype(F32)).astype(BF16)


def dot(a, b):
    return lax.dot_general(a, b, (((1,), (0,)), ((), ())), preferred_element_type=F32)


def dot3(a, b):
    return dot(a[0], b[0]) + (dot(a[0], b[1]) + dot(a[1], b[0]))


def interleave(first, second):
    low = jnp.concatenate([first[:, :KK], second[:, :KK]], axis=1)
    high = jnp.concatenate([first[:, KK:], second[:, KK:]], axis=1)
    return low, high


def pack_kernel(z_ref, lesser, greater, *outs):
    for d in range(NZ):
        start = pl.multiple_of(lax.rem(z_ref[0] + d, NZ) * 128, 128)
        for g, ref in enumerate((lesser, greater)):
            real = ref[0, pl.ds(start, 128), :].reshape(16, 8, 128)
            imag = ref[1, pl.ds(start, 128), :].reshape(16, 8, 128)
            even, odd = interleave(real, imag)
            if len(outs) == 1:
                outs[0][:, 0, d, g] = even
                outs[0][:, 1, d, g] = odd
            else:
                outs[d][:, 0, g] = even
                outs[d][:, 1, g] = odd


def pack(z, lesser, greater, chunk, joined):
    half = pl.BlockSpec((2, 1024, 128), lambda i, z_ref: (0, chunk, 0))
    if joined:
        shapes = [(16, 2, NZ, 2, 8, 128)]
    else:
        shapes = [(16, 2, 2, 8, 128)] * NZ
    outs = pl.pallas_call(
        pack_kernel,
        out_shape=[jax.ShapeDtypeStruct(s, F32) for s in shapes],
        grid_spec=pltpu.PrefetchScalarGridSpec(
            num_scalar_prefetch=1,
            grid=(1,),
            in_specs=[half, half],
            out_specs=[pl.BlockSpec(s, lambda i, z_ref, n=len(s): (0,) * n) for s in shapes],
        ),
        compiler_params=pltpu.CompilerParams(vmem_limit_bytes=LIMIT),
        cost_estimate=pl.CostEstimate(flops=1 << 20, bytes_accessed=1 << 22, transcendentals=0),
        name="pack",
    )(z, lesser, greater)
    if joined:
        return outs[0].reshape(NU, NZ, 16, 128)
    return [o.reshape(NU, 16, 128) for o in outs]


def merge_kernel(*refs):
    sem = refs[-1]
    out = refs[-2]
    copies = [pltpu.make_async_copy(refs[d], out.at[:, d], sem.at[d]) for d in range(NZ)]
    for copy in copies:
        copy.start()
    for copy in copies:
        copy.wait()


def merge(blocks):
    return pl.pallas_call(
        merge_kernel,
        out_shape=jax.ShapeDtypeStruct((NU, NZ, 16, 128), F32),
        in_specs=[HBM] * NZ,
        out_specs=HBM,
        scratch_shapes=[pltpu.SemaphoreType.DMA((NZ,))],
        cost_estimate=pl.CostEstimate(flops=0, bytes_accessed=1 << 22, transcendentals=0),
        name="merge",
    )(*blocks)


def convolve_kernel(joined_in, joined_out, *refs):
    n_in = 1 if joined_in else NZ
    n_out = 1 if joined_out else NZ
    z_ref, weights = refs[:2]
    ins = refs[2 : 2 + n_in]
    consts = refs[2 + n_in : 14 + n_in]
    outs = refs[14 + n_in : 14 + n_in + n_out]
    xin, yout, sem = refs[14 + n_in + n_out :]
    d1, d2, e2, e1p, e1s = [(consts[2 * i][...], consts[2 * i + 1][...]) for i in range(5)]
    cos, sin = consts[10][...], consts[11][...]
    z = z_ref[0]

    copies = []
    for d in range(NZ):
        place = pl.ds(lax.rem(z + (NZ - d), NZ) * NU, NU)
        source = ins[0].at[:, d] if joined_in else ins[d]
        copies.append(pltpu.make_async_copy(source, xin.at[place], sem.at[d]))
    for copy in copies:
        copy.start()
    for copy in copies:
        copy.wait()

    rows_in = xin.reshape(NZ * NU * 16, 128)
    rows_out = yout.reshape(NZ * NU * 16, 128)

    def step(kk, carry):
        turned = []
        for g in range(2):
            for r in range(4):
                parts = []
                for c in range(2):
                    for zh in range(2):
                        base = (zh * 4 + r) * NU * 16 + g * 8 + c * KK + kk
                        parts.append(rows_in[pl.ds(base, NU, stride=16), :])
                y = dot3(d1, split(jnp.concatenate(parts, axis=0)))
                yr, yi = y[:NJ], y[NJ:]
                turned.append(
                    jnp.concatenate([yr * cos + yi * sin, yi * cos - yr * sin], axis=1)
                )
        spec = dot3(split(jnp.concatenate(turned, axis=0)), d2)
        lr, li = spec[:256, :NB], spec[:256, NB:]
        gr, gi = spec[256:, :NB], spec[256:, NB:]
        cr = lr * gr + li * gi
        ci = li * gr - lr * gi
        wr, wi = [], []
        for r in range(4):
            own = weights[r * 8 + kk]
            side = weights[r * 8 + KK + kk]
            for source, dest in ((cr, wr), (ci, wi)):
                rows = [source[q * NJ : (q + 1) * NJ] for q in (r - 1, r + 1) if 0 <= q < 4]
                beside = rows[0] if len(rows) == 1 else rows[0] + rows[1]
                dest.append(own * source[r * NJ : (r + 1) * NJ] + side * beside)
        wr, wi = jnp.concatenate(wr, axis=0), jnp.concatenate(wi, axis=0)
        vr = lr * wr - li * wi
        vi = lr * wi + li * wr
        both = jnp.concatenate(
            [jnp.concatenate([cr, ci], axis=1), jnp.concatenate([vr, vi], axis=1)], axis=0
        )
        back = dot3(split(both), e2)
        for o in range(2):
            for r in range(4):
                part = back[(o * 4 + r) * NJ : (o * 4 + r + 1) * NJ]
                ar, ai = part[:, :NB], part[:, NB:]
                turn = jnp.concatenate([ar * cos - ai * sin, ai * cos + ar * sin], axis=0)
                done = dot3((e1p, e1s)[o], split(turn))
                for c in range(2):
                    for zh in range(2):
                        base = (zh * 4 + r) * NU * 16 + o * 8 + c * KK + kk
                        at = (c * 2 + zh) * NU
                        rows_out[pl.ds(base, NU, stride=16), :] = done[at : at + NU]
        return carry

    lax.fori_loop(0, KK, step, 0)

    copies = []
    for d in range(NZ):
        place = pl.ds(lax.rem(z + d, NZ) * NU, NU)
        dest = outs[0].at[:, d] if joined_out else outs[d]
        copies.append(pltpu.make_async_copy(yout.at[place], dest, sem.at[d]))
    for copy in copies:
        copy.start()
    for copy in copies:
        copy.wait()


def convolve(z, weights, ins, joined_out):
    consts = [jnp.asarray(t) for t in tables()]
    if joined_out:
        shapes = [(NU, NZ, 16, 128)]
    else:
        shapes = [(NU, 16, 128)] * NZ
    outs = pl.pallas_call(
        functools.partial(convolve_kernel, len(ins) == 1, joined_out),
        out_shape=[jax.ShapeDtypeStruct(s, F32) for s in shapes],
        in_specs=[SMEM, SMEM] + [HBM] * len(ins) + [VMEM] * len(consts),
        out_specs=[HBM] * len(shapes),
        scratch_shapes=[
            pltpu.VMEM((NZ * NU, 16, 128), F32),
            pltpu.VMEM((NZ * NU, 16, 128), F32),
            pltpu.SemaphoreType.DMA((NZ,)),
        ],
        compiler_params=pltpu.CompilerParams(vmem_limit_bytes=LIMIT),
        cost_estimate=pl.CostEstimate(flops=6 * 10**9, bytes_accessed=1 << 22, transcendentals=0),
        name="convolve",
    )(z, weights, *ins, *consts)
    return outs


def unpack_kernel(n_in, n_old, z_ref, *refs):
    ins = refs[:n_in]
    outs = refs[n_in + n_old :]
    for d in range(NZ):
        start = pl.multiple_of(lax.rem(z_ref[0] + (NZ - d), NZ) * 128, 128)
        for o in range(2):
            if n_in == 1:
                even, odd = ins[0][:, 0, d, o], ins[0][:, 1, d, o]
            else:
                even, odd = ins[d][:, 0, o], ins[d][:, 1, o]
            real, imag = interleave(even, odd)
            outs[o][0, pl.ds(start, 128), :] = real.reshape(128, 128)
            outs[o][1, pl.ds(start, 128), :] = imag.reshape(128, 128)


def unpack(z, ins, chunk, old):
    if len(ins) == 1:
        ins = [ins[0].reshape(16, 2, NZ, 2, 8, 128)]
    else:
        ins = [x.reshape(16, 2, 2, 8, 128) for x in ins]
    half = pl.BlockSpec((2, 1024, 128), lambda i, z_ref: (0, chunk, 0))
    whole = [pl.BlockSpec(x.shape, lambda i, z_ref, n=x.ndim: (0,) * n) for x in ins]
    return pl.pallas_call(
        functools.partial(unpack_kernel, len(ins), len(old)),
        out_shape=[jax.ShapeDtypeStruct((2, 2048, 128), F32)] * 2,
        grid_spec=pltpu.PrefetchScalarGridSpec(
            num_scalar_prefetch=1,
            grid=(1,),
            in_specs=whole + [HBM] * len(old),
            out_specs=[half, half],
        ),
        input_output_aliases={1 + len(ins) + i: i for i in range(len(old))},
        compiler_params=pltpu.CompilerParams(vmem_limit_bytes=LIMIT),
        cost_estimate=pl.CostEstimate(flops=1 << 20, bytes_accessed=1 << 22, transcendentals=0),
        name="unpack",
    )(z, *ins, *old)


def round_ring(blocks):
    out = [blocks[0]]
    for d in range(1, NZ):
        out.append(lax.ppermute(blocks[d], RING, [(i, (i + d) % NZ) for i in range(NZ)]))
    return out


def over_plane(x):
    return lax.all_to_all(x, PLANE, split_axis=0, concat_axis=0, tiled=True)


def apart(x):
    return [x[:, d] for d in range(NZ)]


def shards(green_lesser, green_greater, screen, couple):
    z = lax.axis_index(RING).astype(jnp.int32)
    u = lax.axis_index(PLANE).astype(jnp.int32)
    z1 = z.reshape(1)
    gains = lax.all_gather(jnp.stack([screen, couple]), "zl")
    weights = [
        lax.dynamic_slice(gains, (0, 0, q * 1024 + z * 128 + u * KK), (4, 2, KK)).reshape(-1)
        for q in range(2)
    ]
    first = round_ring(pack(z1, green_lesser, green_greater, 0, False))
    second = apart(over_plane(pack(z1, green_lesser, green_greater, 1, True)))
    second = round_ring(second)
    first = over_plane(merge(first))
    first = convolve(z1, weights[0], [first], False)
    first = round_ring(first)
    second = convolve(z1, weights[1], second, True)[0]
    second = round_ring(apart(over_plane(second)))
    first = over_plane(merge(first))
    done = unpack(z1, [first], 0, [])
    polar, sigma = unpack(z1, second, 1, done)
    return polar, sigma


def solution(mesh):
    named = Mesh(mesh.devices.reshape(SIZES), AXES)
    placed = P(None, "zl", ("x", "zh", "y", "c"))
    return jax.shard_map(
        shards,
        mesh=named,
        in_specs=(placed, placed, P("zl"), P("zl")),
        out_specs=(placed, placed),
        check_vma=False,
    )
```

time: 521 us -> 438 us (0.84)
  the two profiles are of different devices: /device:TPU:33 before, /device:TPU:1 now
where the time goes in v1:
time: 438 us; the launch traced here: 437 us
  Pallas kernels  151 us (34%)
  waiting for transfers between devices  125 us (29%)
  starting transfers between devices  98.1 us (22%)
  blocking collectives  36.5 us (8%)
  local copies, waits for them, and re-layouts  24.8 us (6%)
    pallas_call x2, Pallas kernels, merge(): pl.pallas_call(merge_kernel, out_shape=jax.ShapeDtypeStruct((NU, NZ, 16,...  129 us
    ppermute x28, waiting for transfers between devices, round_ring(): lax.ppermute(blocks[d], RING, [(i, (i + d) % NZ) for i in range(NZ)])  123 us
    ppermute x28, starting transfers between devices, round_ring(): lax.ppermute(blocks[d], RING, [(i, (i + d) % NZ) for i in range(NZ)])  62.7 us
    all_gather x1, blocking collectives, shards(): gains = lax.all_gather(jnp.stack([screen, couple]), 'zl')  36.5 us
    all_to_all x4, starting transfers between devices, over_plane(): return lax.all_to_all(x, PLANE, split_axis=0, concat_axis=0, tiled=True)  35.5 us
    unnamed x94, local copies, waits for them, and re-layouts  19.1 us
    pallas_call x2, Pallas kernels, convolve(): pl.pallas_call(functools.partial(convolve_kernel, len(ins) == 1, joined_o...  16.5 us
  transfers between devices with their start and end apart: 32, of which 17 were waited for; matrix products, arithmetic and copies ran while one was open for 1% of the time, Pallas kernels for 34%

profile of v1, /device:TPU:1, one launch (start us, length us, event | category | flops | bytes accessed | tf_op | source)
XLA Modules:
  0.0 436.7 jit_solution(10995414093040458268)
XLA Ops:
  5.5 8.8 %all-to-all-start = ((f32[32,8,16,128]{3,2,1,0:T(8,128)}), f32[32,8,16,128]{3,2,1,0:T(8,128)}, u32[]{:S(2)}, u32[]{:S(2)}) async-start(f32[32,8,16,128]{3,2,1,0:T(8,128)} %bitcast.69), calls=%async_computation | async-start | bytes 4194304 | tf_op jit(solution)/shard_map/all_to_all | solution.py:291
  18.6 3.0 collective-permute-start.15
  21.6 3.8 collective-permute-start.16
  25.8 4.5 %collective-permute-start.18 = (f32[32,16,128]{2,1,0:T(8,128)S(1)}, f32[32,16,128]{2,1,0:T(8,128)S(1)}, u32[]{:S(2)}, u32[]{:S(2)}) collective-permute-start(f32[32,16,128]{2,1,0:T(8,128)S(1)} %bitcast.79), channel_id=1, source_target_pairs={{0,33},{1,34},{2,35},{3,0},{32,1},{33,2},{34,3},{35,32},{4,37},{5,... | collective-permute-start | bytes 786440 | tf_op jit(solution)/shard_map/ppermute | solution.py:286
  32.7 3.5 collective-permute-done.15.refs_2_
  36.2 6.7 %collective-permute-start.20 = (f32[32,16,128]{2,1,0:T(8,128)S(1)}, f32[32,16,128]{2,1,0:T(8,128)S(1)}, u32[]{:S(2)}, u32[]{:S(2)}) collective-permute-start(f32[32,16,128]{2,1,0:T(8,128)S(1)} %bitcast.77), channel_id=1, source_target_pairs={{0,35},{1,0},{2,1},{3,2},{32,3},{33,32},{34,33},{35,34},{4,39},{5,... | collective-permute-start | bytes 786440 | tf_op jit(solution)/shard_map/ppermute | solution.py:286
  42.9 14.6 %collective-permute-done.16.refs_3_ = f32[32,16,128]{2,1,0:T(8,128)S(1)} collective-permute-done((f32[32,16,128]{2,1,0:T(8,128)S(1)}, f32[32,16,128]{2,1,0:T(8,128)S(1)}, u32[]{:S(2)}, u32[]{:S(2)}) %collective-permute-start.16) | collective-permute-done | bytes 262176 | tf_op jit(solution)/shard_map/ppermute | solution.py:286
  57.6 4.8 %collective-permute-done.17.refs_4_ = f32[32,16,128]{2,1,0:T(8,128)S(1)} collective-permute-done((f32[32,16,128]{2,1,0:T(8,128)S(1)}, f32[32,16,128]{2,1,0:T(8,128)S(1)}, u32[]{:S(2)}, u32[]{:S(2)}) %collective-permute-start.17) | collective-permute-done | bytes 262176 | tf_op jit(solution)/shard_map/ppermute | solution.py:286
  62.4 7.7 %collective-permute-done.19.refs_6_ = f32[32,16,128]{2,1,0:T(8,128)S(1)} collective-permute-done((f32[32,16,128]{2,1,0:T(8,128)S(1)}, f32[32,16,128]{2,1,0:T(8,128)S(1)}, u32[]{:S(2)}, u32[]{:S(2)}) %collective-permute-start.19) | collective-permute-done | bytes 262176 | tf_op jit(solution)/shard_map/ppermute | solution.py:286
  73.1 64.7 %merge.2 = f32[32,8,16,128]{3,2,1,0:T(8,128)} custom-call(f32[32,16,128]{2,1,0:T(8,128)} %bitcast.76, f32[32,16,128]{2,1,0:T(8,128)} %copy-done.31, f32[32,16,128]{2,1,0:T(8,128)} %copy-done.33, f32[32,16,128]{2,1,0:T(8,128)} %copy-done.35, f32[32,16,128]{2,1,0:T(8,128)} %copy-done.37, f32[32,16,128]{2,1,0:T(8,128)} %copy-done.39, ...), custom_call_target="tpu_custom_call" | custom-call | bytes 4194304 | tf_op jit(solution)/shard_map/merge/pallas_call | solution.py:126
  137.8 8.6 %all-to-all-start.2 = ((f32[32,8,16,128]{3,2,1,0:T(8,128)}), f32[32,8,16,128]{3,2,1,0:T(8,128)S(1)}, u32[]{:S(2)}, u32[]{:S(2)}) async-start(f32[32,8,16,128]{3,2,1,0:T(8,128)} %merge.2), calls=%async_computation.2 | async-start | bytes 4194304 | tf_op jit(solution)/shard_map/all_to_all | solution.py:291
  146.5 2.8 slice_bitcast_fusion.7
  152.5 3.6 collective-permute-start.4
  157.1 3.3 collective-permute-start.2
  162.4 10.5 %collective-permute-done.5.refs_8_ = f32[32,16,128]{2,1,0:T(8,128)S(1)} collective-permute-done((f32[32,16,128]{2,1,0:T(8,128)}, f32[32,16,128]{2,1,0:T(8,128)S(1)}, u32[]{:S(2)}, u32[]{:S(2)}) %collective-permute-start.5) | collective-permute-done | bytes 262176 | tf_op jit(solution)/shard_map/ppermute | solution.py:286
  172.9 36.5 %all-gather.1 = f32[4,2,2048]{2,1,0:T(2,128)S(1)} all-gather(f32[1,2,2048]{2,1,0:T(2,128)S(1)} %maximum_bitcast_fusion), channel_id=2, replica_groups=mesh['x'=4,'zh'=2,'y'=4,'c'=2,'zl'=4] {'zl'}, dimensions={0}, use_global_device_ids=true | all-gather | bytes 81920 | tf_op jit(solution)/shard_map/all_gather | solution.py:302
  218.4 8.8 %convolve.2 = f32[32,8,16,128]{3,2,1,0:T(8,128)S(1)} custom-call(s32[1]{0:T(128)} %bitcast.z_ref.refs_0_, f32[32]{0:T(128)S(1)} %reshape.65.refs_1_, f32[32,16,128]{2,1,0:T(8,128)S(1)} %get-tuple-element.53.refs_2_, f32[32,16,128]{2,1,0:T(8,128)} %collective-permute-done.refs_3_, f32[32,16,128]{2,1,0:T(8,128)} %collective-permute-done.1.refs_4_, ...), custom_call_target="tpu_custom_call" | custom-call | flops 6000000000 | bytes 4194304 | tf_op jit(solution)/shard_map/convolve/pallas_call | solution.py:228
  228.5 9.5 %all-to-all-start.1 = ((f32[32,8,16,128]{3,2,1,0:T(8,128)}), f32[32,8,16,128]{3,2,1,0:T(8,128)}, u32[]{:S(2)}, u32[]{:S(2)}) async-start(f32[32,8,16,128]{3,2,1,0:T(8,128)} %copy-done.5), calls=%async_computation.1 | async-start | bytes 4194304 | tf_op jit(solution)/shard_map/all_to_all | solution.py:291
  238.2 7.8 %convolve.3 = (f32[32,16,128]{2,1,0:T(8,128)S(1)}, f32[32,16,128]{2,1,0:T(8,128)S(1)}, f32[32,16,128]{2,1,0:T(8,128)S(1)}, f32[32,16,128]{2,1,0:T(8,128)S(1)}, f...) custom-call(s32[1]{0:T(128)} %bitcast.z_ref.refs_0_, ...), custom_call_target="tpu_custom_call" | custom-call | flops 6000000000 | bytes 4194304 | tf_op jit(solution)/shard_map/convolve/pallas_call | solution.py:228
  254.6 4.5 %collective-permute-start.25 = (f32[32,16,128]{2,1,0:T(8,128)S(1)}, f32[32,16,128]{2,1,0:T(8,128)S(1)}, u32[]{:S(2)}, u32[]{:S(2)}) collective-permute-start(f32[32,16,128]{2,1,0:T(8,128)S(1)} %get-tuple-element.33), channel_id=1, source_target_pairs={{0,33},{1,34},{2,35},{3,0},{32,1},{33,2},{34,3},{35,32},{4,37},{5,... | collective-permute-start | bytes 786440 | tf_op jit(solution)/shard_map/ppermute | solution.py:286
  260.6 12.1 %collective-permute-done.22.refs_2_ = f32[32,16,128]{2,1,0:T(8,128)S(1)} collective-permute-done((f32[32,16,128]{2,1,0:T(8,128)S(1)}, f32[32,16,128]{2,1,0:T(8,128)S(1)}, u32[]{:S(2)}, u32[]{:S(2)}) %collective-permute-start.22) | collective-permute-done | bytes 262176 | tf_op jit(solution)/shard_map/ppermute | solution.py:286
  272.6 14.0 %collective-permute-done.23.refs_3_ = f32[32,16,128]{2,1,0:T(8,128)S(1)} collective-permute-done((f32[32,16,128]{2,1,0:T(8,128)S(1)}, f32[32,16,128]{2,1,0:T(8,128)S(1)}, u32[]{:S(2)}, u32[]{:S(2)}) %collective-permute-start.23) | collective-permute-done | bytes 262176 | tf_op jit(solution)/shard_map/ppermute | solution.py:286
  286.6 4.0 collective-permute-done.24.refs_4_
  290.6 7.7 %collective-permute-done.26.refs_6_ = f32[32,16,128]{2,1,0:T(8,128)S(1)} collective-permute-done((f32[32,16,128]{2,1,0:T(8,128)S(1)}, f32[32,16,128]{2,1,0:T(8,128)S(1)}, u32[]{:S(2)}, u32[]{:S(2)}) %collective-permute-start.26) | collective-permute-done | bytes 262176 | tf_op jit(solution)/shard_map/ppermute | solution.py:286
  301.6 64.7 %merge.3 = f32[32,8,16,128]{3,2,1,0:T(8,128)} custom-call(f32[32,16,128]{2,1,0:T(8,128)} %copy-done.6, f32[32,16,128]{2,1,0:T(8,128)} %copy-done.32, f32[32,16,128]{2,1,0:T(8,128)} %copy-done.34, f32[32,16,128]{2,1,0:T(8,128)} %copy-done.36, f32[32,16,128]{2,1,0:T(8,128)} %copy-done.38, f32[32,16,128]{2,1,0:T(8,128)} %copy-done.40, ...), custom_call_target="tpu_custom_call" | custom-call | bytes 4194304 | tf_op jit(solution)/shard_map/merge/pallas_call | solution.py:126
  366.3 8.6 %all-to-all-start.3 = ((f32[32,8,16,128]{3,2,1,0:T(8,128)}), f32[32,8,16,128]{3,2,1,0:T(8,128)S(1)}, u32[]{:S(2)}, u32[]{:S(2)}) async-start(f32[32,8,16,128]{3,2,1,0:T(8,128)} %merge.3), calls=%async_computation.3 | async-start | bytes 4194304 | tf_op jit(solution)/shard_map/all_to_all | solution.py:291
  381.1 3.0 collective-permute-start.11
  388.0 2.9 collective-permute-start.8
  390.9 10.1 %collective-permute-done.12 = f32[32,16,128]{2,1,0:T(8,128)S(1)} collective-permute-done((f32[32,16,128]{2,1,0:T(8,128)S(1)}, f32[32,16,128]{2,1,0:T(8,128)S(1)}, u32[]{:S(2)}, u32[]{:S(2)}) %collective-permute-start.12) | collective-permute-done | bytes 262176 | tf_op jit(solution)/shard_map/ppermute | solution.py:286
  404.7 9.1 %collective-permute-done.11 = f32[32,16,128]{2,1,0:T(8,128)S(1)} collective-permute-done((f32[32,16,128]{2,1,0:T(8,128)}, f32[32,16,128]{2,1,0:T(8,128)S(1)}, u32[]{:S(2)}, u32[]{:S(2)}) %collective-permute-start.11) | collective-permute-done | bytes 262176 | tf_op jit(solution)/shard_map/ppermute | solution.py:286
  413.8 5.0 %collective-permute-done.9 = f32[32,16,128]{2,1,0:T(8,128)} collective-permute-done((f32[32,16,128]{2,1,0:T(8,128)}, f32[32,16,128]{2,1,0:T(8,128)}, u32[]{:S(2)}, u32[]{:S(2)}) %collective-permute-start.9) | collective-permute-done | bytes 262176 | tf_op jit(solution)/shard_map/ppermute | solution.py:286
  421.5 12.6 %collective-permute-done.7 = f32[32,16,128]{2,1,0:T(8,128)} collective-permute-done((f32[32,16,128]{2,1,0:T(8,128)}, f32[32,16,128]{2,1,0:T(8,128)}, u32[]{:S(2)}, u32[]{:S(2)}) %collective-permute-start.7) | collective-permute-done | bytes 262176 | tf_op jit(solution)/shard_map/ppermute | solution.py:286
  (141 shorter events, 63.9 us)
Async XLA Ops:
  5.5 132.3 %all-to-all-start = ((f32[32,8,16,128]{3,2,1,0:T(8,128)}), f32[32,8,16,128]{3,2,1,0:T(8,128)}, u32[]{:S(2)}, u32[]{:S(2)}) async-start(f32[32,8,16,128]{3,2,1,0:T(8,128)} %bitcast.69), calls=%async_computation | async-start | bytes 4194304 | tf_op jit(solution)/shard_map/all_to_all | solution.py:291
  17.0 13.3 %collective-permute-start.14 = (f32[32,16,128]{2,1,0:T(8,128)S(1)}, f32[32,16,128]{2,1,0:T(8,128)S(1)}, u32[]{:S(2)}, u32[]{:S(2)}) collective-permute-start(f32[32,16,128]{2,1,0:T(8,128)S(1)} %bitcast.83), channel_id=1, source_target_pairs={{0,1},{1,2},{2,3},{3,32},{32,33},{33,34},{34,35},{35,0},{4,5},{5,6... | collective-permute-start | bytes 786440 | tf_op jit(solution)/shard_map/ppermute | solution.py:286
  18.6 17.6 %collective-permute-start.15 = (f32[32,16,128]{2,1,0:T(8,128)S(1)}, f32[32,16,128]{2,1,0:T(8,128)S(1)}, u32[]{:S(2)}, u32[]{:S(2)}) collective-permute-start(f32[32,16,128]{2,1,0:T(8,128)S(1)} %bitcast.82), channel_id=1, source_target_pairs={{0,2},{1,3},{2,32},{3,33},{32,34},{33,35},{34,0},{35,1},{4,6},{5,7... | collective-permute-start | bytes 786440 | tf_op jit(solution)/shard_map/ppermute | solution.py:286
  21.6 35.9 %collective-permute-start.16 = (f32[32,16,128]{2,1,0:T(8,128)S(1)}, f32[32,16,128]{2,1,0:T(8,128)S(1)}, u32[]{:S(2)}, u32[]{:S(2)}) collective-permute-start(f32[32,16,128]{2,1,0:T(8,128)S(1)} %bitcast.81), channel_id=1, source_target_pairs={{0,3},{1,32},{2,33},{3,34},{32,35},{33,0},{34,1},{35,2},{4,7},{5,3... | collective-permute-start | bytes 786440 | tf_op jit(solution)/shard_map/ppermute | solution.py:286
  25.4 37.0 %collective-permute-start.17 = (f32[32,16,128]{2,1,0:T(8,128)S(1)}, f32[32,16,128]{2,1,0:T(8,128)S(1)}, u32[]{:S(2)}, u32[]{:S(2)}) collective-permute-start(f32[32,16,128]{2,1,0:T(8,128)S(1)} %bitcast.80), channel_id=1, source_target_pairs={{0,32},{1,33},{2,34},{3,35},{32,0},{33,1},{34,2},{35,3},{4,36},{5,... | collective-permute-start | bytes 786440 | tf_op jit(solution)/shard_map/ppermute | solution.py:286
  25.8 36.6 %collective-permute-start.18 = (f32[32,16,128]{2,1,0:T(8,128)S(1)}, f32[32,16,128]{2,1,0:T(8,128)S(1)}, u32[]{:S(2)}, u32[]{:S(2)}) collective-permute-start(f32[32,16,128]{2,1,0:T(8,128)S(1)} %bitcast.79), channel_id=1, source_target_pairs={{0,33},{1,34},{2,35},{3,0},{32,1},{33,2},{34,3},{35,32},{4,37},{5,... | collective-permute-start | bytes 786440 | tf_op jit(solution)/shard_map/ppermute | solution.py:286
  30.3 39.8 %collective-permute-start.19 = (f32[32,16,128]{2,1,0:T(8,128)S(1)}, f32[32,16,128]{2,1,0:T(8,128)S(1)}, u32[]{:S(2)}, u32[]{:S(2)}) collective-permute-start(f32[32,16,128]{2,1,0:T(8,128)S(1)} %bitcast.78), channel_id=1, source_target_pairs={{0,34},{1,35},{2,0},{3,1},{32,2},{33,3},{34,32},{35,33},{4,38},{5,... | collective-permute-start | bytes 786440 | tf_op jit(solution)/shard_map/ppermute | solution.py:286
  36.2 36.2 %collective-permute-start.20 = (f32[32,16,128]{2,1,0:T(8,128)S(1)}, f32[32,16,128]{2,1,0:T(8,128)S(1)}, u32[]{:S(2)}, u32[]{:S(2)}) collective-permute-start(f32[32,16,128]{2,1,0:T(8,128)S(1)} %bitcast.77), channel_id=1, source_target_pairs={{0,35},{1,0},{2,1},{3,2},{32,3},{33,32},{34,33},{35,34},{4,39},{5,... | collective-permute-start | bytes 786440 | tf_op jit(solution)/shard_map/ppermute | solution.py:286
  137.8 90.7 %all-to-all-start.2 = ((f32[32,8,16,128]{3,2,1,0:T(8,128)}), f32[32,8,16,128]{3,2,1,0:T(8,128)S(1)}, u32[]{:S(2)}, u32[]{:S(2)}) async-start(f32[32,8,16,128]{3,2,1,0:T(8,128)} %merge.2), calls=%async_computation.2 | async-start | bytes 4194304 | tf_op jit(solution)/shard_map/all_to_all | solution.py:291
  149.3 11.0 %collective-permute-start.6 = (f32[32,16,128]{2,1,0:T(8,128)}, f32[32,16,128]{2,1,0:T(8,128)S(1)}, u32[]{:S(2)}, u32[]{:S(2)}) collective-permute-start(f32[32,16,128]{2,1,0:T(8,128)} %get-tuple-element.46), channel_id=1, source_target_pairs={{0,35},{1,0},{2,1},{3,2},{32,3},{33,32},{34,33},{35,34},{4,39},{5,... | collective-permute-start | bytes 786440 | tf_op jit(solution)/shard_map/ppermute | solution.py:286
  151.6 21.2 %collective-permute-start.5 = (f32[32,16,128]{2,1,0:T(8,128)}, f32[32,16,128]{2,1,0:T(8,128)S(1)}, u32[]{:S(2)}, u32[]{:S(2)}) collective-permute-start(f32[32,16,128]{2,1,0:T(8,128)} %get-tuple-element.47), channel_id=1, source_target_pairs={{0,34},{1,35},{2,0},{3,1},{32,2},{33,3},{34,32},{35,33},{4,38},{5,... | collective-permute-start | bytes 786440 | tf_op jit(solution)/shard_map/ppermute | solution.py:286
  152.5 57.0 %collective-permute-start.4 = (f32[32,16,128]{2,1,0:T(8,128)}, f32[32,16,128]{2,1,0:T(8,128)S(1)}, u32[]{:S(2)}, u32[]{:S(2)}) collective-permute-start(f32[32,16,128]{2,1,0:T(8,128)} %get-tuple-element.48), channel_id=1, source_target_pairs={{0,33},{1,34},{2,35},{3,0},{32,1},{33,2},{34,3},{35,32},{4,37},{5,... | collective-permute-start | bytes 786440 | tf_op jit(solution)/shard_map/ppermute | solution.py:286
  156.2 53.3 %collective-permute-start.3 = (f32[32,16,128]{2,1,0:T(8,128)}, f32[32,16,128]{2,1,0:T(8,128)S(1)}, u32[]{:S(2)}, u32[]{:S(2)}) collective-permute-start(f32[32,16,128]{2,1,0:T(8,128)} %get-tuple-element.49), channel_id=1, source_target_pairs={{0,32},{1,33},{2,34},{3,35},{32,0},{33,1},{34,2},{35,3},{4,36},{5,... | collective-permute-start | bytes 786440 | tf_op jit(solution)/shard_map/ppermute | solution.py:286
  157.1 52.5 %collective-permute-start.2 = (f32[32,16,128]{2,1,0:T(8,128)}, f32[32,16,128]{2,1,0:T(8,128)}, u32[]{:S(2)}, u32[]{:S(2)}) collective-permute-start(f32[32,16,128]{2,1,0:T(8,128)} %get-tuple-element.50), channel_id=1, source_target_pairs={{0,3},{1,32},{2,33},{3,34},{32,35},{33,0},{34,1},{35,2},{4,7},{5,3... | collective-permute-start | bytes 786440 | tf_op jit(solution)/shard_map/ppermute | solution.py:286
  160.3 49.2 %collective-permute-start.1 = (f32[32,16,128]{2,1,0:T(8,128)}, f32[32,16,128]{2,1,0:T(8,128)}, u32[]{:S(2)}, u32[]{:S(2)}) collective-permute-start(f32[32,16,128]{2,1,0:T(8,128)} %get-tuple-element.51), channel_id=1, source_target_pairs={{0,2},{1,3},{2,32},{3,33},{32,34},{33,35},{34,0},{35,1},{4,6},{5,7... | collective-permute-start | bytes 786440 | tf_op jit(solution)/shard_map/ppermute | solution.py:286
  172.8 36.7 %collective-permute-start = (f32[32,16,128]{2,1,0:T(8,128)}, f32[32,16,128]{2,1,0:T(8,128)}, u32[]{:S(2)}, u32[]{:S(2)}) collective-permute-start(f32[32,16,128]{2,1,0:T(8,128)} %get-tuple-element.52), channel_id=1, source_target_pairs={{0,1},{1,2},{2,3},{3,32},{32,33},{33,34},{34,35},{35,0},{4,5},{5,6... | collective-permute-start | bytes 786440 | tf_op jit(solution)/shard_map/ppermute | solution.py:286
  228.5 137.8 %all-to-all-start.1 = ((f32[32,8,16,128]{3,2,1,0:T(8,128)}), f32[32,8,16,128]{3,2,1,0:T(8,128)}, u32[]{:S(2)}, u32[]{:S(2)}) async-start(f32[32,8,16,128]{3,2,1,0:T(8,128)} %copy-done.5), calls=%async_computation.1 | async-start | bytes 4194304 | tf_op jit(solution)/shard_map/all_to_all | solution.py:291
  246.7 12.4 %collective-permute-start.21 = (f32[32,16,128]{2,1,0:T(8,128)S(1)}, f32[32,16,128]{2,1,0:T(8,128)S(1)}, u32[]{:S(2)}, u32[]{:S(2)}) collective-permute-start(f32[32,16,128]{2,1,0:T(8,128)S(1)} %get-tuple-element.29), channel_id=1, source_target_pairs={{0,1},{1,2},{2,3},{3,32},{32,33},{33,34},{34,35},{35,0},{4,5},{5,6... | collective-permute-start | bytes 786440 | tf_op jit(solution)/shard_map/ppermute | solution.py:286
  248.0 24.6 %collective-permute-start.22 = (f32[32,16,128]{2,1,0:T(8,128)S(1)}, f32[32,16,128]{2,1,0:T(8,128)S(1)}, u32[]{:S(2)}, u32[]{:S(2)}) collective-permute-start(f32[32,16,128]{2,1,0:T(8,128)S(1)} %get-tuple-element.30), channel_id=1, source_target_pairs={{0,2},{1,3},{2,32},{3,33},{32,34},{33,35},{34,0},{35,1},{4,6},{5,7... | collective-permute-start | bytes 786440 | tf_op jit(solution)/shard_map/ppermute | solution.py:286
  250.1 36.5 %collective-permute-start.23 = (f32[32,16,128]{2,1,0:T(8,128)S(1)}, f32[32,16,128]{2,1,0:T(8,128)S(1)}, u32[]{:S(2)}, u32[]{:S(2)}) collective-permute-start(f32[32,16,128]{2,1,0:T(8,128)S(1)} %get-tuple-element.31), channel_id=1, source_target_pairs={{0,3},{1,32},{2,33},{3,34},{32,35},{33,0},{34,1},{35,2},{4,7},{5,3... | collective-permute-start | bytes 786440 | tf_op jit(solution)/shard_map/ppermute | solution.py:286
  252.5 38.1 %collective-permute-start.24 = (f32[32,16,128]{2,1,0:T(8,128)S(1)}, f32[32,16,128]{2,1,0:T(8,128)S(1)}, u32[]{:S(2)}, u32[]{:S(2)}) collective-permute-start(f32[32,16,128]{2,1,0:T(8,128)S(1)} %get-tuple-element.32), channel_id=1, source_target_pairs={{0,32},{1,33},{2,34},{3,35},{32,0},{33,1},{34,2},{35,3},{4,36},{5,... | collective-permute-start | bytes 786440 | tf_op jit(solution)/shard_map/ppermute | solution.py:286
  254.6 36.0 %collective-permute-start.25 = (f32[32,16,128]{2,1,0:T(8,128)S(1)}, f32[32,16,128]{2,1,0:T(8,128)S(1)}, u32[]{:S(2)}, u32[]{:S(2)}) collective-permute-start(f32[32,16,128]{2,1,0:T(8,128)S(1)} %get-tuple-element.33), channel_id=1, source_target_pairs={{0,33},{1,34},{2,35},{3,0},{32,1},{33,2},{34,3},{35,32},{4,37},{5,... | collective-permute-start | bytes 786440 | tf_op jit(solution)/shard_map/ppermute | solution.py:286
  259.1 39.2 %collective-permute-start.26 = (f32[32,16,128]{2,1,0:T(8,128)S(1)}, f32[32,16,128]{2,1,0:T(8,128)S(1)}, u32[]{:S(2)}, u32[]{:S(2)}) collective-permute-start(f32[32,16,128]{2,1,0:T(8,128)S(1)} %get-tuple-element.34), channel_id=1, source_target_pairs={{0,34},{1,35},{2,0},{3,1},{32,2},{33,3},{34,32},{35,33},{4,38},{5,... | collective-permute-start | bytes 786440 | tf_op jit(solution)/shard_map/ppermute | solution.py:286
  272.6 28.2 %collective-permute-start.27 = (f32[32,16,128]{2,1,0:T(8,128)S(1)}, f32[32,16,128]{2,1,0:T(8,128)S(1)}, u32[]{:S(2)}, u32[]{:S(2)}) collective-permute-start(f32[32,16,128]{2,1,0:T(8,128)S(1)} %get-tuple-element.35), channel_id=1, source_target_pairs={{0,35},{1,0},{2,1},{3,2},{32,3},{33,32},{34,33},{35,34},{4,39},{5,... | collective-permute-start | bytes 786440 | tf_op jit(solution)/shard_map/ppermute | solution.py:286
  366.3 36.9 %all-to-all-start.3 = ((f32[32,8,16,128]{3,2,1,0:T(8,128)}), f32[32,8,16,128]{3,2,1,0:T(8,128)S(1)}, u32[]{:S(2)}, u32[]{:S(2)}) async-start(f32[32,8,16,128]{3,2,1,0:T(8,128)} %merge.3), calls=%async_computation.3 | async-start | bytes 4194304 | tf_op jit(solution)/shard_map/all_to_all | solution.py:291
  377.6 10.4 %collective-permute-start.13 = (f32[32,16,128]{2,1,0:T(8,128)S(1)}, f32[32,16,128]{2,1,0:T(8,128)S(1)}, u32[]{:S(2)}, u32[]{:S(2)}) collective-permute-start(f32[32,16,128]{2,1,0:T(8,128)S(1)} %get-tuple-element.38), channel_id=1, source_target_pairs={{0,35},{1,0},{2,1},{3,2},{32,3},{33,32},{34,33},{35,34},{4,39},{5,... | collective-permute-start | bytes 786440 | tf_op jit(solution)/shard_map/ppermute | solution.py:286
  379.9 21.1 %collective-permute-start.12 = (f32[32,16,128]{2,1,0:T(8,128)S(1)}, f32[32,16,128]{2,1,0:T(8,128)S(1)}, u32[]{:S(2)}, u32[]{:S(2)}) collective-permute-start(f32[32,16,128]{2,1,0:T(8,128)S(1)} %get-tuple-element.39), channel_id=1, source_target_pairs={{0,34},{1,35},{2,0},{3,1},{32,2},{33,3},{34,32},{35,33},{4,38},{5,... | collective-permute-start | bytes 786440 | tf_op jit(solution)/shard_map/ppermute | solution.py:286
  381.1 32.7 %collective-permute-start.11 = (f32[32,16,128]{2,1,0:T(8,128)}, f32[32,16,128]{2,1,0:T(8,128)S(1)}, u32[]{:S(2)}, u32[]{:S(2)}) collective-permute-start(f32[32,16,128]{2,1,0:T(8,128)} %get-tuple-element.40), channel_id=1, source_target_pairs={{0,33},{1,34},{2,35},{3,0},{32,1},{33,2},{34,3},{35,32},{4,37},{5,... | collective-permute-start | bytes 786440 | tf_op jit(solution)/shard_map/ppermute | solution.py:286
  384.1 29.7 %collective-permute-start.10 = (f32[32,16,128]{2,1,0:T(8,128)}, f32[32,16,128]{2,1,0:T(8,128)S(1)}, u32[]{:S(2)}, u32[]{:S(2)}) collective-permute-start(f32[32,16,128]{2,1,0:T(8,128)} %get-tuple-element.41), channel_id=1, source_target_pairs={{0,32},{1,33},{2,34},{3,35},{32,0},{33,1},{34,2},{35,3},{4,36},{5,... | collective-permute-start | bytes 786440 | tf_op jit(solution)/shard_map/ppermute | solution.py:286
  385.7 33.1 %collective-permute-start.9 = (f32[32,16,128]{2,1,0:T(8,128)}, f32[32,16,128]{2,1,0:T(8,128)}, u32[]{:S(2)}, u32[]{:S(2)}) collective-permute-start(f32[32,16,128]{2,1,0:T(8,128)} %get-tuple-element.42), channel_id=1, source_target_pairs={{0,3},{1,32},{2,33},{3,34},{32,35},{33,0},{34,1},{35,2},{4,7},{5,3... | collective-permute-start | bytes 786440 | tf_op jit(solution)/shard_map/ppermute | solution.py:286
  388.0 33.5 %collective-permute-start.8 = (f32[32,16,128]{2,1,0:T(8,128)}, f32[32,16,128]{2,1,0:T(8,128)}, u32[]{:S(2)}, u32[]{:S(2)}) collective-permute-start(f32[32,16,128]{2,1,0:T(8,128)} %get-tuple-element.43), channel_id=1, source_target_pairs={{0,2},{1,3},{2,32},{3,33},{32,34},{33,35},{34,0},{35,1},{4,6},{5,7... | collective-permute-start | bytes 786440 | tf_op jit(solution)/shard_map/ppermute | solution.py:286
  401.1 33.0 %collective-permute-start.7 = (f32[32,16,128]{2,1,0:T(8,128)}, f32[32,16,128]{2,1,0:T(8,128)}, u32[]{:S(2)}, u32[]{:S(2)}) collective-permute-start(f32[32,16,128]{2,1,0:T(8,128)} %get-tuple-element.44), channel_id=1, source_target_pairs={{0,1},{1,2},{2,3},{3,32},{32,33},{33,34},{34,35},{35,0},{4,5},{5,6... | collective-permute-start | bytes 786440 | tf_op jit(solution)/shard_map/ppermute | solution.py:286
  (47 other events, 473.5 us)

commit v2 on v1

v2 whole, which is shorter than its diff:
```python
import functools
import math

import jax
import jax.numpy as jnp
import ml_dtypes
import numpy as np
from jax import lax
from jax.experimental import pallas as pl
from jax.experimental.pallas import tpu as pltpu
from jax.sharding import Mesh
from jax.sharding import PartitionSpec as P

SIZES = (4, 2, 4, 2, 4)
AXES = ("x", "zh", "y", "c", "zl")
RING = ("zh", "zl")
PLANE = ("x", "y", "c")
NZ, NU = 8, 32
NXY = NU // 2
STEPS = (1, 2, 3)
BLOCK = (NU, 16, 128)
NJ, NB = 64, 128
NE = NJ * NB
KK = 4
F32, BF16 = jnp.float32, jnp.bfloat16
HBM = pl.BlockSpec(memory_space=pl.ANY)
VMEM = pl.BlockSpec(memory_space=pltpu.VMEM)
SMEM = pl.BlockSpec(memory_space=pltpu.SMEM)
LIMIT = 58 * 1024 * 1024


def halves(table):
    high = table.astype(np.float32).astype(ml_dtypes.bfloat16)
    low = (table - high.astype(np.float64)).astype(np.float32).astype(ml_dtypes.bfloat16)
    return high, low


@functools.lru_cache(maxsize=1)
def tables():
    zh, u = np.meshgrid(np.arange(2), np.arange(NU), indexing="ij")
    j = ((u // 8) * 16 + zh * 8 + u % 8).reshape(-1)
    outer = 2 * math.pi * (j[:, None] * np.arange(NJ)[None, :] % NJ) / NJ
    inner = 2 * math.pi * (np.arange(NB)[:, None] * np.arange(NB)[None, :] % NB) / NB
    twist = 2 * math.pi * (np.arange(NJ)[:, None] * np.arange(NB)[None, :]) / NE
    co, so, ci, si = np.cos(outer), np.sin(outer), np.cos(inner), np.sin(inner)
    d1 = np.block([[co.T, so.T], [-so.T, co.T]])
    d2 = np.block([[ci, -si], [si, ci]])
    e2 = np.block([[ci, si], [-si, ci]])
    polar_scale, sigma_scale = NE**-1.5, -(float(NE) ** -2)
    e1p = polar_scale * np.block([[-so, -co], [co, -so]])
    e1s = sigma_scale * np.block([[co, -so], [so, co]])
    out = []
    for table in (d1, d2, e2, e1p, e1s):
        out.extend(halves(table))
    out.append(np.cos(twist).astype(np.float32))
    out.append(np.sin(twist).astype(np.float32))
    return tuple(out)


def split(x):
    high = x.astype(BF16)
    return high, (x - high.astype(F32)).astype(BF16)


def dot(a, b):
    return lax.dot_general(a, b, (((1,), (0,)), ((), ())), preferred_element_type=F32)


def dot3(a, b):
    return dot(a[0], b[0]) + (dot(a[0], b[1]) + dot(a[1], b[0]))


def interleave(first, second):
    low = jnp.concatenate([first[:, :KK], second[:, :KK]], axis=1)
    high = jnp.concatenate([first[:, KK:], second[:, KK:]], axis=1)
    return low, high


def around(z, shift):
    return lax.rem(z + (shift + NZ), NZ)


def whole(shape):
    return pl.BlockSpec(shape, lambda i, *_: (0,) * len(shape))


def local_call(kernel, scalars, ins, in_specs, after, shapes, out_specs, name, aliases=None):
    count = len(ins)
    return pl.pallas_call(
        lambda *refs: kernel(
            refs[:1], refs[1 : 1 + count], refs[1 + count + len(after) :]
        ),
        out_shape=[jax.ShapeDtypeStruct(s, F32) for s in shapes],
        grid_spec=pltpu.PrefetchScalarGridSpec(
            num_scalar_prefetch=1,
            grid=(1,),
            in_specs=list(in_specs) + [HBM] * len(after),
            out_specs=out_specs,
        ),
        input_output_aliases=aliases or {},
        compiler_params=pltpu.CompilerParams(vmem_limit_bytes=LIMIT),
        cost_estimate=pl.CostEstimate(flops=1 << 20, bytes_accessed=1 << 22, transcendentals=0),
        name=name,
    )(scalars, *ins, *after)


def blocks_of(lesser, greater, zd):
    start = pl.multiple_of(zd * 128, 128)
    for g, ref in enumerate((lesser, greater)):
        real = ref[0, pl.ds(start, 128), :].reshape(NXY, 8, 128)
        imag = ref[1, pl.ds(start, 128), :].reshape(NXY, 8, 128)
        yield g, *interleave(real, imag)


def pack_ring_kernel(scalars, ins, outs):
    lesser, greater, screen, couple = ins
    own, far, keep, give, gains = outs
    z, sign = scalars[0][0], scalars[0][1]
    targets = [(own, 0), (far, 4)]
    targets += [(keep.at[d - 1], sign * d) for d in STEPS]
    targets += [(give.at[d - 1], -sign * d) for d in STEPS]
    for dest, shift in targets:
        for g, even, odd in blocks_of(lesser, greater, around(z, shift)):
            dest[:, 0, g] = even
            dest[:, 1, g] = odd
    for d in range(4):
        zd = around(z, sign * d)
        rows = [ref[pl.ds(zd + q * NZ, 1), :] for ref in (screen, couple) for q in range(2)]
        gains[d] = jnp.concatenate(rows + rows, axis=0)


def pack_ring(scalars, lesser, greater, screen, couple):
    half = pl.BlockSpec((2, 1024, 128), lambda i, *_: (0, 0, 0))
    small = whole((16, 128))
    one = (NXY, 2, 2, 8, 128)
    shapes = [one, one, (3, *one), (3, *one), (4, 8, 128)]
    own, far, keep, give, gains = local_call(
        pack_ring_kernel,
        scalars,
        [lesser, greater, screen.reshape(16, 128), couple.reshape(16, 128)],
        [half, half, small, small],
        [],
        shapes,
        [whole(s) for s in shapes],
        "pack_ring",
    )
    return own.reshape(BLOCK), far.reshape(BLOCK), keep.reshape(3, *BLOCK), give.reshape(3, *BLOCK), gains


def pack_plane_kernel(scalars, ins, outs):
    lesser, greater = ins
    out = outs[0]
    z = scalars[0][0]
    for shift in range(-3, 5):
        for g, even, odd in blocks_of(lesser, greater, around(z, shift)):
            if shift in (0, 4):
                out[:, 0, shift // 4, g] = even
                out[:, 1, shift // 4, g] = odd
            elif shift > 0:
                out[:, 0, 2 * shift, g] = even
                out[:, 0, 2 * shift + 1, g] = odd
            else:
                out[:, 1, -2 * shift, g] = odd
                out[:, 1, -2 * shift + 1, g] = even


def pack_plane(scalars, lesser, greater, after):
    half = pl.BlockSpec((2, 1024, 128), lambda i, *_: (0, 1, 0))
    shape = (NXY, 2, NZ, 2, 8, 128)
    (out,) = local_call(
        pack_plane_kernel, scalars, [lesser, greater], [half, half], after, [shape], [whole(shape)], "pack_plane"
    )
    return out.reshape(NU, NZ, 16, 128)


def merge_kernel(scalars, ins, outs):
    out = outs[0]
    out[:, 0] = ins[0][...]
    out[:, 1] = ins[1][...]
    for d in STEPS:
        for m in range(2):
            out[:, 2 * d + m] = ins[1 + d][m * 64 : m * 64 + 64].reshape(BLOCK)


def merge(scalars, own, far, paid, after):
    ins = [own, far] + paid
    out = (NU, NZ, 16, 128)
    return local_call(
        merge_kernel,
        scalars,
        ins,
        [whole(x.shape) for x in ins],
        after,
        [out],
        [whole(out)],
        "merge",
    )[0]


def fan_kernel(scalars, ins, outs):
    outs[0][...] = ins[0][:, 1]
    for d in STEPS:
        for m in range(2):
            outs[d][:, m] = ins[0][:, 2 * d + m]


def fan(scalars, joined, after):
    shapes = [BLOCK] + [(NU, 2, 16, 128)] * 3
    out = local_call(
        fan_kernel, scalars, [joined], [whole(joined.shape)], after, shapes, [whole(s) for s in shapes], "fan"
    )
    return out[0], list(out[1:])


def convolve_kernel(joined_in, joined_out, chunk, n_after, *refs):
    n_in = 1 if joined_in else 6
    n_out = 1 if joined_out else 4
    refs = list(refs)
    scalars, weights = refs[:2]
    ins = refs[2 : 2 + n_in]
    tabs = refs[2 + n_in : 14 + n_in]
    outs = refs[14 + n_in + n_after : 14 + n_in + n_after + n_out]
    xin, yout, sem, tab_sem = refs[14 + n_in + n_after + n_out :][:4]
    held = refs[18 + n_in + n_after + n_out :]
    z, sign = scalars[0], scalars[1]

    tab_copies = [pltpu.make_async_copy(t, h, tab_sem.at[i]) for i, (t, h) in enumerate(zip(tabs, held))]
    x_at = xin.at[: NZ * NU].reshape(NZ, NXY, 2, 16, 128)
    y_at = yout.at[: NZ * NU].reshape(NZ, NXY, 2, 16, 128)

    def joined_places(direction):
        for c in range(2):
            way = direction * (1 - 2 * c)
            yield c, 0, z, c
            yield c, 1, around(z, 4), c
            for d in STEPS:
                for m in range(2):
                    yield c, 2 * d + m, around(z, way * d), c ^ m

    pairs = []
    if joined_in:
        source = ins[0].reshape(NXY, 2, NZ, 16, 128)
        for c, slot, zs, core in joined_places(-1):
            pairs.append((source.at[:, c, slot], x_at.at[zs, :, core]))
    else:
        own, far, got = ins[0], ins[1], ins[5]
        pairs.append((own.at[:, 0], xin.at[pl.ds(z * NU, NU)]))
        pairs.append((far, xin.at[pl.ds(around(z, 4) * NU, NU)]))
        for d in STEPS:
            pairs.append((ins[1 + d].at[:, 0], xin.at[pl.ds(around(z, -sign * d) * NU, NU)]))
            pairs.append((got.at[d - 1], xin.at[pl.ds(around(z, sign * d) * NU, NU)]))
    copies = [pltpu.make_async_copy(s, t, sem.at[i]) for i, (s, t) in enumerate(pairs)]
    for copy in copies + tab_copies:
        copy.start()
    for copy in copies + tab_copies:
        copy.wait()

    d1, d2, e2, e1p, e1s = [(held[2 * i][...], held[2 * i + 1][...]) for i in range(5)]
    cos, sin = held[10][...], held[11][...]
    rows_in = xin.reshape((NZ * NU + 1) * 16, 128)
    rows_out = yout.reshape((NZ * NU + 1) * 16, 128)

    def step(kk, carry):
        turned = []
        for g in range(2):
            for r in range(4):
                parts = []
                for c in range(2):
                    for zh in range(2):
                        base = (zh * 4 + r) * NU * 16 + g * 8 + c * KK + kk
                        parts.append(rows_in[pl.ds(base, NU, stride=16), :])
                y = dot3(d1, split(jnp.concatenate(parts, axis=0)))
                yr, yi = y[:NJ], y[NJ:]
                turned.append(jnp.concatenate([yr * cos + yi * sin, yi * cos - yr * sin], axis=1))
        spec = dot3(split(jnp.concatenate(turned, axis=0)), d2)
        lr, li = spec[:256, :NB], spec[:256, NB:]
        gr, gi = spec[256:, :NB], spec[256:, NB:]
        cr = lr * gr + li * gi
        ci = li * gr - lr * gi
        wr, wi = [], []
        for r in range(4):
            d = lax.rem((z + (NZ - r)) * sign + 4 * NZ, 4)
            own_gain = weights[d * 16 + chunk * KK + kk]
            side_gain = weights[d * 16 + 8 + chunk * KK + kk]
            for source, dest in ((cr, wr), (ci, wi)):
                rows = [source[q * NJ : (q + 1) * NJ] for q in (r - 1, r + 1) if 0 <= q < 4]
                beside = rows[0] if len(rows) == 1 else rows[0] + rows[1]
                dest.append(own_gain * source[r * NJ : (r + 1) * NJ] + side_gain * beside)
        wr, wi = jnp.concatenate(wr, axis=0), jnp.concatenate(wi, axis=0)
        vr = lr * wr - li * wi
        vi = lr * wi + li * wr
        both = jnp.concatenate(
            [jnp.concatenate([cr, ci], axis=1), jnp.concatenate([vr, vi], axis=1)], axis=0
        )
        back = dot3(split(both), e2)
        for o in range(2):
            for r in range(4):
                part = back[(o * 4 + r) * NJ : (o * 4 + r + 1) * NJ]
                ar, ai = part[:, :NB], part[:, NB:]
                turn = jnp.concatenate([ar * cos - ai * sin, ai * cos + ar * sin], axis=0)
                done = dot3((e1p, e1s)[o], split(turn))
                for c in range(2):
                    for zh in range(2):
                        base = (zh * 4 + r) * NU * 16 + o * 8 + c * KK + kk
                        at = (c * 2 + zh) * NU
                        rows_out[pl.ds(base, NU, stride=16), :] = done[at : at + NU]
        return carry

    lax.fori_loop(0, KK, step, 0)

    pairs = []
    if joined_out:
        dest = outs[0].reshape(NXY, 2, NZ, 16, 128)
        for c, slot, zd, core in joined_places(1):
            pairs.append((y_at.at[zd, :, core], dest.at[:, c, slot]))
    else:
        own, far, keep, give = outs
        pairs.append((yout.at[pl.ds(z * NU, NU)], own))
        pairs.append((yout.at[pl.ds(around(z, 4) * NU, NU)], far))
        for d in STEPS:
            pairs.append((yout.at[pl.ds(around(z, sign * d) * NU, NU)], keep.at[d - 1]))
            pairs.append((yout.at[pl.ds(around(z, -sign * d) * NU, NU)], give.at[d - 1]))
    copies = [pltpu.make_async_copy(s, t, sem.at[i]) for i, (s, t) in enumerate(pairs)]
    for copy in copies:
        copy.start()
    for copy in copies:
        copy.wait()


def convolve(scalars, weights, ins, joined_out, chunk, after):
    consts = [jnp.asarray(t) for t in tables()]
    if joined_out:
        shapes = [(NU, NZ, 16, 128)]
    else:
        shapes = [BLOCK, BLOCK, (3, *BLOCK), (3, *BLOCK)]
    return pl.pallas_call(
        functools.partial(convolve_kernel, len(ins) == 1, joined_out, chunk, len(after)),
        out_shape=[jax.ShapeDtypeStruct(s, F32) for s in shapes],
        in_specs=[SMEM, SMEM] + [HBM] * (len(ins) + len(consts) + len(after)),
        out_specs=[HBM] * len(shapes),
        scratch_shapes=[
            pltpu.VMEM((NZ * NU + 1, 16, 128), F32),
            pltpu.VMEM((NZ * NU + 1, 16, 128), F32),
            pltpu.SemaphoreType.DMA((2 * NZ,)),
            pltpu.SemaphoreType.DMA((12,)),
        ]
        + [pltpu.VMEM(t.shape, t.dtype) for t in consts],
        compiler_params=pltpu.CompilerParams(vmem_limit_bytes=LIMIT),
        cost_estimate=pl.CostEstimate(flops=6 * 10**9, bytes_accessed=1 << 22, transcendentals=0),
        name="convolve",
    )(scalars, weights, *ins, *consts, *after)


def unpack_kernel(joined, scalars, ins, outs):
    z, sign = scalars[0][0], scalars[0][1]

    def put(shift, even, odd):
        start = pl.multiple_of(around(z, shift) * 128, 128)
        for o in range(2):
            real, imag = interleave(even[o], odd[o])
            outs[o][0, pl.ds(start, 128), :] = real.reshape(128, 128)
            outs[o][1, pl.ds(start, 128), :] = imag.reshape(128, 128)

    if joined:
        v = ins[0]
        for shift in range(-3, 5):
            if shift in (0, 4):
                even, odd = (0, shift // 4), (1, shift // 4)
            elif shift < 0:
                even, odd = (0, -2 * shift), (0, -2 * shift + 1)
            else:
                even, odd = (1, 2 * shift + 1), (1, 2 * shift)
            put(shift, [v[:, *even, o] for o in range(2)], [v[:, *odd, o] for o in range(2)])
    else:
        own, far, *paid, got = ins
        put(0, *[[own[:, c, 0, o] for o in range(2)] for c in range(2)])
        put(4, *[[far[:, c, o] for o in range(2)] for c in range(2)])
        for d in STEPS:
            put(-sign * d, *[[paid[d - 1][:, c, 0, o] for o in range(2)] for c in range(2)])
            put(sign * d, *[[got[d - 1, :, c, o] for o in range(2)] for c in range(2)])


def unpack(scalars, ins, chunk, old):
    half = pl.BlockSpec((2, 1024, 128), lambda i, *_: (0, chunk, 0))
    joined = len(ins) == 1
    if joined:
        ins = [ins[0].reshape(NXY, 2, NZ, 2, 8, 128)]
    else:
        own, far, *paid, got = ins
        ins = [own.reshape(NXY, 2, NZ, 2, 8, 128), far.reshape(NXY, 2, 2, 8, 128)]
        ins += [x.reshape(NXY, 2, 2, 2, 8, 128) for x in paid]
        ins.append(got.reshape(3, NXY, 2, 2, 8, 128))
    return local_call(
        functools.partial(unpack_kernel, joined),
        scalars,
        ins,
        [whole(x.shape) for x in ins],
        old,
        [(2, 2048, 128)] * 2,
        [half, half],
        "unpack",
        {1 + len(ins) + i: i for i in range(len(old))},
    )


def to_ring(x, shift):
    moves = []
    for zh in range(2):
        for c in range(2):
            for zl in range(4):
                to = (zh * 4 + zl + (1 - 2 * c) * shift) % NZ
                moves.append((zh * 8 + c * 4 + zl, (to // 4) * 8 + c * 4 + to % 4))
    return lax.ppermute(x, ("zh", "c", "zl"), moves)


def to_far(x):
    return lax.ppermute(x, RING, [(i, (i + 4) % NZ) for i in range(NZ)])


def to_core(x):
    return lax.ppermute(x, "c", [(0, 1), (1, 0)])


def over_plane(x):
    return lax.all_to_all(x, PLANE, split_axis=0, concat_axis=0, tiled=True)


def shards(green_lesser, green_greater, screen, couple):
    z = lax.axis_index(RING).astype(jnp.int32)
    u = lax.axis_index(PLANE).astype(jnp.int32)
    scalars = jnp.stack([z, 1 - 2 * lax.rem(u, 2)])
    own, far, keep, give, gains = pack_ring(scalars, green_lesser, green_greater, screen, couple)
    far = to_far(far)
    got = to_core(give)
    rows = [
        jnp.concatenate([keep[d - 1].reshape(512, 128), got[d - 1].reshape(512, 128), gains[d]], axis=0)
        for d in STEPS
    ]
    second = over_plane(pack_plane(scalars, green_lesser, green_greater, rows))
    rows = [to_ring(x, d) for d, x in zip(STEPS, rows)]
    paid = [x.reshape(129, 8, 128) for x in rows]

    far2, paid2 = fan(scalars, second, [])
    order = [paid2[0]]
    far2 = to_far(far2)
    paid2 = [to_ring(x, d) for d, x in zip(STEPS, paid2)]

    first = merge(scalars, own, far, paid, order)
    gains = jnp.stack([gains[0, :4]] + [x[1024:1028] for x in rows])
    weights = lax.dynamic_slice(gains, (0, 0, u * KK), (4, 4, KK)).reshape(-1)
    first = over_plane(first)
    own, far, keep, give = convolve(scalars, weights, [first], False, 0, [])
    far = to_far(far)
    got = to_core(give)
    paid = [jnp.concatenate([keep[d - 1], got[d - 1]], axis=0) for d in STEPS]
    order = [paid[0]]
    paid = [to_ring(x, d).reshape(128, 8, 128) for d, x in zip(STEPS, paid)]

    got2 = to_core(jnp.stack([x[:, 1] for x in paid2]))
    (second,) = convolve(scalars, weights, [second, far2, *paid2, got2], True, 1, order)
    second = over_plane(second)
    far2, paid2 = fan(scalars, second, [])
    order = [paid2[0]]
    far2 = to_far(far2)
    paid2 = [to_ring(x, d) for d, x in zip(STEPS, paid2)]

    first = over_plane(merge(scalars, own, far, paid, order))
    done = unpack(scalars, [first], 0, [])
    got2 = to_core(jnp.stack([x[:, 1] for x in paid2]))
    polar, sigma = unpack(scalars, [second, far2, *paid2, got2], 1, done)
    return polar, sigma


def solution(mesh):
    named = Mesh(mesh.devices.reshape(SIZES), AXES)
    placed = P(None, "zl", ("x", "zh", "y", "c"))
    return jax.shard_map(
        shards,
        mesh=named,
        in_specs=(placed, placed, P("zl"), P("zl")),
        out_specs=(placed, placed),
        check_vma=False,
    )
```

time: 438 us -> 289 us (0.66)
  Pallas kernels: 151 us -> 51.6 us
  blocking collectives: 36.5 us -> 0 us
  waiting for transfers between devices: 125 us -> 106 us
  other arithmetic: 0.02 us -> 6.79 us
    pallas_call x6 -> x8, Pallas kernels: 134 us -> 29.9 us  [local_call(): pl.pallas_call(lambda *refs: kernel(refs[:1], refs[1:1 + count], refs[1 +...]
    ppermute x28 -> x20, waiting for transfers between devices: 123 us -> 54.7 us  [the longest x12 42.9 us: to_ring(): return lax.ppermute(x, ('zh', 'c', 'zl'), moves)]
    all_to_all x4, waiting for transfers between devices: 2.17 us -> 51.4 us  [over_plane(): return lax.all_to_all(x, PLANE, split_axis=0, concat_axis=0, tiled=True)]
    all_gather x1 -> x0, blocking collectives: 36.5 us -> none  [shards(): gains = lax.all_gather(jnp.stack([screen, couple]), 'zl')]
    ppermute x28 -> x20, starting transfers between devices: 62.7 us -> 50.5 us  [the longest x12 21.9 us: to_ring(): return lax.ppermute(x, ('zh', 'c', 'zl'), moves)]
    all_to_all x4, starting transfers between devices: 35.5 us -> 46.5 us  [over_plane(): return lax.all_to_all(x, PLANE, split_axis=0, concat_axis=0, tiled=True)]
    unnamed x94 -> x36, local copies, waits for them, and re-layouts: 19.1 us -> 8.45 us
    pallas_call x0 -> x5, local copies, waits for them, and re-layouts: none -> 5.44 us  [local_call(): pl.pallas_call(lambda *refs: kernel(refs[:1], refs[1:1 + count], refs[1 +...]
  transfers between devices with their start and end apart: 32 -> 24, of which waited for: 17 -> 12; matrix products, arithmetic and copies ran while one was open for 1% -> 7% of each run, Pallas kernels for 34% -> 9%
where the time goes in v2:
time: 289 us; the launch traced here: 288 us
  waiting for transfers between devices  106 us (37%)
  starting transfers between devices  97 us (34%)
  Pallas kernels  51.6 us (18%)
  local copies, waits for them, and re-layouts  25.7 us (9%)
  other arithmetic  6.79 us (2%)
    all_to_all x4, waiting for transfers between devices, over_plane(): return lax.all_to_all(x, PLANE, split_axis=0, concat_axis=0, tiled=True)  51.4 us
    all_to_all x4, starting transfers between devices, over_plane(): return lax.all_to_all(x, PLANE, split_axis=0, concat_axis=0, tiled=True)  46.5 us
    ppermute x12, waiting for transfers between devices, to_ring(): return lax.ppermute(x, ('zh', 'c', 'zl'), moves)  42.9 us
    pallas_call x8, Pallas kernels, local_call(): pl.pallas_call(lambda *refs: kernel(refs[:1], refs[1:1 + count], refs[1 +...  29.9 us
    ppermute x12, starting transfers between devices, to_ring(): return lax.ppermute(x, ('zh', 'c', 'zl'), moves)  21.9 us
    pallas_call x2, Pallas kernels, convolve(): pl.pallas_call(functools.partial(convolve_kernel, len(ins) == 1, joined_o...  21.7 us
    ppermute x4, starting transfers between devices, to_far(): return lax.ppermute(x, RING, [(i, (i + 4) % NZ) for i in range(NZ)])  16.2 us
    ppermute x4, starting transfers between devices, to_core(): return lax.ppermute(x, 'c', [(0, 1), (1, 0)])  12.4 us
  transfers between devices with their start and end apart: 24, of which 12 were waited for; matrix products, arithmetic and copies ran while one was open for 7% of the time, Pallas kernels for 9%

profile of v2, /device:TPU:1, one launch (start us, length us, event | category | flops | bytes accessed | tf_op | source)
XLA Modules:
  0.0 288.1 jit_solution(4021372279333264603)
XLA Ops:
  1.3 3.7 %pack_ring.1 = (f32[16,2,2,8,128]{4,3,2,1,0:T(8,128)}, f32[16,2,2,8,128]{4,3,2,1,0:T(8,128)}, f32[3,16,2,2,8,128]{5,4,3,2,1,0:T(8,128)}, f32[3,16,2,2,8,128]{5,4,3,2,1,0:T(8,128)}, f32[4,8,128]{2,1,0:T(8,128)}) custom-call(s32[2]{0:T(128)} %pad_add_fusion.refs_0_, f32[2,2048,128]{2,1,0:T(8,128)} %refs_1_.3, f32[2,2048,128]{2,1,0:T(8,128)} %refs_2_.3, ...), custom_call_target="tpu_custom_call" | custom-call | flops 1048576 | bytes 4194304 | tf_op jit(solution)/shard_map/pack_ring/pallas_call | solution.py:89
  5.0 3.2 %collective-permute-start = (f32[3,32,16,128]{3,2,1,0:T(8,128)}, f32[3,32,16,128]{3,2,1,0:T(8,128)S(1)}, u32[]{:S(2)}, u32[]{:S(2)}) collective-permute-start(f32[3,32,16,128]{3,2,1,0:T(8,128)} %bitcast.80), channel_id=1, source_target_pairs={{0,4},{4,0},{1,5},{5,1},{2,6},{6,2},{3,7},{7,3},{8,12},{12,8},{9,1... | collective-permute-start | bytes 2359304 | tf_op jit(solution)/shard_map/ppermute | solution.py:421
  12.9 3.7 %pack_plane.1 = f32[16,2,8,2,8,128]{5,4,3,2,1,0:T(8,128)} custom-call(s32[2]{0:T(128)} %pad_add_fusion.refs_0_, f32[2,2048,128]{2,1,0:T(8,128)} %refs_1_.3, f32[2,2048,128]{2,1,0:T(8,128)} %refs_2_.3, f32[1032,128]{1,0:T(8,128)} %pad_maximum_fusion.2.refs_3_, f32[1032,128]{1,0:T(8,128)} %pad_maximum_fusion.3.refs_4_, f32[1032,128]{1,0:T(8,128)} %pad_maximum_fusion.4.refs_5_), custom_call_target="tpu_custom_call" | custom-call | flops 1048576 | bytes 4194304 | tf_op jit(solution)/shard_map/pack_plane/pallas_call | solution.py:89
  16.6 5.9 %all-to-all-start = ((f32[32,8,16,128]{3,2,1,0:T(8,128)}), f32[32,8,16,128]{3,2,1,0:T(8,128)S(1)}, u32[]{:S(2)}, u32[]{:S(2)}) async-start(f32[32,8,16,128]{3,2,1,0:T(8,128)} %bitcast.64), calls=%async_computation | async-start | bytes 4194304 | tf_op jit(solution)/shard_map/all_to_all | solution.py:425
  22.5 6.1 %collective-permute-start.2 = (f32[1032,128]{1,0:T(8,128)}, f32[1032,128]{1,0:T(8,128)}, u32[]{:S(2)}, u32[]{:S(2)}) collective-permute-start(f32[1032,128]{1,0:T(8,128)} %pad_maximum_fusion.3.refs_4_), channel_id=1, source_target_pairs={{0,2},{1,3},{2,32},{3,33},{4,38},{5,39},{6,4},{7,5},{32,34},{33,35... | collective-permute-start | bytes 1585160 | tf_op jit(solution)/shard_map/ppermute | solution.py:413
  29.9 4.4 %collective-permute-start.9 = (f32[32,16,128]{2,1,0:T(8,128)}, f32[32,16,128]{2,1,0:T(8,128)S(1)}, u32[]{:S(2)}, u32[]{:S(2)}) collective-permute-start(f32[32,16,128]{2,1,0:T(8,128)} %bitcast.81), channel_id=1, source_target_pairs={{0,32},{1,33},{2,34},{3,35},{32,0},{33,1},{34,2},{35,3},{4,36},{5,... | collective-permute-start | bytes 786440 | tf_op jit(solution)/shard_map/ppermute | solution.py:417
  34.3 16.5 %all-to-all-done.refs_1_.refs_2_ = f32[32,8,16,128]{3,2,1,0:T(8,128)S(1)} async-done(((f32[32,8,16,128]{3,2,1,0:T(8,128)}), f32[32,8,16,128]{3,2,1,0:T(8,128)S(1)}, u32[]{:S(2)}, u32[]{:S(2)}) %all-to-all-start) | async-done | bytes 2097184 | tf_op jit(solution)/shard_map/all_to_all | solution.py:425
  52.1 3.5 %fan.2 = (f32[32,16,128]{2,1,0:T(8,128)}, f32[32,2,16,128]{3,2,1,0:T(8,128)}, f32[32,2,16,128]{3,2,1,0:T(8,128)}, f32[32,2,16,128]{3,2,1,0:T(8,128)}) custom-call(s32[2]{0:T(128)} %pad_add_fusion.refs_0_, f32[32,8,16,128]{3,2,1,0:T(8,128)} %copy-done.1), custom_call_target="tpu_custom_call" | custom-call | flops 1048576 | bytes 4194304 | tf_op jit(solution)/shard_map/fan/pallas_call | solution.py:89
  57.9 5.3 %collective-permute-done.3 = f32[1032,128]{1,0:T(8,128)} collective-permute-done((f32[1032,128]{1,0:T(8,128)S(1)}, f32[1032,128]{1,0:T(8,128)}, u32[]{:S(2)}, u32[]{:S(2)}) %collective-permute-start.3) | collective-permute-done | bytes 528416 | tf_op jit(solution)/shard_map/ppermute | solution.py:413
  63.2 11.3 %collective-permute-done.1 = f32[1032,128]{1,0:T(8,128)} collective-permute-done((f32[1032,128]{1,0:T(8,128)S(1)}, f32[1032,128]{1,0:T(8,128)}, u32[]{:S(2)}, u32[]{:S(2)}) %collective-permute-start.1) | collective-permute-done | bytes 528416 | tf_op jit(solution)/shard_map/ppermute | solution.py:413
  74.5 3.6 %merge.2 = f32[32,8,16,128]{3,2,1,0:T(8,128)} custom-call(s32[2]{0:T(128)} %pad_add_fusion.refs_0_, f32[32,16,128]{2,1,0:T(8,128)} %bitcast.76, f32[32,16,128]{2,1,0:T(8,128)} %copy-done.13, f32[129,8,128]{2,1,0:T(8,128)} %bitcast.23.refs_3_, f32[129,8,128]{2,1,0:T(8,128)} %bitcast.24.refs_4_, f32[129,8,128]{2,1,0:T(8,128)} %bitcast.25.refs_5_, ...), custom_call_target="tpu_custom_call" | custom-call | flops 1048576 | bytes 4194304 | tf_op jit(solution)/shard_map/merge/pallas_call | solution.py:89
  78.2 9.3 %all-to-all-start.1 = ((f32[32,8,16,128]{3,2,1,0:T(8,128)}), f32[32,8,16,128]{3,2,1,0:T(8,128)S(1)}, u32[]{:S(2)}, u32[]{:S(2)}) async-start(f32[32,8,16,128]{3,2,1,0:T(8,128)} %merge.2), calls=%async_computation.1 | async-start | bytes 4194304 | tf_op jit(solution)/shard_map/all_to_all | solution.py:425
  97.5 3.0 %collective-permute-start.6 = (f32[32,2,16,128]{3,2,0,1:T(8,128)}, f32[32,2,16,128]{3,2,0,1:T(8,128)}, u32[]{:S(2)}, u32[]{:S(2)}) collective-permute-start(f32[32,2,16,128]{3,2,0,1:T(8,128)} %copy.21), channel_id=1, source_target_pairs={{0,2},{1,3},{2,32},{3,33},{4,38},{5,39},{6,4},{7,5},{32,34},{33,35... | collective-permute-start | bytes 1572872 | tf_op jit(solution)/shard_map/ppermute | solution.py:413
  100.6 15.2 %all-to-all-done.1.refs_2_ = f32[32,8,16,128]{3,2,1,0:T(8,128)S(1)} async-done(((f32[32,8,16,128]{3,2,1,0:T(8,128)}), f32[32,8,16,128]{3,2,1,0:T(8,128)S(1)}, u32[]{:S(2)}, u32[]{:S(2)}) %all-to-all-start.1) | async-done | bytes 2097184 | tf_op jit(solution)/shard_map/all_to_all | solution.py:425
  117.1 10.9 %convolve.2 = (f32[32,16,128]{2,1,0:T(8,128)}, f32[32,16,128]{2,1,0:T(8,128)}, f32[3,32,16,128]{3,2,1,0:T(8,128)}, f32[3,32,16,128]{3,2,1,0:T(8,128)}) custom-call(s32[2]{0:T(128)} %pad_add_fusion.refs_0_, f32[64]{0:T(128)} %reshape.74.refs_1_, f32[32,8,16,128]{3,2,1,0:T(8,128)} %copy-done.5, bf16[128,128]{1,0:T(8,128)(2,1)} %constant.58.clone.refs_3_.refs_8_, ...), custom_call_target="tpu_custom_call" | custom-call | flops 6000000000 | bytes 4194304 | tf_op jit(solution)/shard_map/convolve/pallas_call | solution.py:336
  130.1 5.8 %collective-permute-start.4 = (f32[32,16,128]{2,1,0:T(8,128)S(1)}, f32[32,16,128]{2,1,0:T(8,128)S(1)}, u32[]{:S(2)}, u32[]{:S(2)}) collective-permute-start(f32[32,16,128]{2,1,0:T(8,128)S(1)} %copy-done.16), channel_id=1, source_target_pairs={{0,32},{1,33},{2,34},{3,35},{32,0},{33,1},{34,2},{35,3},{4,36},{5,... | collective-permute-start | bytes 786440 | tf_op jit(solution)/shard_map/ppermute | solution.py:417
  140.4 2.4 collective-permute-done.4.refs_3_
  144.5 10.8 %convolve.3 = f32[32,8,16,128]{3,2,1,0:T(8,128)} custom-call(s32[2]{0:T(128)} %pad_add_fusion.refs_0_, f32[64]{0:T(128)} %reshape.74.refs_1_, f32[32,8,16,128]{3,2,1,0:T(8,128)} %copy-done.1, f32[32,16,128]{2,1,0:T(8,128)} %copy-done.17, f32[32,2,16,128]{3,2,1,0:T(8,128)} %copy.23.refs_4_, f32[32,2,16,128]{3,2,1,0:T(8,128)} %copy.24.refs_5_, ...), custom_call_target="tpu_custom_call" | custom-call | flops 6000000000 | bytes 4194304 | tf_op jit(solution)/shard_map/convolve/pallas_call | solution.py:336
  155.3 13.0 %all-to-all-start.2 = ((f32[32,8,16,128]{3,2,1,0:T(8,128)}), f32[32,8,16,128]{3,2,1,0:T(8,128)S(1)}, u32[]{:S(2)}, u32[]{:S(2)}) async-start(f32[32,8,16,128]{3,2,1,0:T(8,128)} %convolve.3), calls=%async_computation.2 | async-start | bytes 4194304 | tf_op jit(solution)/shard_map/all_to_all | solution.py:425
  169.2 4.7 %collective-permute-start.18 = (f32[64,16,128]{2,1,0:T(8,128)}, f32[64,16,128]{2,1,0:T(8,128)}, u32[]{:S(2)}, u32[]{:S(2)}) collective-permute-start(f32[64,16,128]{2,1,0:T(8,128)} %pad_maximum_fusion.6), channel_id=1, source_target_pairs={{0,2},{1,3},{2,32},{3,33},{4,38},{5,39},{6,4},{7,5},{32,34},{33,35... | collective-permute-start | bytes 1572872 | tf_op jit(solution)/shard_map/ppermute | solution.py:413
  176.9 19.7 %all-to-all-done.2.refs_1_ = f32[32,8,16,128]{3,2,1,0:T(8,128)S(1)} async-done(((f32[32,8,16,128]{3,2,1,0:T(8,128)}), f32[32,8,16,128]{3,2,1,0:T(8,128)S(1)}, u32[]{:S(2)}, u32[]{:S(2)}) %all-to-all-start.2) | async-done | bytes 2097184 | tf_op jit(solution)/shard_map/all_to_all | solution.py:425
  197.9 3.5 %fan.3 = (f32[32,16,128]{2,1,0:T(8,128)}, f32[32,2,16,128]{3,2,1,0:T(8,128)}, f32[32,2,16,128]{3,2,1,0:T(8,128)}, f32[32,2,16,128]{3,2,1,0:T(8,128)}) custom-call(s32[2]{0:T(128)} %pad_add_fusion.refs_0_, f32[32,8,16,128]{3,2,1,0:T(8,128)} %copy-done), custom_call_target="tpu_custom_call" | custom-call | flops 1048576 | bytes 4194304 | tf_op jit(solution)/shard_map/fan/pallas_call | solution.py:89
  203.3 5.9 %collective-permute-done.19 = f32[64,16,128]{2,1,0:T(8,128)S(1)} collective-permute-done((f32[64,16,128]{2,1,0:T(8,128)}, f32[64,16,128]{2,1,0:T(8,128)S(1)}, u32[]{:S(2)}, u32[]{:S(2)}) %collective-permute-start.19) | collective-permute-done | bytes 524320 | tf_op jit(solution)/shard_map/ppermute | solution.py:413
  210.0 3.6 %merge.3 = f32[32,8,16,128]{3,2,1,0:T(8,128)} custom-call(s32[2]{0:T(128)} %pad_add_fusion.refs_0_, f32[32,16,128]{2,1,0:T(8,128)} %get-tuple-element.36.refs_1_, f32[32,16,128]{2,1,0:T(8,128)} %copy-done.12, f32[128,8,128]{2,1,0:T(8,128)} %bitcast.37.refs_3_, f32[128,8,128]{2,1,0:T(8,128)} %bitcast.40.refs_4_, f32[128,8,128]{2,1,0:T(8,128)} %bitcast.75, ...), custom_call_target="tpu_custom_call" | custom-call | flops 1048576 | bytes 4194304 | tf_op jit(solution)/shard_map/merge/pallas_call | solution.py:89
  213.7 18.4 %all-to-all-start.3 = ((f32[32,8,16,128]{3,2,1,0:T(8,128)}), f32[32,8,16,128]{3,2,1,0:T(8,128)S(1)}, u32[]{:S(2)}, u32[]{:S(2)}) async-start(f32[32,8,16,128]{3,2,1,0:T(8,128)} %merge.3), calls=%async_computation.3 | async-start | bytes 4194304 | tf_op jit(solution)/shard_map/all_to_all | solution.py:425
  235.8 10.5 %collective-permute-done.13 = f32[32,2,16,128]{3,2,0,1:T(8,128)S(1)} collective-permute-done((f32[32,2,16,128]{3,2,0,1:T(8,128)S(1)}, f32[32,2,16,128]{3,2,0,1:T(8,128)S(1)}, u32[]{:S(2)}, u32[]{:S(2)}) %collective-permute-start.13) | collective-permute-done | bytes 524320 | tf_op jit(solution)/shard_map/ppermute | solution.py:413
  246.2 9.9 %collective-permute-done.14 = f32[32,2,16,128]{3,2,1,0:T(8,128)S(1)} collective-permute-done((f32[32,2,16,128]{3,2,1,0:T(8,128)}, f32[32,2,16,128]{3,2,1,0:T(8,128)S(1)}, u32[]{:S(2)}, u32[]{:S(2)}) %collective-permute-start.14) | collective-permute-done | bytes 524320 | tf_op jit(solution)/shard_map/ppermute | solution.py:413
  257.2 8.1 %collective-permute-start.15 = (f32[3,32,16,128]{3,2,1,0:T(8,128)}, f32[3,32,16,128]{3,2,1,0:T(8,128)}, u32[]{:S(2)}, u32[]{:S(2)}) collective-permute-start(f32[3,32,16,128]{3,2,1,0:T(8,128)} %pad_maximum_fusion.1), channel_id=1, source_target_pairs={{0,4},{4,0},{1,5},{5,1},{2,6},{6,2},{3,7},{7,3},{8,12},{12,8},{9,1... | collective-permute-start | bytes 2359304 | tf_op jit(solution)/shard_map/ppermute | solution.py:421
  265.3 4.0 %collective-permute-start.11 = (f32[32,16,128]{2,1,0:T(8,128)}, f32[32,16,128]{2,1,0:T(8,128)S(1)}, u32[]{:S(2)}, u32[]{:S(2)}) collective-permute-start(f32[32,16,128]{2,1,0:T(8,128)} %get-tuple-element.32), channel_id=1, source_target_pairs={{0,32},{1,33},{2,34},{3,35},{32,0},{33,1},{34,2},{35,3},{4,36},{5,... | collective-permute-start | bytes 786440 | tf_op jit(solution)/shard_map/ppermute | solution.py:417
  272.4 3.7 %unpack.2 = (f32[2,2048,128]{2,1,0:T(8,128)}, f32[2,2048,128]{2,1,0:T(8,128)}) custom-call(s32[2]{0:T(128)} %pad_add_fusion.refs_0_, f32[16,2,8,2,8,128]{5,4,3,2,1,0:T(8,128)} %bitcast.65), custom_call_target="tpu_custom_call" | custom-call | flops 1048576 | bytes 4194304 | tf_op jit(solution)/shard_map/unpack/pallas_call | solution.py:89
  276.1 6.8 %collective-permute-done.11 = f32[32,16,128]{2,1,0:T(8,128)S(1)} collective-permute-done((f32[32,16,128]{2,1,0:T(8,128)}, f32[32,16,128]{2,1,0:T(8,128)S(1)}, u32[]{:S(2)}, u32[]{:S(2)}) %collective-permute-start.11) | collective-permute-done | bytes 262176 | tf_op jit(solution)/shard_map/ppermute | solution.py:417
  283.7 4.5 %unpack.3 = (f32[2,2048,128]{2,1,0:T(8,128)}, f32[2,2048,128]{2,1,0:T(8,128)}) custom-call(s32[2]{0:T(128)} %pad_add_fusion.refs_0_, f32[16,2,8,2,8,128]{5,4,3,2,1,0:T(8,128)} %bitcast.63, f32[16,2,2,8,128]{4,3,2,1,0:T(8,128)} %bitcast.77, f32[16,2,2,2,8,128]{5,4,3,2,1,0:T(8,128)} %bitcast.66, ...), custom_call_target="tpu_custom_call", output_to_operand_aliasing={{0}: (7, {}), {1}: (8, {})} | custom-call | flops 1048576 | bytes 4194304 | tf_op jit(solution)/shard_map/unpack/pallas_call | solution.py:89
  (98 shorter events, 46.2 us)
Async XLA Ops:
  5.0 5.4 %collective-permute-start = (f32[3,32,16,128]{3,2,1,0:T(8,128)}, f32[3,32,16,128]{3,2,1,0:T(8,128)S(1)}, u32[]{:S(2)}, u32[]{:S(2)}) collective-permute-start(f32[3,32,16,128]{3,2,1,0:T(8,128)} %bitcast.80), channel_id=1, source_target_pairs={{0,4},{4,0},{1,5},{5,1},{2,6},{6,2},{3,7},{7,3},{8,12},{12,8},{9,1... | collective-permute-start | bytes 2359304 | tf_op jit(solution)/shard_map/ppermute | solution.py:421
  16.6 12.0 %copy-start.4 = (f32[1032,128]{1,0:T(8,128)S(1)}, f32[1032,128]{1,0:T(8,128)}, u32[]{:S(2)}) copy-start(f32[1032,128]{1,0:T(8,128)} %pad_maximum_fusion.4.refs_5_) | copy-start | bytes 1585156
  16.6 12.7 %copy-start.3 = (f32[1032,128]{1,0:T(8,128)S(1)}, f32[1032,128]{1,0:T(8,128)}, u32[]{:S(2)}) copy-start(f32[1032,128]{1,0:T(8,128)} %pad_maximum_fusion.2.refs_3_) | copy-start | bytes 1585156
  16.6 34.2 %all-to-all-start = ((f32[32,8,16,128]{3,2,1,0:T(8,128)}), f32[32,8,16,128]{3,2,1,0:T(8,128)S(1)}, u32[]{:S(2)}, u32[]{:S(2)}) async-start(f32[32,8,16,128]{3,2,1,0:T(8,128)} %bitcast.64), calls=%async_computation | async-start | bytes 4194304 | tf_op jit(solution)/shard_map/all_to_all | solution.py:425
  22.5 35.4 %collective-permute-start.2 = (f32[1032,128]{1,0:T(8,128)}, f32[1032,128]{1,0:T(8,128)}, u32[]{:S(2)}, u32[]{:S(2)}) collective-permute-start(f32[1032,128]{1,0:T(8,128)} %pad_maximum_fusion.3.refs_4_), channel_id=1, source_target_pairs={{0,2},{1,3},{2,32},{3,33},{4,38},{5,39},{6,4},{7,5},{32,34},{33,35... | collective-permute-start | bytes 1585160 | tf_op jit(solution)/shard_map/ppermute | solution.py:413
  28.6 34.6 %collective-permute-start.3 = (f32[1032,128]{1,0:T(8,128)S(1)}, f32[1032,128]{1,0:T(8,128)}, u32[]{:S(2)}, u32[]{:S(2)}) collective-permute-start(f32[1032,128]{1,0:T(8,128)S(1)} %copy-done.4), channel_id=1, source_target_pairs={{0,3},{1,32},{2,33},{3,34},{4,37},{5,38},{6,39},{7,4},{32,35},{33,... | collective-permute-start | bytes 1585160 | tf_op jit(solution)/shard_map/ppermute | solution.py:413
  29.3 45.2 %collective-permute-start.1 = (f32[1032,128]{1,0:T(8,128)S(1)}, f32[1032,128]{1,0:T(8,128)}, u32[]{:S(2)}, u32[]{:S(2)}) collective-permute-start(f32[1032,128]{1,0:T(8,128)S(1)} %copy-done.3), channel_id=1, source_target_pairs={{0,1},{1,2},{2,3},{3,32},{4,39},{5,4},{6,5},{7,6},{32,33},{33,34},... | collective-permute-start | bytes 1585160 | tf_op jit(solution)/shard_map/ppermute | solution.py:413
  29.9 28.0 %collective-permute-start.9 = (f32[32,16,128]{2,1,0:T(8,128)}, f32[32,16,128]{2,1,0:T(8,128)S(1)}, u32[]{:S(2)}, u32[]{:S(2)}) collective-permute-start(f32[32,16,128]{2,1,0:T(8,128)} %bitcast.81), channel_id=1, source_target_pairs={{0,32},{1,33},{2,34},{3,35},{32,0},{33,1},{34,2},{35,3},{4,36},{5,... | collective-permute-start | bytes 786440 | tf_op jit(solution)/shard_map/ppermute | solution.py:417
  57.9 16.6 %copy-start.13 = (f32[32,16,128]{2,1,0:T(8,128)}, f32[32,16,128]{2,1,0:T(8,128)S(1)}, u32[]{:S(2)}) copy-start(f32[32,16,128]{2,1,0:T(8,128)S(1)} %collective-permute-done.9.refs_2_) | copy-start | bytes 786436
  78.2 10.7 %copy-start.6 = (f32[32,2,16,128]{3,2,1,0:T(8,128)S(1)}, f32[32,2,16,128]{3,2,1,0:T(8,128)}, u32[]{:S(2)}) copy-start(f32[32,2,16,128]{3,2,1,0:T(8,128)} %get-tuple-element.25.refs_6_) | copy-start | bytes 1572868
  78.2 37.6 %all-to-all-start.1 = ((f32[32,8,16,128]{3,2,1,0:T(8,128)}), f32[32,8,16,128]{3,2,1,0:T(8,128)S(1)}, u32[]{:S(2)}, u32[]{:S(2)}) async-start(f32[32,8,16,128]{3,2,1,0:T(8,128)} %merge.2), calls=%async_computation.1 | async-start | bytes 4194304 | tf_op jit(solution)/shard_map/all_to_all | solution.py:425
  87.4 7.5 %copy-start.10 = (f32[32,2,16,128]{3,2,1,0:T(8,128)S(1)}, f32[32,2,16,128]{3,2,1,0:T(8,128)}, u32[]{:S(2)}) copy-start(f32[32,2,16,128]{3,2,1,0:T(8,128)} %get-tuple-element.27) | copy-start | bytes 1572868
  89.7 10.9 %collective-permute-start.5 = (f32[32,2,16,128]{3,2,0,1:T(8,128)}, f32[32,2,16,128]{3,2,0,1:T(8,128)S(1)}, u32[]{:S(2)}, u32[]{:S(2)}) collective-permute-start(f32[32,2,16,128]{3,2,0,1:T(8,128)} %copy.20), channel_id=1, source_target_pairs={{0,1},{1,2},{2,3},{3,32},{4,39},{5,4},{6,5},{7,6},{32,33},{33,34},... | collective-permute-start | bytes 1572872 | tf_op jit(solution)/shard_map/ppermute | solution.py:413
  95.7 33.2 %collective-permute-start.7 = (f32[32,2,16,128]{3,2,0,1:T(8,128)}, f32[32,2,16,128]{3,2,0,1:T(8,128)S(1)}, u32[]{:S(2)}, u32[]{:S(2)}) collective-permute-start(f32[32,2,16,128]{3,2,0,1:T(8,128)} %copy.22), channel_id=1, source_target_pairs={{0,3},{1,32},{2,33},{3,34},{4,37},{5,38},{6,39},{7,4},{32,35},{33,... | collective-permute-start | bytes 1572872 | tf_op jit(solution)/shard_map/ppermute | solution.py:413
  97.5 31.4 %collective-permute-start.6 = (f32[32,2,16,128]{3,2,0,1:T(8,128)}, f32[32,2,16,128]{3,2,0,1:T(8,128)}, u32[]{:S(2)}, u32[]{:S(2)}) collective-permute-start(f32[32,2,16,128]{3,2,0,1:T(8,128)} %copy.21), channel_id=1, source_target_pairs={{0,2},{1,3},{2,32},{3,33},{4,38},{5,39},{6,4},{7,5},{32,34},{33,35... | collective-permute-start | bytes 1572872 | tf_op jit(solution)/shard_map/ppermute | solution.py:413
  127.9 11.6 %collective-permute-start.10 = (f32[3,32,16,128]{3,2,1,0:T(8,128)}, f32[3,32,16,128]{3,2,1,0:T(8,128)S(1)}, u32[]{:S(2)}, u32[]{:S(2)}) collective-permute-start(f32[3,32,16,128]{3,2,1,0:T(8,128)} %get-tuple-element.31), channel_id=1, source_target_pairs={{0,4},{4,0},{1,5},{5,1},{2,6},{6,2},{3,7},{7,3},{8,12},{12,8},{9,1... | collective-permute-start | bytes 2359304 | tf_op jit(solution)/shard_map/ppermute | solution.py:421
  129.9 9.6 %copy-start.8 = (f32[3,32,16,128]{3,2,1,0:T(8,128)S(1)}, f32[3,32,16,128]{3,2,1,0:T(8,128)}, u32[]{:S(2)}) copy-start(f32[3,32,16,128]{3,2,1,0:T(8,128)} %get-tuple-element.30) | copy-start | bytes 2359300
  130.0 12.9 %collective-permute-start.8 = (f32[3,32,16,128]{3,2,1,0:T(8,128)S(1)}, f32[3,32,16,128]{3,2,1,0:T(8,128)S(1)}, u32[]{:S(2)}, u32[]{:S(2)}) collective-permute-start(f32[3,32,16,128]{3,2,1,0:T(8,128)S(1)} %pad_maximum_fusion), channel_id=1, source_target_pairs={{0,4},{4,0},{1,5},{5,1},{2,6},{6,2},{3,7},{7,3},{8,12},{12,8},{9,1... | collective-permute-start | bytes 2359304 | tf_op jit(solution)/shard_map/ppermute | solution.py:421
  130.1 12.8 %collective-permute-start.4 = (f32[32,16,128]{2,1,0:T(8,128)S(1)}, f32[32,16,128]{2,1,0:T(8,128)S(1)}, u32[]{:S(2)}, u32[]{:S(2)}) collective-permute-start(f32[32,16,128]{2,1,0:T(8,128)S(1)} %copy-done.16), channel_id=1, source_target_pairs={{0,32},{1,33},{2,34},{3,35},{32,0},{33,1},{34,2},{35,3},{4,36},{5,... | collective-permute-start | bytes 786440 | tf_op jit(solution)/shard_map/ppermute | solution.py:417
  155.3 41.3 %all-to-all-start.2 = ((f32[32,8,16,128]{3,2,1,0:T(8,128)}), f32[32,8,16,128]{3,2,1,0:T(8,128)S(1)}, u32[]{:S(2)}, u32[]{:S(2)}) async-start(f32[32,8,16,128]{3,2,1,0:T(8,128)} %convolve.3), calls=%async_computation.2 | async-start | bytes 4194304 | tf_op jit(solution)/shard_map/all_to_all | solution.py:425
  168.3 35.0 %collective-permute-start.17 = (f32[64,16,128]{2,1,0:T(8,128)}, f32[64,16,128]{2,1,0:T(8,128)}, u32[]{:S(2)}, u32[]{:S(2)}) collective-permute-start(f32[64,16,128]{2,1,0:T(8,128)} %pad_maximum_fusion.5.refs_20_), channel_id=1, source_target_pairs={{0,1},{1,2},{2,3},{3,32},{4,39},{5,4},{6,5},{7,6},{32,33},{33,34},... | collective-permute-start | bytes 1572872 | tf_op jit(solution)/shard_map/ppermute | solution.py:413
  169.2 34.1 %collective-permute-start.18 = (f32[64,16,128]{2,1,0:T(8,128)}, f32[64,16,128]{2,1,0:T(8,128)}, u32[]{:S(2)}, u32[]{:S(2)}) collective-permute-start(f32[64,16,128]{2,1,0:T(8,128)} %pad_maximum_fusion.6), channel_id=1, source_target_pairs={{0,2},{1,3},{2,32},{3,33},{4,38},{5,39},{6,4},{7,5},{32,34},{33,35... | collective-permute-start | bytes 1572872 | tf_op jit(solution)/shard_map/ppermute | solution.py:413
  174.8 34.4 %collective-permute-start.19 = (f32[64,16,128]{2,1,0:T(8,128)}, f32[64,16,128]{2,1,0:T(8,128)S(1)}, u32[]{:S(2)}, u32[]{:S(2)}) collective-permute-start(f32[64,16,128]{2,1,0:T(8,128)} %pad_maximum_fusion.7), channel_id=1, source_target_pairs={{0,3},{1,32},{2,33},{3,34},{4,37},{5,38},{6,39},{7,4},{32,35},{33,... | collective-permute-start | bytes 1572872 | tf_op jit(solution)/shard_map/ppermute | solution.py:413
  174.9 28.5 %collective-permute-start.16 = (f32[32,16,128]{2,1,0:T(8,128)}, f32[32,16,128]{2,1,0:T(8,128)S(1)}, u32[]{:S(2)}, u32[]{:S(2)}) collective-permute-start(f32[32,16,128]{2,1,0:T(8,128)} %get-tuple-element.37), channel_id=1, source_target_pairs={{0,32},{1,33},{2,34},{3,35},{32,0},{33,1},{34,2},{35,3},{4,36},{5,... | collective-permute-start | bytes 786440 | tf_op jit(solution)/shard_map/ppermute | solution.py:417
  203.3 32.4 %collective-permute-start.12 = (f32[32,2,16,128]{3,2,0,1:T(8,128)}, f32[32,2,16,128]{3,2,0,1:T(8,128)S(1)}, u32[]{:S(2)}, u32[]{:S(2)}) collective-permute-start(f32[32,2,16,128]{3,2,0,1:T(8,128)} %copy.26), channel_id=1, source_target_pairs={{0,1},{1,2},{2,3},{3,32},{4,39},{5,4},{6,5},{7,6},{32,33},{33,34},... | collective-permute-start | bytes 1572872 | tf_op jit(solution)/shard_map/ppermute | solution.py:413
  213.7 18.4 %copy-start.11 = (f32[32,2,16,128]{3,2,1,0:T(8,128)S(1)}, f32[32,2,16,128]{3,2,1,0:T(8,128)}, u32[]{:S(2)}) copy-start(f32[32,2,16,128]{3,2,1,0:T(8,128)} %get-tuple-element.34) | copy-start | bytes 1572868
  213.7 57.4 %all-to-all-start.3 = ((f32[32,8,16,128]{3,2,1,0:T(8,128)}), f32[32,8,16,128]{3,2,1,0:T(8,128)S(1)}, u32[]{:S(2)}, u32[]{:S(2)}) async-start(f32[32,8,16,128]{3,2,1,0:T(8,128)} %merge.3), calls=%async_computation.3 | async-start | bytes 4194304 | tf_op jit(solution)/shard_map/all_to_all | solution.py:425
  232.1 14.1 %collective-permute-start.13 = (f32[32,2,16,128]{3,2,0,1:T(8,128)S(1)}, f32[32,2,16,128]{3,2,0,1:T(8,128)S(1)}, u32[]{:S(2)}, u32[]{:S(2)}) collective-permute-start(f32[32,2,16,128]{3,2,0,1:T(8,128)S(1)} %copy.28), channel_id=1, source_target_pairs={{0,2},{1,3},{2,32},{3,33},{4,38},{5,39},{6,4},{7,5},{32,34},{33,35... | collective-permute-start | bytes 1572872 | tf_op jit(solution)/shard_map/ppermute | solution.py:413
  234.5 21.6 %collective-permute-start.14 = (f32[32,2,16,128]{3,2,1,0:T(8,128)}, f32[32,2,16,128]{3,2,1,0:T(8,128)S(1)}, u32[]{:S(2)}, u32[]{:S(2)}) collective-permute-start(f32[32,2,16,128]{3,2,1,0:T(8,128)} %get-tuple-element.35), channel_id=1, source_target_pairs={{0,3},{1,32},{2,33},{3,34},{4,37},{5,38},{6,39},{7,4},{32,35},{33,... | collective-permute-start | bytes 1572872 | tf_op jit(solution)/shard_map/ppermute | solution.py:413
  256.1 14.9 %copy-start.7 = (f32[32,2,16,128]{3,2,1,0:T(8,128)}, f32[32,2,16,128]{3,2,1,0:T(8,128)S(1)}, u32[]{:S(2)}) copy-start(f32[32,2,16,128]{3,2,1,0:T(8,128)S(1)} %collective-permute-done.14) | copy-start | bytes 1572868
  257.2 25.8 %collective-permute-start.15 = (f32[3,32,16,128]{3,2,1,0:T(8,128)}, f32[3,32,16,128]{3,2,1,0:T(8,128)}, u32[]{:S(2)}, u32[]{:S(2)}) collective-permute-start(f32[3,32,16,128]{3,2,1,0:T(8,128)} %pad_maximum_fusion.1), channel_id=1, source_target_pairs={{0,4},{4,0},{1,5},{5,1},{2,6},{6,2},{3,7},{7,3},{8,12},{12,8},{9,1... | collective-permute-start | bytes 2359304 | tf_op jit(solution)/shard_map/ppermute | solution.py:421
  265.3 17.7 %collective-permute-start.11 = (f32[32,16,128]{2,1,0:T(8,128)}, f32[32,16,128]{2,1,0:T(8,128)S(1)}, u32[]{:S(2)}, u32[]{:S(2)}) collective-permute-start(f32[32,16,128]{2,1,0:T(8,128)} %get-tuple-element.32), channel_id=1, source_target_pairs={{0,32},{1,33},{2,34},{3,35},{32,0},{33,1},{34,2},{35,3},{4,36},{5,... | collective-permute-start | bytes 786440 | tf_op jit(solution)/shard_map/ppermute | solution.py:417
  (10 other events, 16.5 us)

commit v3 on v2

--- a/solution.py
+++ b/solution.py
@@ -18,6 +18,7 @@
 NZ, NU = 8, 32
 NXY = NU // 2
 STEPS = (1, 2, 3)
+PARTS = 1
 BLOCK = (NU, 16, 128)
 NJ, NB = 64, 128
 NE = NJ * NB
@@ -26,7 +27,9 @@
 HBM = pl.BlockSpec(memory_space=pl.ANY)
 VMEM = pl.BlockSpec(memory_space=pltpu.VMEM)
 SMEM = pl.BlockSpec(memory_space=pltpu.SMEM)
-LIMIT = 58 * 1024 * 1024
+LIMIT = 20 * 1024 * 1024
+FULL = 58 * 1024 * 1024
+LONG = 2 * 10**11
 
 
 def halves(table):
@@ -49,12 +52,11 @@
     polar_scale, sigma_scale = NE**-1.5, -(float(NE) ** -2)
     e1p = polar_scale * np.block([[-so, -co], [co, -so]])
     e1s = sigma_scale * np.block([[co, -so], [so, co]])
-    out = []
-    for table in (d1, d2, e2, e1p, e1s):
-        out.extend(halves(table))
-    out.append(np.cos(twist).astype(np.float32))
-    out.append(np.sin(twist).astype(np.float32))
-    return tuple(out)
+    products = [np.concatenate(halves(table), axis=1) for table in (d1, e1p, e1s)]
+    for table in (d2, e2):
+        products.extend(halves(table))
+    turns = np.concatenate([np.cos(twist), np.sin(twist)], axis=1).astype(np.float32)
+    return np.concatenate(products, axis=0), turns
 
 
 def split(x):
@@ -68,6 +70,12 @@
 
 def dot3(a, b):
     return dot(a[0], b[0]) + (dot(a[0], b[1]) + dot(a[1], b[0]))
+
+
+def dot_pair(table, first, second):
+    high, low = split(jnp.concatenate([first, second], axis=1))
+    out = dot(table, jnp.concatenate([high, high], axis=0)) + dot(table[:, :128], low)
+    return out[:, :NB], out[:, NB:]
 
 
 def interleave(first, second):
@@ -84,32 +92,46 @@
     return pl.BlockSpec(shape, lambda i, *_: (0,) * len(shape))
 
 
-def local_call(kernel, scalars, ins, in_specs, after, shapes, out_specs, name, aliases=None):
+def part(shape, dim, at=()):
+    block, fixed = list(shape), [0] * len(shape)
+    block[dim] //= PARTS
+    for where, length, index in at:
+        block[where], fixed[where] = length, index
+    return pl.BlockSpec(
+        tuple(block), lambda i, *_: tuple(i if n == dim else f for n, f in enumerate(fixed))
+    )
+
+
+def local_call(
+    kernel, scalars, ins, in_specs, after, shapes, out_specs, name, aliases=None, work=0, limit=LIMIT
+):
     count = len(ins)
     return pl.pallas_call(
-        lambda *refs: kernel(
-            refs[:1], refs[1 : 1 + count], refs[1 + count + len(after) :]
-        ),
+        lambda *refs: kernel(refs[:1], refs[1 : 1 + count], refs[1 + count + len(after) :]),
         out_shape=[jax.ShapeDtypeStruct(s, F32) for s in shapes],
         grid_spec=pltpu.PrefetchScalarGridSpec(
             num_scalar_prefetch=1,
-            grid=(1,),
+            grid=(PARTS,),
             in_specs=list(in_specs) + [HBM] * len(after),
             out_specs=out_specs,
         ),
         input_output_aliases=aliases or {},
-        compiler_params=pltpu.CompilerParams(vmem_limit_bytes=LIMIT),
-        cost_estimate=pl.CostEstimate(flops=1 << 20, bytes_accessed=1 << 22, transcendentals=0),
+        compiler_params=pltpu.CompilerParams(vmem_limit_bytes=limit),
+        cost_estimate=pl.CostEstimate(flops=work, bytes_accessed=0, transcendentals=0),
         name=name,
     )(scalars, *ins, *after)
 
 
+GRID_IN = (2, 2 * NZ, NXY, 8, 128)
+
+
+def chunk_part(chunk):
+    return part(GRID_IN, 2, [(1, NZ, chunk)])
+
+
 def blocks_of(lesser, greater, zd):
-    start = pl.multiple_of(zd * 128, 128)
     for g, ref in enumerate((lesser, greater)):
-        real = ref[0, pl.ds(start, 128), :].reshape(NXY, 8, 128)
-        imag = ref[1, pl.ds(start, 128), :].reshape(NXY, 8, 128)
-        yield g, *interleave(real, imag)
+        yield g, *interleave(ref[0, zd], ref[1, zd])
 
 
 def pack_ring_kernel(scalars, ins, outs):
@@ -126,23 +148,23 @@
     for d in range(4):
         zd = around(z, sign * d)
         rows = [ref[pl.ds(zd + q * NZ, 1), :] for ref in (screen, couple) for q in range(2)]
-        gains[d] = jnp.concatenate(rows + rows, axis=0)
+        gains[d] = jnp.concatenate(rows * 4, axis=0)
 
 
 def pack_ring(scalars, lesser, greater, screen, couple):
-    half = pl.BlockSpec((2, 1024, 128), lambda i, *_: (0, 0, 0))
     small = whole((16, 128))
     one = (NXY, 2, 2, 8, 128)
-    shapes = [one, one, (3, *one), (3, *one), (4, 8, 128)]
+    shapes = [one, one, (3, *one), (3, *one), (4, 16, 128)]
     own, far, keep, give, gains = local_call(
         pack_ring_kernel,
         scalars,
-        [lesser, greater, screen.reshape(16, 128), couple.reshape(16, 128)],
-        [half, half, small, small],
+        [lesser.reshape(GRID_IN), greater.reshape(GRID_IN), screen.reshape(16, 128), couple.reshape(16, 128)],
+        [chunk_part(0), chunk_part(0), small, small],
         [],
         shapes,
-        [whole(s) for s in shapes],
+        [part(one, 0), part(one, 0), part((3, *one), 1), part((3, *one), 1), whole((4, 16, 128))],
         "pack_ring",
+        limit=FULL,
     )
     return own.reshape(BLOCK), far.reshape(BLOCK), keep.reshape(3, *BLOCK), give.reshape(3, *BLOCK), gains
 
@@ -165,51 +187,83 @@
 
 
 def pack_plane(scalars, lesser, greater, after):
-    half = pl.BlockSpec((2, 1024, 128), lambda i, *_: (0, 1, 0))
     shape = (NXY, 2, NZ, 2, 8, 128)
     (out,) = local_call(
-        pack_plane_kernel, scalars, [lesser, greater], [half, half], after, [shape], [whole(shape)], "pack_plane"
+        pack_plane_kernel,
+        scalars,
+        [lesser.reshape(GRID_IN), greater.reshape(GRID_IN)],
+        [chunk_part(1), chunk_part(1)],
+        after,
+        [shape],
+        [part(shape, 0)],
+        "pack_plane",
+        limit=FULL,
     )
     return out.reshape(NU, NZ, 16, 128)
 
 
-def merge_kernel(scalars, ins, outs):
-    out = outs[0]
-    out[:, 0] = ins[0][...]
-    out[:, 1] = ins[1][...]
+def shuttle(ins, shapes, routes, name, through=None, after=(), work=LONG):
+    count, n_after = len(ins), len(after) + (through is not None)
+    extra = [] if through is None else [through]
+
+    def kernel(*refs):
+        outs = refs[count + n_after :]
+        held, in_sem, out_sem = refs[-3:]
+        pulls = [
+            pltpu.make_async_copy(refs[i].at[a], held.at[n], in_sem.at[n]) for n, (i, a, _, _) in enumerate(routes)
+        ]
+        pushes = [
+            pltpu.make_async_copy(held.at[n], outs[o].at[b], out_sem.at[n]) for n, (_, _, o, b) in enumerate(routes)
+        ]
+        for copy in pulls:
+            copy.start()
+        for pull, push in zip(pulls, pushes):
+            pull.wait()
+            push.start()
+        for copy in pushes:
+            copy.wait()
+
+    return pl.pallas_call(
+        kernel,
+        out_shape=[jax.ShapeDtypeStruct(s, F32) for s in shapes + [x.shape for x in extra]],
+        in_specs=[HBM] * (count + n_after),
+        out_specs=[HBM] * (len(shapes) + len(extra)),
+        scratch_shapes=[
+            pltpu.VMEM((len(routes), *BLOCK), F32),
+            pltpu.SemaphoreType.DMA((len(routes),)),
+            pltpu.SemaphoreType.DMA((len(routes),)),
+        ],
+        input_output_aliases={count: len(shapes)} if extra else {},
+        compiler_params=pltpu.CompilerParams(vmem_limit_bytes=LIMIT),
+        cost_estimate=pl.CostEstimate(flops=work, bytes_accessed=0, transcendentals=0),
+        name=name,
+    )(*ins, *extra, *after)
+
+
+ALL = slice(None)
+
+
+def merge(own, far, paid):
+    ins = [own.reshape(NU, 16, 128), far] + [x.reshape(-1, 16, 128) for x in paid]
+    routes = [(0, ALL, 0, (ALL, 0)), (1, ALL, 0, (ALL, 1))]
     for d in STEPS:
         for m in range(2):
-            out[:, 2 * d + m] = ins[1 + d][m * 64 : m * 64 + 64].reshape(BLOCK)
-
-
-def merge(scalars, own, far, paid, after):
-    ins = [own, far] + paid
-    out = (NU, NZ, 16, 128)
-    return local_call(
-        merge_kernel,
-        scalars,
-        ins,
-        [whole(x.shape) for x in ins],
-        after,
-        [out],
-        [whole(out)],
-        "merge",
-    )[0]
-
-
-def fan_kernel(scalars, ins, outs):
-    outs[0][...] = ins[0][:, 1]
+            routes.append((1 + d, pl.ds(m * NU, NU), 0, (ALL, 2 * d + m)))
+    return shuttle(ins, [(NU, NZ, 16, 128)], routes, "merge")[0]
+
+
+def give_back(paid, far):
+    routes = [(d - 1, 1, 0, d - 1) for d in STEPS]
+    return shuttle(paid, [(3, *BLOCK)], routes, "give", after=[far])[0]
+
+
+def fan(joined, through):
+    routes = [(0, (ALL, 1), 0, ALL)]
     for d in STEPS:
         for m in range(2):
-            outs[d][:, m] = ins[0][:, 2 * d + m]
-
-
-def fan(scalars, joined, after):
-    shapes = [BLOCK] + [(NU, 2, 16, 128)] * 3
-    out = local_call(
-        fan_kernel, scalars, [joined], [whole(joined.shape)], after, shapes, [whole(s) for s in shapes], "fan"
-    )
-    return out[0], list(out[1:])
+            routes.append((0, (ALL, 2 * d + m), d, m))
+    out = shuttle([joined], [BLOCK] + [(2, *BLOCK)] * 3, routes, "fan", through=through, work=0)
+    return out[0], list(out[1:4]), out[4]
 
 
 def convolve_kernel(joined_in, joined_out, chunk, n_after, *refs):
@@ -218,10 +272,10 @@
     refs = list(refs)
     scalars, weights = refs[:2]
     ins = refs[2 : 2 + n_in]
-    tabs = refs[2 + n_in : 14 + n_in]
-    outs = refs[14 + n_in + n_after : 14 + n_in + n_after + n_out]
-    xin, yout, sem, tab_sem = refs[14 + n_in + n_after + n_out :][:4]
-    held = refs[18 + n_in + n_after + n_out :]
+    tabs = refs[2 + n_in : 4 + n_in]
+    outs = refs[4 + n_in + n_after : 4 + n_in + n_after + n_out]
+    xin, yout, sem, tab_sem = refs[4 + n_in + n_after + n_out :][:4]
+    held = refs[8 + n_in + n_after + n_out :]
     z, sign = scalars[0], scalars[1]
 
     tab_copies = [pltpu.make_async_copy(t, h, tab_sem.at[i]) for i, (t, h) in enumerate(zip(tabs, held))]
@@ -247,7 +301,7 @@
         pairs.append((own.at[:, 0], xin.at[pl.ds(z * NU, NU)]))
         pairs.append((far, xin.at[pl.ds(around(z, 4) * NU, NU)]))
         for d in STEPS:
-            pairs.append((ins[1 + d].at[:, 0], xin.at[pl.ds(around(z, -sign * d) * NU, NU)]))
+            pairs.append((ins[1 + d].at[0], xin.at[pl.ds(around(z, -sign * d) * NU, NU)]))
             pairs.append((got.at[d - 1], xin.at[pl.ds(around(z, sign * d) * NU, NU)]))
     copies = [pltpu.make_async_copy(s, t, sem.at[i]) for i, (s, t) in enumerate(pairs)]
     for copy in copies + tab_copies:
@@ -255,23 +309,30 @@
     for copy in copies + tab_copies:
         copy.wait()
 
-    d1, d2, e2, e1p, e1s = [(held[2 * i][...], held[2 * i + 1][...]) for i in range(5)]
-    cos, sin = held[10][...], held[11][...]
+    products, turns = held
+    d1, e1p, e1s = [products[i * 128 : i * 128 + 128] for i in range(3)]
+    d2, e2 = [
+        (products[i * 512 + 384 : i * 512 + 640], products[i * 512 + 640 : i * 512 + 896]) for i in range(2)
+    ]
+    cos, sin = turns[:, :NB], turns[:, NB:]
     rows_in = xin.reshape((NZ * NU + 1) * 16, 128)
     rows_out = yout.reshape((NZ * NU + 1) * 16, 128)
 
     def step(kk, carry):
         turned = []
         for g in range(2):
-            for r in range(4):
-                parts = []
-                for c in range(2):
-                    for zh in range(2):
-                        base = (zh * 4 + r) * NU * 16 + g * 8 + c * KK + kk
-                        parts.append(rows_in[pl.ds(base, NU, stride=16), :])
-                y = dot3(d1, split(jnp.concatenate(parts, axis=0)))
-                yr, yi = y[:NJ], y[NJ:]
-                turned.append(jnp.concatenate([yr * cos + yi * sin, yi * cos - yr * sin], axis=1))
+            for r in (0, 2):
+                sides = []
+                for row in (r, r + 1):
+                    parts = []
+                    for c in range(2):
+                        for zh in range(2):
+                            base = (zh * 4 + row) * NU * 16 + g * 8 + c * KK + kk
+                            parts.append(rows_in[pl.ds(base, NU, stride=16), :])
+                    sides.append(jnp.concatenate(parts, axis=0))
+                for y in dot_pair(d1, *sides):
+                    yr, yi = y[:NJ], y[NJ:]
+                    turned.append(jnp.concatenate([yr * cos + yi * sin, yi * cos - yr * sin], axis=1))
         spec = dot3(split(jnp.concatenate(turned, axis=0)), d2)
         lr, li = spec[:256, :NB], spec[:256, NB:]
         gr, gi = spec[256:, :NB], spec[256:, NB:]
@@ -294,19 +355,21 @@
         )
         back = dot3(split(both), e2)
         for o in range(2):
-            for r in range(4):
-                part = back[(o * 4 + r) * NJ : (o * 4 + r + 1) * NJ]
-                ar, ai = part[:, :NB], part[:, NB:]
-                turn = jnp.concatenate([ar * cos - ai * sin, ai * cos + ar * sin], axis=0)
-                done = dot3((e1p, e1s)[o], split(turn))
-                for c in range(2):
-                    for zh in range(2):
-                        base = (zh * 4 + r) * NU * 16 + o * 8 + c * KK + kk
-                        at = (c * 2 + zh) * NU
-                        rows_out[pl.ds(base, NU, stride=16), :] = done[at : at + NU]
+            for r in (0, 2):
+                sides = []
+                for row in (r, r + 1):
+                    part = back[(o * 4 + row) * NJ : (o * 4 + row + 1) * NJ]
+                    ar, ai = part[:, :NB], part[:, NB:]
+                    sides.append(jnp.concatenate([ar * cos - ai * sin, ai * cos + ar * sin], axis=0))
+                for row, done in zip((r, r + 1), dot_pair((e1p, e1s)[o], *sides)):
+                    for c in range(2):
+                        for zh in range(2):
+                            base = (zh * 4 + row) * NU * 16 + o * 8 + c * KK + kk
+                            at = (c * 2 + zh) * NU
+                            rows_out[pl.ds(base, NU, stride=16), :] = done[at : at + NU]
         return carry
 
-    lax.fori_loop(0, KK, step, 0)
+    lax.fori_loop(0, KK, step, 0, unroll=True)
 
     pairs = []
     if joined_out:
@@ -342,11 +405,11 @@
             pltpu.VMEM((NZ * NU + 1, 16, 128), F32),
             pltpu.VMEM((NZ * NU + 1, 16, 128), F32),
             pltpu.SemaphoreType.DMA((2 * NZ,)),
-            pltpu.SemaphoreType.DMA((12,)),
+            pltpu.SemaphoreType.DMA((2,)),
         ]
         + [pltpu.VMEM(t.shape, t.dtype) for t in consts],
         compiler_params=pltpu.CompilerParams(vmem_limit_bytes=LIMIT),
-        cost_estimate=pl.CostEstimate(flops=6 * 10**9, bytes_accessed=1 << 22, transcendentals=0),
+        cost_estimate=pl.CostEstimate(flops=LONG * chunk, bytes_accessed=0, transcendentals=0),
         name="convolve",
     )(scalars, weights, *ins, *consts, *after)
 
@@ -355,11 +418,10 @@
     z, sign = scalars[0][0], scalars[0][1]
 
     def put(shift, even, odd):
-        start = pl.multiple_of(around(z, shift) * 128, 128)
         for o in range(2):
             real, imag = interleave(even[o], odd[o])
-            outs[o][0, pl.ds(start, 128), :] = real.reshape(128, 128)
-            outs[o][1, pl.ds(start, 128), :] = imag.reshape(128, 128)
+            outs[o][0, around(z, shift)] = real
+            outs[o][1, around(z, shift)] = imag
 
     if joined:
         v = ins[0]
@@ -376,28 +438,31 @@
         put(0, *[[own[:, c, 0, o] for o in range(2)] for c in range(2)])
         put(4, *[[far[:, c, o] for o in range(2)] for c in range(2)])
         for d in STEPS:
-            put(-sign * d, *[[paid[d - 1][:, c, 0, o] for o in range(2)] for c in range(2)])
+            put(-sign * d, *[[paid[d - 1][0, :, c, o] for o in range(2)] for c in range(2)])
             put(sign * d, *[[got[d - 1, :, c, o] for o in range(2)] for c in range(2)])
 
 
-def unpack(scalars, ins, chunk, old):
-    half = pl.BlockSpec((2, 1024, 128), lambda i, *_: (0, chunk, 0))
+def unpack(scalars, ins, chunk, old, after):
     joined = len(ins) == 1
+    wide, one = (NXY, 2, NZ, 2, 8, 128), (NXY, 2, 2, 8, 128)
     if joined:
-        ins = [ins[0].reshape(NXY, 2, NZ, 2, 8, 128)]
+        ins = [ins[0].reshape(wide)]
+        specs = [part(wide, 0)]
     else:
         own, far, *paid, got = ins
-        ins = [own.reshape(NXY, 2, NZ, 2, 8, 128), far.reshape(NXY, 2, 2, 8, 128)]
-        ins += [x.reshape(NXY, 2, 2, 2, 8, 128) for x in paid]
-        ins.append(got.reshape(3, NXY, 2, 2, 8, 128))
+        ins = [own.reshape(wide), far.reshape(one)]
+        ins += [x.reshape(2, *one) for x in paid]
+        ins.append(got.reshape(3, *one))
+        specs = [part(wide, 0, [(2, 1, 0)]), part(one, 0)]
+        specs += [part((2, *one), 1, [(0, 1, 0)])] * 3 + [part((3, *one), 1)]
     return local_call(
         functools.partial(unpack_kernel, joined),
         scalars,
         ins,
-        [whole(x.shape) for x in ins],
-        old,
-        [(2, 2048, 128)] * 2,
-        [half, half],
+        specs,
+        list(old) + after,
+        [GRID_IN] * 2,
+        [chunk_part(chunk)] * 2,
         "unpack",
         {1 + len(ins) + i: i for i in range(len(old))},
     )
@@ -438,37 +503,36 @@
     ]
     second = over_plane(pack_plane(scalars, green_lesser, green_greater, rows))
     rows = [to_ring(x, d) for d, x in zip(STEPS, rows)]
-    paid = [x.reshape(129, 8, 128) for x in rows]
-
-    far2, paid2 = fan(scalars, second, [])
-    order = [paid2[0]]
+    first = merge(own, far, rows)
+
+    far2, paid2, first = fan(second, first)
+    first = over_plane(first)
     far2 = to_far(far2)
     paid2 = [to_ring(x, d) for d, x in zip(STEPS, paid2)]
-
-    first = merge(scalars, own, far, paid, order)
     gains = jnp.stack([gains[0, :4]] + [x[1024:1028] for x in rows])
     weights = lax.dynamic_slice(gains, (0, 0, u * KK), (4, 4, KK)).reshape(-1)
-    first = over_plane(first)
-    own, far, keep, give = convolve(scalars, weights, [first], False, 0, [])
+    give2 = give_back(paid2, far2)
+
+    own, far, keep, give = convolve(scalars, weights, [first], False, 0, [give2])
+    got = to_core(give)
+    got2 = to_core(give2)
+    paid = [jnp.concatenate([keep[d - 1], got[d - 1]], axis=0) for d in STEPS]
+    order = list(paid)
     far = to_far(far)
-    got = to_core(give)
-    paid = [jnp.concatenate([keep[d - 1], got[d - 1]], axis=0) for d in STEPS]
-    order = [paid[0]]
-    paid = [to_ring(x, d).reshape(128, 8, 128) for d, x in zip(STEPS, paid)]
-
-    got2 = to_core(jnp.stack([x[:, 1] for x in paid2]))
+    paid = [to_ring(x, d) for d, x in zip(STEPS, paid)]
     (second,) = convolve(scalars, weights, [second, far2, *paid2, got2], True, 1, order)
     second = over_plane(second)
-    far2, paid2 = fan(scalars, second, [])
-    order = [paid2[0]]
+    first = merge(own, far, paid)
+
+    far2, paid2, first = fan(second, first)
+    first = over_plane(first)
     far2 = to_far(far2)
     paid2 = [to_ring(x, d) for d, x in zip(STEPS, paid2)]
-
-    first = over_plane(merge(scalars, own, far, paid, order))
-    done = unpack(scalars, [first], 0, [])
-    got2 = to_core(jnp.stack([x[:, 1] for x in paid2]))
-    polar, sigma = unpack(scalars, [second, far2, *paid2, got2], 1, done)
-    return polar, sigma
+    give2 = give_back(paid2, far2)
+    got2 = to_core(give2)
+    done = unpack(scalars, [first], 0, [], [give2])
+    polar, sigma = unpack(scalars, [second, far2, *paid2, got2], 1, done, [])
+    return polar.reshape(2, 2048, 128), sigma.reshape(2, 2048, 128)
 
 
 def solution(mesh):

time: 289 us -> 247 us (0.85)
  local copies, waits for them, and re-layouts: 25.7 us -> 3.46 us
  starting transfers between devices: 97 us -> 82.1 us
  Pallas kernels: 51.6 us -> 40.6 us
  waiting for transfers between devices: 106 us -> 115 us
    all_to_all x4, waiting for transfers between devices: 51.4 us -> 9.55 us  [over_plane(): return lax.all_to_all(x, PLANE, split_axis=0, concat_axis=0, tiled=True)]
    ppermute x12, waiting for transfers between devices: 42.9 us -> 81.9 us  [to_ring(): return lax.ppermute(x, ('zh', 'c', 'zl'), moves)]
    pallas_call x8 -> x4, Pallas kernels: 29.9 us -> 14 us  [local_call(): pl.pallas_call(lambda *refs: kernel(refs[:1], refs[1:1 + count], refs[1 +...]
    all_to_all x4, starting transfers between devices: 46.5 us -> 31.3 us  [over_plane(): return lax.all_to_all(x, PLANE, split_axis=0, concat_axis=0, tiled=True)]
    ppermute x4, waiting for transfers between devices: 11.5 us -> 22.4 us  [to_far(): return lax.ppermute(x, RING, [(i, (i + 4) % NZ) for i in range(NZ)])]
    pallas_call x0 -> x6, Pallas kernels: none -> 8.43 us  [shuttle(): pl.pallas_call(kernel, out_shape=[jax.ShapeDtypeStruct(s, F32) for s in s...]
    unnamed x36 -> x22, local copies, waits for them, and re-layouts: 8.45 us -> 0.04 us
    ppermute x4, starting transfers between devices: 12.4 us -> 19 us  [to_core(): return lax.ppermute(x, 'c', [(0, 1), (1, 0)])]
  transfers between devices with their start and end apart: 24 -> 24, of which waited for: 12 -> 16; matrix products, arithmetic and copies ran while one was open for 7% -> 3% of each run, Pallas kernels for 9% -> 8%
where the time goes in v3:
time: 247 us; the launch traced here: 246 us
  waiting for transfers between devices  115 us (47%)
  starting transfers between devices  82.1 us (33%)
  Pallas kernels  40.6 us (16%)
  other arithmetic  4.13 us (2%)
  local copies, waits for them, and re-layouts  3.46 us (1%)
    ppermute x12, waiting for transfers between devices, to_ring(): return lax.ppermute(x, ('zh', 'c', 'zl'), moves)  81.9 us
    all_to_all x4, starting transfers between devices, over_plane(): return lax.all_to_all(x, PLANE, split_axis=0, concat_axis=0, tiled=True)  31.3 us
    ppermute x4, waiting for transfers between devices, to_far(): return lax.ppermute(x, RING, [(i, (i + 4) % NZ) for i in range(NZ)])  22.4 us
    ppermute x12, starting transfers between devices, to_ring(): return lax.ppermute(x, ('zh', 'c', 'zl'), moves)  21.4 us
    ppermute x4, starting transfers between devices, to_core(): return lax.ppermute(x, 'c', [(0, 1), (1, 0)])  19 us
    pallas_call x2, Pallas kernels, convolve(): pl.pallas_call(functools.partial(convolve_kernel, len(ins) == 1, joined_o...  18.1 us
    pallas_call x4, Pallas kernels, local_call(): pl.pallas_call(lambda *refs: kernel(refs[:1], refs[1:1 + count], refs[1 +...  14 us
    ppermute x4, starting transfers between devices, to_far(): return lax.ppermute(x, RING, [(i, (i + 4) % NZ) for i in range(NZ)])  10.4 us
  transfers between devices with their start and end apart: 24, of which 16 were waited for; matrix products, arithmetic and copies ran while one was open for 3% of the time, Pallas kernels for 8%

profile of v3, /device:TPU:1, one launch (start us, length us, event | category | flops | bytes accessed | tf_op | source)
XLA Modules:
  0.0 246.1 jit_solution(3052173271766356054)
XLA Ops:
  1.3 3.7 %pack_ring.1 = (f32[16,2,2,8,128]{4,3,2,1,0:T(8,128)}, f32[16,2,2,8,128]{4,3,2,1,0:T(8,128)}, f32[3,16,2,2,8,128]{5,4,3,2,1,0:T(8,128)}, f32[3,16,2,2,8,128]{5,4,3,2,1,0:T(8,128)}, f32[4,16,128]{2,1,0:T(8,128)}) custom-call(s32[2]{0:T(128)} %pad_add_fusion.refs_0_, f32[2,16,16,8,128]{4,3,2,1,0:T(8,128)} %bitcast.61, f32[2,16,16,8,128]{4,3,2,1,0:T(8,128)} %bitcast.63, ...), custom_call_target="tpu_custom_call" | custom-call | tf_op jit(solution)/shard_map/pack_ring/pallas_call | solution.py:109
  5.0 3.2 %collective-permute-start = (f32[3,32,16,128]{3,2,1,0:T(8,128)}, f32[3,32,16,128]{3,2,1,0:T(8,128)S(1)}, u32[]{:S(2)}, u32[]{:S(2)}) collective-permute-start(f32[3,32,16,128]{3,2,1,0:T(8,128)} %bitcast.76), channel_id=1, source_target_pairs={{0,4},{4,0},{1,5},{5,1},{2,6},{6,2},{3,7},{7,3},{8,12},{12,8},{9,1... | collective-permute-start | bytes 2359304 | tf_op jit(solution)/shard_map/ppermute | solution.py:486
  10.4 4.4 %collective-permute-start.2 = (f32[1040,128]{1,0:T(8,128)S(1)}, f32[1040,128]{1,0:T(8,128)S(1)}, u32[]{:S(2)}, u32[]{:S(2)}) collective-permute-start(f32[1040,128]{1,0:T(8,128)S(1)} %pad_maximum_fusion.1.refs_4_), channel_id=1, source_target_pairs={{0,2},{1,3},{2,32},{3,33},{4,38},{5,39},{6,4},{7,5},{32,34},{33,35... | collective-permute-start | bytes 1597448 | tf_op jit(solution)/shard_map/ppermute | solution.py:478
  17.0 4.5 %collective-permute-start.4 = (f32[32,16,128]{2,1,0:T(8,128)S(1)}, f32[32,16,128]{2,1,0:T(8,128)S(1)}, u32[]{:S(2)}, u32[]{:S(2)}) collective-permute-start(f32[32,16,128]{2,1,0:T(8,128)S(1)} %bitcast.77), channel_id=1, source_target_pairs={{0,32},{1,33},{2,34},{3,35},{32,0},{33,1},{34,2},{35,3},{4,36},{5,... | collective-permute-start | bytes 786440 | tf_op jit(solution)/shard_map/ppermute | solution.py:482
  22.7 3.7 %pack_plane.1 = f32[16,2,8,2,8,128]{5,4,3,2,1,0:T(8,128)} custom-call(s32[2]{0:T(128)} %pad_add_fusion.refs_0_, f32[2,16,16,8,128]{4,3,2,1,0:T(8,128)} %bitcast.62, f32[2,16,16,8,128]{4,3,2,1,0:T(8,128)} %bitcast.64, f32[1040,128]{1,0:T(8,128)} %pad_maximum_fusion.refs_3_, f32[1040,128]{1,0:T(8,128)} %copy-done.7, f32[1040,128]{1,0:T(8,128)} %copy-done.8), custom_call_target="tpu_custom_call" | custom-call | tf_op jit(solution)/shard_map/pack_plane/pallas_call | solution.py:109
  26.4 7.4 %all-to-all-start = ((f32[32,8,16,128]{3,2,1,0:T(8,128)}), f32[32,8,16,128]{3,2,1,0:T(8,128)}, u32[]{:S(2)}, u32[]{:S(2)}) async-start(f32[32,8,16,128]{3,2,1,0:T(8,128)} %bitcast.65), calls=%async_computation | async-start | bytes 4194304 | tf_op jit(solution)/shard_map/all_to_all | solution.py:490
  33.8 11.4 %collective-permute-done.4.refs_1_ = f32[32,16,128]{2,1,0:T(8,128)S(1)} collective-permute-done((f32[32,16,128]{2,1,0:T(8,128)S(1)}, f32[32,16,128]{2,1,0:T(8,128)S(1)}, u32[]{:S(2)}, u32[]{:S(2)}) %collective-permute-start.4) | collective-permute-done | bytes 262176 | tf_op jit(solution)/shard_map/ppermute | solution.py:482
  45.3 3.5 %collective-permute-done.3 = f32[1040,128]{1,0:T(8,128)S(1)} collective-permute-done((f32[1040,128]{1,0:T(8,128)S(1)}, f32[1040,128]{1,0:T(8,128)S(1)}, u32[]{:S(2)}, u32[]{:S(2)}) %collective-permute-start.3) | collective-permute-done | bytes 532512 | tf_op jit(solution)/shard_map/ppermute | solution.py:478
  48.8 10.5 %collective-permute-done.1 = f32[1040,128]{1,0:T(8,128)S(1)} collective-permute-done((f32[1040,128]{1,0:T(8,128)}, f32[1040,128]{1,0:T(8,128)S(1)}, u32[]{:S(2)}, u32[]{:S(2)}) %collective-permute-start.1) | collective-permute-done | bytes 532512 | tf_op jit(solution)/shard_map/ppermute | solution.py:478
  65.5 4.7 %collective-permute-start.7 = (f32[2,32,16,128]{3,2,1,0:T(8,128)}, f32[2,32,16,128]{3,2,1,0:T(8,128)S(1)}, u32[]{:S(2)}, u32[]{:S(2)}) collective-permute-start(f32[2,32,16,128]{3,2,1,0:T(8,128)} %get-tuple-element.32), channel_id=1, source_target_pairs={{0,2},{1,3},{2,32},{3,33},{4,38},{5,39},{6,4},{7,5},{32,34},{33,35... | collective-permute-start | bytes 1572872 | tf_op jit(solution)/shard_map/ppermute | solution.py:478
  72.0 10.8 %all-to-all-start.1 = ((f32[32,8,16,128]{3,2,1,0:T(8,128)}), f32[32,8,16,128]{3,2,1,0:T(8,128)}, u32[]{:S(2)}, u32[]{:S(2)}) async-start(f32[32,8,16,128]{3,2,1,0:T(8,128)} %get-tuple-element.34), calls=%async_computation.1 | async-start | bytes 4194304 | tf_op jit(solution)/shard_map/all_to_all | solution.py:490
  82.8 3.4 %collective-permute-done.5.refs_3_ = f32[32,16,128]{2,1,0:T(8,128)S(1)} collective-permute-done((f32[32,16,128]{2,1,0:T(8,128)S(1)}, f32[32,16,128]{2,1,0:T(8,128)S(1)}, u32[]{:S(2)}, u32[]{:S(2)}) %collective-permute-start.5) | collective-permute-done | bytes 262176 | tf_op jit(solution)/shard_map/ppermute | solution.py:482
  86.2 7.9 %collective-permute-done.7.refs_1_.refs_5_ = f32[2,32,16,128]{3,2,1,0:T(8,128)S(1)} collective-permute-done((f32[2,32,16,128]{3,2,1,0:T(8,128)}, f32[2,32,16,128]{3,2,1,0:T(8,128)S(1)}, u32[]{:S(2)}, u32[]{:S(2)}) %collective-permute-start.7) | collective-permute-done | bytes 524320 | tf_op jit(solution)/shard_map/ppermute | solution.py:478
  94.0 14.1 %collective-permute-done.8.refs_2_.refs_6_ = f32[2,32,16,128]{3,2,1,0:T(8,128)S(1)} collective-permute-done((f32[2,32,16,128]{3,2,1,0:T(8,128)}, f32[2,32,16,128]{3,2,1,0:T(8,128)S(1)}, u32[]{:S(2)}, u32[]{:S(2)}) %collective-permute-start.8) | collective-permute-done | bytes 524320 | tf_op jit(solution)/shard_map/ppermute | solution.py:478
  108.3 2.9 %all-to-all-done.1.refs_2_ = f32[32,8,16,128]{3,2,1,0:T(8,128)} async-done(((f32[32,8,16,128]{3,2,1,0:T(8,128)}), f32[32,8,16,128]{3,2,1,0:T(8,128)}, u32[]{:S(2)}, u32[]{:S(2)}) %all-to-all-start.1) | async-done | bytes 2097184 | tf_op jit(solution)/shard_map/all_to_all | solution.py:490
  111.2 9.1 %convolve.2 = (f32[32,16,128]{2,1,0:T(8,128)S(1)}, f32[32,16,128]{2,1,0:T(8,128)}, f32[3,32,16,128]{3,2,1,0:T(8,128)S(1)}, f32[3,32,16,128]{3,2,1,0:T(8,128)S(1)}) custom-call(s32[2]{0:T(128)S(1)} %copy-done.2, f32[64]{0:T(128)S(1)} %reshape.81.refs_1_, f32[32,8,16,128]{3,2,1,0:T(8,128)} %all-to-all-done.1.refs_2_, bf16[1408,256]{1,0:T(8,128)(2,1)S(1)} %copy-done, ...), custom_call_target="tpu_custom_call" | custom-call | tf_op jit(solution)/shard_map/convolve/pallas_call | solution.py:399
  120.3 9.8 %collective-permute-start.10 = (f32[3,32,16,128]{3,2,1,0:T(8,128)S(1)}, f32[3,32,16,128]{3,2,1,0:T(8,128)S(1)}, u32[]{:S(2)}, u32[]{:S(2)}) collective-permute-start(f32[3,32,16,128]{3,2,1,0:T(8,128)S(1)} %get-tuple-element.36), channel_id=1, source_target_pairs={{0,4},{4,0},{1,5},{5,1},{2,6},{6,2},{3,7},{7,3},{8,12},{12,8},{9,1... | collective-permute-start | bytes 2359304 | tf_op jit(solution)/shard_map/ppermute | solution.py:486
  134.5 3.9 %collective-permute-start.14 = (f32[64,16,128]{2,1,0:T(8,128)}, f32[64,16,128]{2,1,0:T(8,128)}, u32[]{:S(2)}, u32[]{:S(2)}) collective-permute-start(f32[64,16,128]{2,1,0:T(8,128)} %pad_maximum_fusion.5.refs_12_), channel_id=1, source_target_pairs={{0,3},{1,32},{2,33},{3,34},{4,37},{5,38},{6,39},{7,4},{32,35},{33,... | collective-permute-start | bytes 1572872 | tf_op jit(solution)/shard_map/ppermute | solution.py:478
  138.5 9.0 %convolve.3 = f32[32,8,16,128]{3,2,1,0:T(8,128)} custom-call(s32[2]{0:T(128)S(1)} %copy-done.2, f32[64]{0:T(128)S(1)} %reshape.81.refs_1_, f32[32,8,16,128]{3,2,1,0:T(8,128)} %all-to-all-done.refs_0_.refs_2_, f32[32,16,128]{2,1,0:T(8,128)S(1)} %collective-permute-done.5.refs_3_, f32[2,32,16,128]{3,2,1,0:T(8,128)S(1)} %collective-permute-done.6.refs_0_.refs_4_, ...), custom_call_target="tpu_custom_call" | custom-call | flops 199999995904 | tf_op jit(solution)/shard_map/convolve/pallas_call | solution.py:399
  147.5 8.5 %all-to-all-start.2 = ((f32[32,8,16,128]{3,2,1,0:T(8,128)}), f32[32,8,16,128]{3,2,1,0:T(8,128)}, u32[]{:S(2)}, u32[]{:S(2)}) async-start(f32[32,8,16,128]{3,2,1,0:T(8,128)} %convolve.3), calls=%async_computation.2 | async-start | bytes 4194304 | tf_op jit(solution)/shard_map/all_to_all | solution.py:490
  156.1 4.9 %collective-permute-done.13.refs_3_ = f32[64,16,128]{2,1,0:T(8,128)} collective-permute-done((f32[64,16,128]{2,1,0:T(8,128)}, f32[64,16,128]{2,1,0:T(8,128)}, u32[]{:S(2)}, u32[]{:S(2)}) %collective-permute-start.13) | collective-permute-done | bytes 524320 | tf_op jit(solution)/shard_map/ppermute | solution.py:478
  161.0 15.6 %collective-permute-done.14.refs_4_ = f32[64,16,128]{2,1,0:T(8,128)} collective-permute-done((f32[64,16,128]{2,1,0:T(8,128)}, f32[64,16,128]{2,1,0:T(8,128)}, u32[]{:S(2)}, u32[]{:S(2)}) %collective-permute-start.14) | collective-permute-done | bytes 524320 | tf_op jit(solution)/shard_map/ppermute | solution.py:478
  179.0 5.4 %all-to-all-done.2.refs_0_ = f32[32,8,16,128]{3,2,1,0:T(8,128)} async-done(((f32[32,8,16,128]{3,2,1,0:T(8,128)}), f32[32,8,16,128]{3,2,1,0:T(8,128)}, u32[]{:S(2)}, u32[]{:S(2)}) %all-to-all-start.2) | async-done | bytes 2097184 | tf_op jit(solution)/shard_map/all_to_all | solution.py:490
  186.2 2.5 %collective-permute-start.16 = (f32[2,32,16,128]{3,2,1,0:T(8,128)S(1)}, f32[2,32,16,128]{3,2,1,0:T(8,128)S(1)}, u32[]{:S(2)}, u32[]{:S(2)}) collective-permute-start(f32[2,32,16,128]{3,2,1,0:T(8,128)S(1)} %get-tuple-element.40), channel_id=1, source_target_pairs={{0,1},{1,2},{2,3},{3,32},{4,39},{5,4},{6,5},{7,6},{32,33},{33,34},... | collective-permute-start | bytes 1572872 | tf_op jit(solution)/shard_map/ppermute | solution.py:478
  191.8 4.0 %collective-permute-start.15 = (f32[32,16,128]{2,1,0:T(8,128)}, f32[32,16,128]{2,1,0:T(8,128)S(1)}, u32[]{:S(2)}, u32[]{:S(2)}) collective-permute-start(f32[32,16,128]{2,1,0:T(8,128)} %get-tuple-element.39), channel_id=1, source_target_pairs={{0,32},{1,33},{2,34},{3,35},{32,0},{33,1},{34,2},{35,3},{4,36},{5,... | collective-permute-start | bytes 786440 | tf_op jit(solution)/shard_map/ppermute | solution.py:482
  195.8 4.5 %all-to-all-start.3 = ((f32[32,8,16,128]{3,2,1,0:T(8,128)}), f32[32,8,16,128]{3,2,1,0:T(8,128)}, u32[]{:S(2)}, u32[]{:S(2)}) async-start(f32[32,8,16,128]{3,2,1,0:T(8,128)} %get-tuple-element.43), calls=%async_computation.3 | async-start | bytes 4194304 | tf_op jit(solution)/shard_map/all_to_all | solution.py:490
  200.3 7.6 %collective-permute-done.15.refs_3_ = f32[32,16,128]{2,1,0:T(8,128)S(1)} collective-permute-done((f32[32,16,128]{2,1,0:T(8,128)}, f32[32,16,128]{2,1,0:T(8,128)S(1)}, u32[]{:S(2)}, u32[]{:S(2)}) %collective-permute-start.15) | collective-permute-done | bytes 262176 | tf_op jit(solution)/shard_map/ppermute | solution.py:482
  208.0 8.0 %collective-permute-done.17.refs_1_ = f32[2,32,16,128]{3,2,1,0:T(8,128)S(1)} collective-permute-done((f32[2,32,16,128]{3,2,1,0:T(8,128)S(1)}, f32[2,32,16,128]{3,2,1,0:T(8,128)S(1)}, u32[]{:S(2)}, u32[]{:S(2)}) %collective-permute-start.17) | collective-permute-done | bytes 524320 | tf_op jit(solution)/shard_map/ppermute | solution.py:478
  216.0 17.5 %collective-permute-done.18.refs_2_ = f32[2,32,16,128]{3,2,1,0:T(8,128)S(1)} collective-permute-done((f32[2,32,16,128]{3,2,1,0:T(8,128)S(1)}, f32[2,32,16,128]{3,2,1,0:T(8,128)S(1)}, u32[]{:S(2)}, u32[]{:S(2)}) %collective-permute-start.18) | collective-permute-done | bytes 524320 | tf_op jit(solution)/shard_map/ppermute | solution.py:478
  233.7 5.9 %collective-permute-start.19 = (f32[3,32,16,128]{3,2,1,0:T(8,128)S(1)}, f32[3,32,16,128]{3,2,1,0:T(8,128)S(1)}, u32[]{:S(2)}, u32[]{:S(2)}) collective-permute-start(f32[3,32,16,128]{3,2,1,0:T(8,128)S(1)} %give.3.refs_2_), channel_id=1, source_target_pairs={{0,4},{4,0},{1,5},{5,1},{2,6},{6,2},{3,7},{7,3},{8,12},{12,8},{9,1... | collective-permute-start | bytes 2359304 | tf_op jit(solution)/shard_map/ppermute | solution.py:486
  239.6 3.6 %unpack.2 = (f32[2,16,16,8,128]{4,3,2,1,0:T(8,128)}, f32[2,16,16,8,128]{4,3,2,1,0:T(8,128)}) custom-call(s32[2]{0:T(128)S(1)} %copy-done.3, f32[16,2,8,2,8,128]{5,4,3,2,1,0:T(8,128)} %bitcast.37.refs_1_, f32[3,32,16,128]{3,2,1,0:T(8,128)S(1)} %give.3.refs_2_), custom_call_target="tpu_custom_call" | custom-call | tf_op jit(solution)/shard_map/unpack/pallas_call | solution.py:109
  243.2 3.0 %unpack.3 = (f32[2,16,16,8,128]{4,3,2,1,0:T(8,128)}, f32[2,16,16,8,128]{4,3,2,1,0:T(8,128)}) custom-call(s32[2]{0:T(128)S(1)} %copy-done.3, f32[16,2,8,2,8,128]{5,4,3,2,1,0:T(8,128)} %bitcast.31.refs_1_, f32[16,2,2,8,128]{4,3,2,1,0:T(8,128)S(1)} %bitcast.56, f32[2,16,2,2,8,128]{5,4,3,2,1,0:T(8,128)S(1)} %bitcast.53, ...), custom_call_target="tpu_custom_call", output_to_operand_aliasing={{0}: (7, {}), {1}: (8, {})} | custom-call | tf_op jit(solution)/shard_map/unpack/pallas_call | solution.py:109
  (68 shorter events, 26.5 us)
Async XLA Ops:
  5.0 5.4 %collective-permute-start = (f32[3,32,16,128]{3,2,1,0:T(8,128)}, f32[3,32,16,128]{3,2,1,0:T(8,128)S(1)}, u32[]{:S(2)}, u32[]{:S(2)}) collective-permute-start(f32[3,32,16,128]{3,2,1,0:T(8,128)} %bitcast.76), channel_id=1, source_target_pairs={{0,4},{4,0},{1,5},{5,1},{2,6},{6,2},{3,7},{7,3},{8,12},{12,8},{9,1... | collective-permute-start | bytes 2359304 | tf_op jit(solution)/shard_map/ppermute | solution.py:486
  10.1 6.9 %copy-start.10 = (f32[16,2,2,8,128]{4,3,2,1,0:T(8,128)S(1)}, f32[16,2,2,8,128]{4,3,2,1,0:T(8,128)}, u32[]{:S(2)}) copy-start(f32[16,2,2,8,128]{4,3,2,1,0:T(8,128)} %get-tuple-element.29) | copy-start | bytes 786436
  10.4 12.3 %copy-start.7 = (f32[1040,128]{1,0:T(8,128)}, f32[1040,128]{1,0:T(8,128)S(1)}, u32[]{:S(2)}) copy-start(f32[1040,128]{1,0:T(8,128)S(1)} %pad_maximum_fusion.1.refs_4_) | copy-start | bytes 1597444
  10.4 34.8 %collective-permute-start.2 = (f32[1040,128]{1,0:T(8,128)S(1)}, f32[1040,128]{1,0:T(8,128)S(1)}, u32[]{:S(2)}, u32[]{:S(2)}) collective-permute-start(f32[1040,128]{1,0:T(8,128)S(1)} %pad_maximum_fusion.1.refs_4_), channel_id=1, source_target_pairs={{0,2},{1,3},{2,32},{3,33},{4,38},{5,39},{6,4},{7,5},{32,34},{33,35... | collective-permute-start | bytes 1597448 | tf_op jit(solution)/shard_map/ppermute | solution.py:478
  14.8 7.9 %copy-start.8 = (f32[1040,128]{1,0:T(8,128)}, f32[1040,128]{1,0:T(8,128)S(1)}, u32[]{:S(2)}) copy-start(f32[1040,128]{1,0:T(8,128)S(1)} %pad_maximum_fusion.2.refs_5_) | copy-start | bytes 1597444
  14.8 33.9 %collective-permute-start.3 = (f32[1040,128]{1,0:T(8,128)S(1)}, f32[1040,128]{1,0:T(8,128)S(1)}, u32[]{:S(2)}, u32[]{:S(2)}) collective-permute-start(f32[1040,128]{1,0:T(8,128)S(1)} %pad_maximum_fusion.2.refs_5_), channel_id=1, source_target_pairs={{0,3},{1,32},{2,33},{3,34},{4,37},{5,38},{6,39},{7,4},{32,35},{33,... | collective-permute-start | bytes 1597448 | tf_op jit(solution)/shard_map/ppermute | solution.py:478
  16.5 42.8 %collective-permute-start.1 = (f32[1040,128]{1,0:T(8,128)}, f32[1040,128]{1,0:T(8,128)S(1)}, u32[]{:S(2)}, u32[]{:S(2)}) collective-permute-start(f32[1040,128]{1,0:T(8,128)} %pad_maximum_fusion.refs_3_), channel_id=1, source_target_pairs={{0,1},{1,2},{2,3},{3,32},{4,39},{5,4},{6,5},{7,6},{32,33},{33,34},... | collective-permute-start | bytes 1597448 | tf_op jit(solution)/shard_map/ppermute | solution.py:478
  17.0 28.3 %collective-permute-start.4 = (f32[32,16,128]{2,1,0:T(8,128)S(1)}, f32[32,16,128]{2,1,0:T(8,128)S(1)}, u32[]{:S(2)}, u32[]{:S(2)}) collective-permute-start(f32[32,16,128]{2,1,0:T(8,128)S(1)} %bitcast.77), channel_id=1, source_target_pairs={{0,32},{1,33},{2,34},{3,35},{32,0},{33,1},{34,2},{35,3},{4,36},{5,... | collective-permute-start | bytes 786440 | tf_op jit(solution)/shard_map/ppermute | solution.py:482
  26.4 32.8 %copy-start.4 = (f32[16,2,2,8,128]{4,3,2,1,0:T(8,128)S(1)}, f32[16,2,2,8,128]{4,3,2,1,0:T(8,128)}, u32[]{:S(2)}) copy-start(f32[16,2,2,8,128]{4,3,2,1,0:T(8,128)} %get-tuple-element.28) | copy-start | bytes 786436
  26.4 35.7 %all-to-all-start = ((f32[32,8,16,128]{3,2,1,0:T(8,128)}), f32[32,8,16,128]{3,2,1,0:T(8,128)}, u32[]{:S(2)}, u32[]{:S(2)}) async-start(f32[32,8,16,128]{3,2,1,0:T(8,128)} %bitcast.65), calls=%async_computation | async-start | bytes 4194304 | tf_op jit(solution)/shard_map/all_to_all | solution.py:490
  60.9 10.9 %copy-start.9 = (f32[1,4,128]{2,1,0:T(4,128)S(1)}, f32[1,4,128]{2,1,0:T(4,128)}, u32[]{:S(2)}) copy-start(f32[1,4,128]{2,1,0:T(4,128)} %slice.60) | copy-start | bytes 6148
  64.5 21.7 %collective-permute-start.6 = (f32[2,32,16,128]{3,2,1,0:T(8,128)}, f32[2,32,16,128]{3,2,1,0:T(8,128)S(1)}, u32[]{:S(2)}, u32[]{:S(2)}) collective-permute-start(f32[2,32,16,128]{3,2,1,0:T(8,128)} %get-tuple-element.31), channel_id=1, source_target_pairs={{0,1},{1,2},{2,3},{3,32},{4,39},{5,4},{6,5},{7,6},{32,33},{33,34},... | collective-permute-start | bytes 1572872 | tf_op jit(solution)/shard_map/ppermute | solution.py:478
  65.5 28.5 %collective-permute-start.7 = (f32[2,32,16,128]{3,2,1,0:T(8,128)}, f32[2,32,16,128]{3,2,1,0:T(8,128)S(1)}, u32[]{:S(2)}, u32[]{:S(2)}) collective-permute-start(f32[2,32,16,128]{3,2,1,0:T(8,128)} %get-tuple-element.32), channel_id=1, source_target_pairs={{0,2},{1,3},{2,32},{3,33},{4,38},{5,39},{6,4},{7,5},{32,34},{33,35... | collective-permute-start | bytes 1572872 | tf_op jit(solution)/shard_map/ppermute | solution.py:478
  70.2 37.9 %collective-permute-start.8 = (f32[2,32,16,128]{3,2,1,0:T(8,128)}, f32[2,32,16,128]{3,2,1,0:T(8,128)S(1)}, u32[]{:S(2)}, u32[]{:S(2)}) collective-permute-start(f32[2,32,16,128]{3,2,1,0:T(8,128)} %get-tuple-element.33), channel_id=1, source_target_pairs={{0,3},{1,32},{2,33},{3,34},{4,37},{5,38},{6,39},{7,4},{32,35},{33,... | collective-permute-start | bytes 1572872 | tf_op jit(solution)/shard_map/ppermute | solution.py:478
  70.7 15.5 %collective-permute-start.5 = (f32[32,16,128]{2,1,0:T(8,128)S(1)}, f32[32,16,128]{2,1,0:T(8,128)S(1)}, u32[]{:S(2)}, u32[]{:S(2)}) collective-permute-start(f32[32,16,128]{2,1,0:T(8,128)S(1)} %get-tuple-element.30), channel_id=1, source_target_pairs={{0,32},{1,33},{2,34},{3,35},{32,0},{33,1},{34,2},{35,3},{4,36},{5,... | collective-permute-start | bytes 786440 | tf_op jit(solution)/shard_map/ppermute | solution.py:482
  72.0 39.2 %all-to-all-start.1 = ((f32[32,8,16,128]{3,2,1,0:T(8,128)}), f32[32,8,16,128]{3,2,1,0:T(8,128)}, u32[]{:S(2)}, u32[]{:S(2)}) async-start(f32[32,8,16,128]{3,2,1,0:T(8,128)} %get-tuple-element.34), calls=%async_computation.1 | async-start | bytes 4194304 | tf_op jit(solution)/shard_map/all_to_all | solution.py:490
  120.3 12.6 %copy-start.5 = (f32[32,16,128]{2,1,0:T(8,128)}, f32[32,16,128]{2,1,0:T(8,128)S(1)}, u32[]{:S(2)}) copy-start(f32[32,16,128]{2,1,0:T(8,128)S(1)} %get-tuple-element.37.refs_0_) | copy-start | bytes 786436
  120.3 11.7 %collective-permute-start.10 = (f32[3,32,16,128]{3,2,1,0:T(8,128)S(1)}, f32[3,32,16,128]{3,2,1,0:T(8,128)S(1)}, u32[]{:S(2)}, u32[]{:S(2)}) collective-permute-start(f32[3,32,16,128]{3,2,1,0:T(8,128)S(1)} %get-tuple-element.36), channel_id=1, source_target_pairs={{0,4},{4,0},{1,5},{5,1},{2,6},{6,2},{3,7},{7,3},{8,12},{12,8},{9,1... | collective-permute-start | bytes 2359304 | tf_op jit(solution)/shard_map/ppermute | solution.py:486
  130.1 8.4 %collective-permute-start.9 = (f32[3,32,16,128]{3,2,1,0:T(8,128)S(1)}, f32[3,32,16,128]{3,2,1,0:T(8,128)S(1)}, u32[]{:S(2)}, u32[]{:S(2)}) collective-permute-start(f32[3,32,16,128]{3,2,1,0:T(8,128)S(1)} %give.2.refs_5_), channel_id=1, source_target_pairs={{0,4},{4,0},{1,5},{5,1},{2,6},{6,2},{3,7},{7,3},{8,12},{12,8},{9,1... | collective-permute-start | bytes 2359304 | tf_op jit(solution)/shard_map/ppermute | solution.py:486
  130.2 25.9 %collective-permute-start.11 = (f32[32,16,128]{2,1,0:T(8,128)}, f32[32,16,128]{2,1,0:T(8,128)}, u32[]{:S(2)}, u32[]{:S(2)}) collective-permute-start(f32[32,16,128]{2,1,0:T(8,128)} %get-tuple-element.38), channel_id=1, source_target_pairs={{0,32},{1,33},{2,34},{3,35},{32,0},{33,1},{34,2},{35,3},{4,36},{5,... | collective-permute-start | bytes 786440 | tf_op jit(solution)/shard_map/ppermute | solution.py:482
  132.9 23.2 %collective-permute-start.12 = (f32[64,16,128]{2,1,0:T(8,128)}, f32[64,16,128]{2,1,0:T(8,128)}, u32[]{:S(2)}, u32[]{:S(2)}) collective-permute-start(f32[64,16,128]{2,1,0:T(8,128)} %pad_maximum_fusion.3.refs_10_), channel_id=1, source_target_pairs={{0,1},{1,2},{2,3},{3,32},{4,39},{5,4},{6,5},{7,6},{32,33},{33,34},... | collective-permute-start | bytes 1572872 | tf_op jit(solution)/shard_map/ppermute | solution.py:478
  133.7 27.3 %collective-permute-start.13 = (f32[64,16,128]{2,1,0:T(8,128)}, f32[64,16,128]{2,1,0:T(8,128)}, u32[]{:S(2)}, u32[]{:S(2)}) collective-permute-start(f32[64,16,128]{2,1,0:T(8,128)} %pad_maximum_fusion.4.refs_11_), channel_id=1, source_target_pairs={{0,2},{1,3},{2,32},{3,33},{4,38},{5,39},{6,4},{7,5},{32,34},{33,35... | collective-permute-start | bytes 1572872 | tf_op jit(solution)/shard_map/ppermute | solution.py:478
  134.5 42.1 %collective-permute-start.14 = (f32[64,16,128]{2,1,0:T(8,128)}, f32[64,16,128]{2,1,0:T(8,128)}, u32[]{:S(2)}, u32[]{:S(2)}) collective-permute-start(f32[64,16,128]{2,1,0:T(8,128)} %pad_maximum_fusion.5.refs_12_), channel_id=1, source_target_pairs={{0,3},{1,32},{2,33},{3,34},{4,37},{5,38},{6,39},{7,4},{32,35},{33,... | collective-permute-start | bytes 1572872 | tf_op jit(solution)/shard_map/ppermute | solution.py:478
  147.5 29.1 %copy-start.6 = (f32[32,16,128]{2,1,0:T(8,128)S(1)}, f32[32,16,128]{2,1,0:T(8,128)}, u32[]{:S(2)}) copy-start(f32[32,16,128]{2,1,0:T(8,128)} %copy-done.5) | copy-start | bytes 786436
  147.5 36.9 %all-to-all-start.2 = ((f32[32,8,16,128]{3,2,1,0:T(8,128)}), f32[32,8,16,128]{3,2,1,0:T(8,128)}, u32[]{:S(2)}, u32[]{:S(2)}) async-start(f32[32,8,16,128]{3,2,1,0:T(8,128)} %convolve.3), calls=%async_computation.2 | async-start | bytes 4194304 | tf_op jit(solution)/shard_map/all_to_all | solution.py:490
  186.2 21.8 %collective-permute-start.16 = (f32[2,32,16,128]{3,2,1,0:T(8,128)S(1)}, f32[2,32,16,128]{3,2,1,0:T(8,128)S(1)}, u32[]{:S(2)}, u32[]{:S(2)}) collective-permute-start(f32[2,32,16,128]{3,2,1,0:T(8,128)S(1)} %get-tuple-element.40), channel_id=1, source_target_pairs={{0,1},{1,2},{2,3},{3,32},{4,39},{5,4},{6,5},{7,6},{32,33},{33,34},... | collective-permute-start | bytes 1572872 | tf_op jit(solution)/shard_map/ppermute | solution.py:478
  188.6 27.4 %collective-permute-start.17 = (f32[2,32,16,128]{3,2,1,0:T(8,128)S(1)}, f32[2,32,16,128]{3,2,1,0:T(8,128)S(1)}, u32[]{:S(2)}, u32[]{:S(2)}) collective-permute-start(f32[2,32,16,128]{3,2,1,0:T(8,128)S(1)} %get-tuple-element.41), channel_id=1, source_target_pairs={{0,2},{1,3},{2,32},{3,33},{4,38},{5,39},{6,4},{7,5},{32,34},{33,35... | collective-permute-start | bytes 1572872 | tf_op jit(solution)/shard_map/ppermute | solution.py:478
  190.2 43.3 %collective-permute-start.18 = (f32[2,32,16,128]{3,2,1,0:T(8,128)S(1)}, f32[2,32,16,128]{3,2,1,0:T(8,128)S(1)}, u32[]{:S(2)}, u32[]{:S(2)}) collective-permute-start(f32[2,32,16,128]{3,2,1,0:T(8,128)S(1)} %get-tuple-element.42), channel_id=1, source_target_pairs={{0,3},{1,32},{2,33},{3,34},{4,37},{5,38},{6,39},{7,4},{32,35},{33,... | collective-permute-start | bytes 1572872 | tf_op jit(solution)/shard_map/ppermute | solution.py:478
  191.8 16.2 %collective-permute-start.15 = (f32[32,16,128]{2,1,0:T(8,128)}, f32[32,16,128]{2,1,0:T(8,128)S(1)}, u32[]{:S(2)}, u32[]{:S(2)}) collective-permute-start(f32[32,16,128]{2,1,0:T(8,128)} %get-tuple-element.39), channel_id=1, source_target_pairs={{0,32},{1,33},{2,34},{3,35},{32,0},{33,1},{34,2},{35,3},{4,36},{5,... | collective-permute-start | bytes 786440 | tf_op jit(solution)/shard_map/ppermute | solution.py:482
  195.8 43.8 %all-to-all-start.3 = ((f32[32,8,16,128]{3,2,1,0:T(8,128)}), f32[32,8,16,128]{3,2,1,0:T(8,128)}, u32[]{:S(2)}, u32[]{:S(2)}) async-start(f32[32,8,16,128]{3,2,1,0:T(8,128)} %get-tuple-element.43), calls=%async_computation.3 | async-start | bytes 4194304 | tf_op jit(solution)/shard_map/all_to_all | solution.py:490
  233.5 6.1 %copy-start.3 = (s32[2]{0:T(128)S(1)}, s32[2]{0:T(128)}, u32[]{:S(2)}) copy-start(s32[2]{0:T(128)} %pad_add_fusion.refs_0_) | copy-start | bytes 28
  233.7 9.5 %collective-permute-start.19 = (f32[3,32,16,128]{3,2,1,0:T(8,128)S(1)}, f32[3,32,16,128]{3,2,1,0:T(8,128)S(1)}, u32[]{:S(2)}, u32[]{:S(2)}) collective-permute-start(f32[3,32,16,128]{3,2,1,0:T(8,128)S(1)} %give.3.refs_2_), channel_id=1, source_target_pairs={{0,4},{4,0},{1,5},{5,1},{2,6},{6,2},{3,7},{7,3},{8,12},{12,8},{9,1... | collective-permute-start | bytes 2359304 | tf_op jit(solution)/shard_map/ppermute | solution.py:486
  (3 other events, 9.2 us)

commit v4 on v3

--- a/solution.py
+++ b/solution.py
@@ -253,8 +253,8 @@
 
 
 def give_back(paid, far):
-    routes = [(d - 1, 1, 0, d - 1) for d in STEPS]
-    return shuttle(paid, [(3, *BLOCK)], routes, "give", after=[far])[0]
+    routes = [(i, 1, 0, i) for i in range(len(paid))]
+    return shuttle(paid, [(len(paid), *BLOCK)], routes, "give", after=[far])[0]
 
 
 def fan(joined, through):
@@ -267,7 +267,7 @@
 
 
 def convolve_kernel(joined_in, joined_out, chunk, n_after, *refs):
-    n_in = 1 if joined_in else 6
+    n_in = 1 if joined_in else 7
     n_out = 1 if joined_out else 4
     refs = list(refs)
     scalars, weights = refs[:2]
@@ -297,12 +297,13 @@
         for c, slot, zs, core in joined_places(-1):
             pairs.append((source.at[:, c, slot], x_at.at[zs, :, core]))
     else:
-        own, far, got = ins[0], ins[1], ins[5]
+        own, far = ins[:2]
+        got = [ins[5].at[0], ins[5].at[1], ins[6]]
         pairs.append((own.at[:, 0], xin.at[pl.ds(z * NU, NU)]))
         pairs.append((far, xin.at[pl.ds(around(z, 4) * NU, NU)]))
         for d in STEPS:
             pairs.append((ins[1 + d].at[0], xin.at[pl.ds(around(z, -sign * d) * NU, NU)]))
-            pairs.append((got.at[d - 1], xin.at[pl.ds(around(z, sign * d) * NU, NU)]))
+            pairs.append((got[d - 1], xin.at[pl.ds(around(z, sign * d) * NU, NU)]))
     copies = [pltpu.make_async_copy(s, t, sem.at[i]) for i, (s, t) in enumerate(pairs)]
     for copy in copies + tab_copies:
         copy.start()
@@ -409,7 +410,7 @@
         ]
         + [pltpu.VMEM(t.shape, t.dtype) for t in consts],
         compiler_params=pltpu.CompilerParams(vmem_limit_bytes=LIMIT),
-        cost_estimate=pl.CostEstimate(flops=LONG * chunk, bytes_accessed=0, transcendentals=0),
+        cost_estimate=pl.CostEstimate(flops=LONG, bytes_accessed=0, transcendentals=0),
         name="convolve",
     )(scalars, weights, *ins, *consts, *after)
 
@@ -511,16 +512,16 @@
     paid2 = [to_ring(x, d) for d, x in zip(STEPS, paid2)]
     gains = jnp.stack([gains[0, :4]] + [x[1024:1028] for x in rows])
     weights = lax.dynamic_slice(gains, (0, 0, u * KK), (4, 4, KK)).reshape(-1)
-    give2 = give_back(paid2, far2)
+    give2 = give_back(paid2[:2], far2)
 
     own, far, keep, give = convolve(scalars, weights, [first], False, 0, [give2])
     got = to_core(give)
-    got2 = to_core(give2)
+    got2 = [to_core(give2), to_core(paid2[2][1])]
     paid = [jnp.concatenate([keep[d - 1], got[d - 1]], axis=0) for d in STEPS]
     order = list(paid)
     far = to_far(far)
     paid = [to_ring(x, d) for d, x in zip(STEPS, paid)]
-    (second,) = convolve(scalars, weights, [second, far2, *paid2, got2], True, 1, order)
+    (second,) = convolve(scalars, weights, [second, far2, *paid2, *got2], True, 1, order)
     second = over_plane(second)
     first = merge(own, far, paid)
 

time: 247 us -> 237 us (0.960)
  waiting for transfers between devices: 115 us -> 108 us
  starting transfers between devices: 82.1 us -> 76.5 us
    ppermute x12, waiting for transfers between devices: 81.9 us -> 73.3 us  [to_ring(): return lax.ppermute(x, ('zh', 'c', 'zl'), moves)]
    all_to_all x4, starting transfers between devices: 31.3 us -> 26 us  [over_plane(): return lax.all_to_all(x, PLANE, split_axis=0, concat_axis=0, tiled=True)]
    ppermute x4 -> x5, starting transfers between devices: 19 us -> 16.4 us  [to_core(): return lax.ppermute(x, 'c', [(0, 1), (1, 0)])]
  transfers between devices with their start and end apart: 24 -> 25, of which waited for: 16 -> 13; matrix products, arithmetic and copies ran while one was open for 3% -> 4% of each run, Pallas kernels for 8% -> 13%
where the time goes in v4:
time: 237 us
  waiting for transfers between devices  108 us (46%)
  starting transfers between devices  76.5 us (32%)
  Pallas kernels  40.6 us (17%)
  local copies, waits for them, and re-layouts  5.1 us (2%)
  other arithmetic  4.95 us (2%)
    ppermute x12, waiting for transfers between devices, to_ring(): return lax.ppermute(x, ('zh', 'c', 'zl'), moves)  73.3 us
    all_to_all x4, starting transfers between devices, over_plane(): return lax.all_to_all(x, PLANE, split_axis=0, concat_axis=0, tiled=True)  26 us
    ppermute x4, waiting for transfers between devices, to_far(): return lax.ppermute(x, RING, [(i, (i + 4) % NZ) for i in range(NZ)])  23 us
    ppermute x12, starting transfers between devices, to_ring(): return lax.ppermute(x, ('zh', 'c', 'zl'), moves)  22.9 us
    pallas_call x2, Pallas kernels, convolve(): pl.pallas_call(functools.partial(convolve_kernel, len(ins) == 1, joined_o...  18.2 us
    ppermute x5, starting transfers between devices, to_core(): return lax.ppermute(x, 'c', [(0, 1), (1, 0)])  16.4 us
    pallas_call x4, Pallas kernels, local_call(): pl.pallas_call(lambda *refs: kernel(refs[:1], refs[1:1 + count], refs[1 +...  14 us
    all_to_all x4, waiting for transfers between devices, over_plane(): return lax.all_to_all(x, PLANE, split_axis=0, concat_axis=0, tiled=True)  12 us
  transfers between devices with their start and end apart: 25, of which 13 were waited for; matrix products, arithmetic and copies ran while one was open for 4% of the time, Pallas kernels for 13%

profile of v4, /device:TPU:1, one launch (start us, length us, event | category | flops | bytes accessed | tf_op | source)
XLA Modules:
  0.0 236.5 jit_solution(4242101176734801274)
XLA Ops:
  1.3 3.7 %pack_ring.1 = (f32[16,2,2,8,128]{4,3,2,1,0:T(8,128)}, f32[16,2,2,8,128]{4,3,2,1,0:T(8,128)}, f32[3,16,2,2,8,128]{5,4,3,2,1,0:T(8,128)}, f32[3,16,2,2,8,128]{5,4,3,2,1,0:T(8,128)}, f32[4,16,128]{2,1,0:T(8,128)}) custom-call(s32[2]{0:T(128)} %pad_add_fusion.refs_0_, f32[2,16,16,8,128]{4,3,2,1,0:T(8,128)} %bitcast.63, f32[2,16,16,8,128]{4,3,2,1,0:T(8,128)} %bitcast.65, ...), custom_call_target="tpu_custom_call" | custom-call | tf_op jit(solution)/shard_map/pack_ring/pallas_call | solution.py:109
  5.0 3.2 %collective-permute-start = (f32[3,32,16,128]{3,2,1,0:T(8,128)}, f32[3,32,16,128]{3,2,1,0:T(8,128)S(1)}, u32[]{:S(2)}, u32[]{:S(2)}) collective-permute-start(f32[3,32,16,128]{3,2,1,0:T(8,128)} %bitcast.78), channel_id=1, source_target_pairs={{0,4},{4,0},{1,5},{5,1},{2,6},{6,2},{3,7},{7,3},{8,12},{12,8},{9,1... | collective-permute-start | bytes 2359304 | tf_op jit(solution)/shard_map/ppermute | solution.py:487
  10.4 4.4 %collective-permute-start.2 = (f32[1040,128]{1,0:T(8,128)S(1)}, f32[1040,128]{1,0:T(8,128)S(1)}, u32[]{:S(2)}, u32[]{:S(2)}) collective-permute-start(f32[1040,128]{1,0:T(8,128)S(1)} %pad_maximum_fusion.1.refs_4_), channel_id=1, source_target_pairs={{0,2},{1,3},{2,32},{3,33},{4,38},{5,39},{6,4},{7,5},{32,34},{33,35... | collective-permute-start | bytes 1597448 | tf_op jit(solution)/shard_map/ppermute | solution.py:479
  17.7 4.4 %collective-permute-start.4 = (f32[32,16,128]{2,1,0:T(8,128)S(1)}, f32[32,16,128]{2,1,0:T(8,128)S(1)}, u32[]{:S(2)}, u32[]{:S(2)}) collective-permute-start(f32[32,16,128]{2,1,0:T(8,128)S(1)} %bitcast.79), channel_id=1, source_target_pairs={{0,32},{1,33},{2,34},{3,35},{32,0},{33,1},{34,2},{35,3},{4,36},{5,... | collective-permute-start | bytes 786440 | tf_op jit(solution)/shard_map/ppermute | solution.py:483
  23.4 3.7 %pack_plane.1 = f32[16,2,8,2,8,128]{5,4,3,2,1,0:T(8,128)} custom-call(s32[2]{0:T(128)} %pad_add_fusion.refs_0_, f32[2,16,16,8,128]{4,3,2,1,0:T(8,128)} %bitcast.64, f32[2,16,16,8,128]{4,3,2,1,0:T(8,128)} %bitcast.66, f32[1040,128]{1,0:T(8,128)} %pad_maximum_fusion.refs_3_, f32[1040,128]{1,0:T(8,128)} %copy-done.7, f32[1040,128]{1,0:T(8,128)} %pad_maximum_fusion.2.refs_5_), custom_call_target="tpu_custom_call" | custom-call | tf_op jit(solution)/shard_map/pack_plane/pallas_call | solution.py:109
  27.1 7.4 %all-to-all-start = ((f32[32,8,16,128]{3,2,1,0:T(8,128)}), f32[32,8,16,128]{3,2,1,0:T(8,128)}, u32[]{:S(2)}, u32[]{:S(2)}) async-start(f32[32,8,16,128]{3,2,1,0:T(8,128)} %bitcast.67), calls=%async_computation | async-start | bytes 4194304 | tf_op jit(solution)/shard_map/all_to_all | solution.py:491
  34.5 11.7 %collective-permute-done.4.refs_1_ = f32[32,16,128]{2,1,0:T(8,128)S(1)} collective-permute-done((f32[32,16,128]{2,1,0:T(8,128)S(1)}, f32[32,16,128]{2,1,0:T(8,128)S(1)}, u32[]{:S(2)}, u32[]{:S(2)}) %collective-permute-start.4) | collective-permute-done | bytes 262176 | tf_op jit(solution)/shard_map/ppermute | solution.py:483
  46.3 2.5 %collective-permute-done.3 = f32[1040,128]{1,0:T(8,128)S(1)} collective-permute-done((f32[1040,128]{1,0:T(8,128)}, f32[1040,128]{1,0:T(8,128)S(1)}, u32[]{:S(2)}, u32[]{:S(2)}) %collective-permute-start.3) | collective-permute-done | bytes 532512 | tf_op jit(solution)/shard_map/ppermute | solution.py:479
  48.8 10.5 %collective-permute-done.1 = f32[1040,128]{1,0:T(8,128)S(1)} collective-permute-done((f32[1040,128]{1,0:T(8,128)}, f32[1040,128]{1,0:T(8,128)S(1)}, u32[]{:S(2)}, u32[]{:S(2)}) %collective-permute-start.1) | collective-permute-done | bytes 532512 | tf_op jit(solution)/shard_map/ppermute | solution.py:479
  60.9 2.0 all-to-all-done.refs_0_.refs_2_
  62.9 2.3 fan.2
  66.0 4.2 %collective-permute-start.7 = (f32[2,32,16,128]{3,2,1,0:T(8,128)S(1)}, f32[2,32,16,128]{3,2,1,0:T(8,128)S(1)}, u32[]{:S(2)}, u32[]{:S(2)}) collective-permute-start(f32[2,32,16,128]{3,2,1,0:T(8,128)S(1)} %get-tuple-element.32), channel_id=1, source_target_pairs={{0,2},{1,3},{2,32},{3,33},{4,38},{5,39},{6,4},{7,5},{32,34},{33,35... | collective-permute-start | bytes 1572872 | tf_op jit(solution)/shard_map/ppermute | solution.py:479
  71.9 9.4 %all-to-all-start.1 = ((f32[32,8,16,128]{3,2,1,0:T(8,128)}), f32[32,8,16,128]{3,2,1,0:T(8,128)}, u32[]{:S(2)}, u32[]{:S(2)}) async-start(f32[32,8,16,128]{3,2,1,0:T(8,128)} %get-tuple-element.34), calls=%async_computation.1 | async-start | bytes 4194304 | tf_op jit(solution)/shard_map/all_to_all | solution.py:491
  82.2 3.5 %collective-permute-done.5.refs_2_.refs_3_ = f32[32,16,128]{2,1,0:T(8,128)S(1)} collective-permute-done((f32[32,16,128]{2,1,0:T(8,128)}, f32[32,16,128]{2,1,0:T(8,128)S(1)}, u32[]{:S(2)}, u32[]{:S(2)}) %collective-permute-start.5) | collective-permute-done | bytes 262176 | tf_op jit(solution)/shard_map/ppermute | solution.py:483
  85.7 13.8 %collective-permute-done.7.refs_1_.refs_5_ = f32[2,32,16,128]{3,2,1,0:T(8,128)S(1)} collective-permute-done((f32[2,32,16,128]{3,2,1,0:T(8,128)S(1)}, f32[2,32,16,128]{3,2,1,0:T(8,128)S(1)}, u32[]{:S(2)}, u32[]{:S(2)}) %collective-permute-start.7) | collective-permute-done | bytes 524320 | tf_op jit(solution)/shard_map/ppermute | solution.py:479
  99.6 10.0 %all-to-all-done.1.refs_2_ = f32[32,8,16,128]{3,2,1,0:T(8,128)} async-done(((f32[32,8,16,128]{3,2,1,0:T(8,128)}), f32[32,8,16,128]{3,2,1,0:T(8,128)}, u32[]{:S(2)}, u32[]{:S(2)}) %all-to-all-start.1) | async-done | bytes 2097184 | tf_op jit(solution)/shard_map/all_to_all | solution.py:491
  109.6 9.1 %convolve.2 = (f32[32,16,128]{2,1,0:T(8,128)S(1)}, f32[32,16,128]{2,1,0:T(8,128)}, f32[3,32,16,128]{3,2,1,0:T(8,128)S(1)}, f32[3,32,16,128]{3,2,1,0:T(8,128)S(1)}) custom-call(s32[2]{0:T(128)S(1)} %copy-done, f32[64]{0:T(128)S(1)} %reshape.81.refs_1_, f32[32,8,16,128]{3,2,1,0:T(8,128)} %all-to-all-done.1.refs_2_, bf16[1408,256]{1,0:T(8,128)(2,1)S(1)} %copy-done.3, ...), custom_call_target="tpu_custom_call" | custom-call | flops 199999995904 | tf_op jit(solution)/shard_map/convolve/pallas_call | solution.py:400
  123.6 2.9 %collective-permute-start.13 = (f32[64,16,128]{2,1,0:T(8,128)}, f32[64,16,128]{2,1,0:T(8,128)}, u32[]{:S(2)}, u32[]{:S(2)}) collective-permute-start(f32[64,16,128]{2,1,0:T(8,128)} %pad_maximum_fusion.3.refs_11_), channel_id=1, source_target_pairs={{0,1},{1,2},{2,3},{3,32},{4,39},{5,4},{6,5},{7,6},{32,33},{33,34},... | collective-permute-start | bytes 1572872 | tf_op jit(solution)/shard_map/ppermute | solution.py:479
  129.2 3.6 %collective-permute-start.15 = (f32[64,16,128]{2,1,0:T(8,128)}, f32[64,16,128]{2,1,0:T(8,128)}, u32[]{:S(2)}, u32[]{:S(2)}) collective-permute-start(f32[64,16,128]{2,1,0:T(8,128)} %pad_maximum_fusion.5.refs_13_), channel_id=1, source_target_pairs={{0,3},{1,32},{2,33},{3,34},{4,37},{5,38},{6,39},{7,4},{32,35},{33,... | collective-permute-start | bytes 1572872 | tf_op jit(solution)/shard_map/ppermute | solution.py:479
  132.8 9.1 %convolve.3 = f32[32,8,16,128]{3,2,1,0:T(8,128)} custom-call(s32[2]{0:T(128)S(1)} %copy-done, f32[64]{0:T(128)S(1)} %reshape.81.refs_1_, f32[32,8,16,128]{3,2,1,0:T(8,128)} %all-to-all-done.refs_0_.refs_2_, f32[32,16,128]{2,1,0:T(8,128)S(1)} %collective-permute-done.5.refs_2_.refs_3_, f32[2,32,16,128]{3,2,1,0:T(8,128)S(1)} %collective-permute-done.6.refs_0_.refs_4_, ...), custom_call_target="tpu_custom_call" | custom-call | flops 199999995904 | tf_op jit(solution)/shard_map/convolve/pallas_call | solution.py:400
  142.0 4.7 %all-to-all-start.2 = ((f32[32,8,16,128]{3,2,1,0:T(8,128)}), f32[32,8,16,128]{3,2,1,0:T(8,128)}, u32[]{:S(2)}, u32[]{:S(2)}) async-start(f32[32,8,16,128]{3,2,1,0:T(8,128)} %convolve.3), calls=%async_computation.2 | async-start | bytes 4194304 | tf_op jit(solution)/shard_map/all_to_all | solution.py:491
  146.7 8.9 %collective-permute-done.14.refs_3_ = f32[64,16,128]{2,1,0:T(8,128)} collective-permute-done((f32[64,16,128]{2,1,0:T(8,128)}, f32[64,16,128]{2,1,0:T(8,128)}, u32[]{:S(2)}, u32[]{:S(2)}) %collective-permute-start.14) | collective-permute-done | bytes 524320 | tf_op jit(solution)/shard_map/ppermute | solution.py:479
  155.6 17.9 %collective-permute-done.15.refs_4_ = f32[64,16,128]{2,1,0:T(8,128)} collective-permute-done((f32[64,16,128]{2,1,0:T(8,128)}, f32[64,16,128]{2,1,0:T(8,128)}, u32[]{:S(2)}, u32[]{:S(2)}) %collective-permute-start.15) | collective-permute-done | bytes 524320 | tf_op jit(solution)/shard_map/ppermute | solution.py:479
  173.6 2.4 %merge.3.refs_1_ = f32[32,8,16,128]{3,2,1,0:T(8,128)} custom-call(f32[32,16,128]{2,1,0:T(8,128)S(1)} %copy-done.6, f32[32,16,128]{2,1,0:T(8,128)} %collective-permute-done.12.refs_1_, f32[64,16,128]{2,1,0:T(8,128)} %collective-permute-done.13.refs_2_, f32[64,16,128]{2,1,0:T(8,128)} %collective-permute-done.14.refs_3_, ...), custom_call_target="tpu_custom_call" | custom-call | flops 199999995904 | tf_op jit(solution)/shard_map/merge/pallas_call | solution.py:226
  181.7 4.4 %collective-permute-start.16 = (f32[32,16,128]{2,1,0:T(8,128)}, f32[32,16,128]{2,1,0:T(8,128)S(1)}, u32[]{:S(2)}, u32[]{:S(2)}) collective-permute-start(f32[32,16,128]{2,1,0:T(8,128)} %get-tuple-element.39), channel_id=1, source_target_pairs={{0,32},{1,33},{2,34},{3,35},{32,0},{33,1},{34,2},{35,3},{4,36},{5,... | collective-permute-start | bytes 786440 | tf_op jit(solution)/shard_map/ppermute | solution.py:483
  186.1 4.5 %all-to-all-start.3 = ((f32[32,8,16,128]{3,2,1,0:T(8,128)}), f32[32,8,16,128]{3,2,1,0:T(8,128)}, u32[]{:S(2)}, u32[]{:S(2)}) async-start(f32[32,8,16,128]{3,2,1,0:T(8,128)} %get-tuple-element.43), calls=%async_computation.3 | async-start | bytes 4194304 | tf_op jit(solution)/shard_map/all_to_all | solution.py:491
  190.7 7.8 %collective-permute-done.16.refs_3_ = f32[32,16,128]{2,1,0:T(8,128)S(1)} collective-permute-done((f32[32,16,128]{2,1,0:T(8,128)}, f32[32,16,128]{2,1,0:T(8,128)S(1)}, u32[]{:S(2)}, u32[]{:S(2)}) %collective-permute-start.16) | collective-permute-done | bytes 262176 | tf_op jit(solution)/shard_map/ppermute | solution.py:483
  198.5 3.1 %collective-permute-done.18.refs_1_ = f32[2,32,16,128]{3,2,1,0:T(8,128)S(1)} collective-permute-done((f32[2,32,16,128]{3,2,1,0:T(8,128)S(1)}, f32[2,32,16,128]{3,2,1,0:T(8,128)S(1)}, u32[]{:S(2)}, u32[]{:S(2)}) %collective-permute-start.18) | collective-permute-done | bytes 524320 | tf_op jit(solution)/shard_map/ppermute | solution.py:479
  201.5 16.5 %collective-permute-done.19.refs_2_ = f32[2,32,16,128]{3,2,1,0:T(8,128)S(1)} collective-permute-done((f32[2,32,16,128]{3,2,1,0:T(8,128)S(1)}, f32[2,32,16,128]{3,2,1,0:T(8,128)S(1)}, u32[]{:S(2)}, u32[]{:S(2)}) %collective-permute-start.19) | collective-permute-done | bytes 524320 | tf_op jit(solution)/shard_map/ppermute | solution.py:479
  218.2 11.7 %collective-permute-start.20 = (f32[3,32,16,128]{3,2,1,0:T(8,128)S(1)}, f32[3,32,16,128]{3,2,1,0:T(8,128)S(1)}, u32[]{:S(2)}, u32[]{:S(2)}) collective-permute-start(f32[3,32,16,128]{3,2,1,0:T(8,128)S(1)} %give.3.refs_2_), channel_id=1, source_target_pairs={{0,4},{4,0},{1,5},{5,1},{2,6},{6,2},{3,7},{7,3},{8,12},{12,8},{9,1... | collective-permute-start | bytes 2359304 | tf_op jit(solution)/shard_map/ppermute | solution.py:487
  229.9 3.6 %unpack.2 = (f32[2,16,16,8,128]{4,3,2,1,0:T(8,128)}, f32[2,16,16,8,128]{4,3,2,1,0:T(8,128)}) custom-call(s32[2]{0:T(128)S(1)} %copy-done.1, f32[16,2,8,2,8,128]{5,4,3,2,1,0:T(8,128)} %bitcast.38.refs_1_, f32[3,32,16,128]{3,2,1,0:T(8,128)S(1)} %give.3.refs_2_), custom_call_target="tpu_custom_call" | custom-call | tf_op jit(solution)/shard_map/unpack/pallas_call | solution.py:109
  233.6 3.0 %unpack.3 = (f32[2,16,16,8,128]{4,3,2,1,0:T(8,128)}, f32[2,16,16,8,128]{4,3,2,1,0:T(8,128)}) custom-call(s32[2]{0:T(128)S(1)} %copy-done.1, f32[16,2,8,2,8,128]{5,4,3,2,1,0:T(8,128)} %bitcast.32.refs_1_, f32[16,2,2,8,128]{4,3,2,1,0:T(8,128)S(1)} %bitcast.58, f32[2,16,2,2,8,128]{5,4,3,2,1,0:T(8,128)S(1)} %bitcast.55, ...), custom_call_target="tpu_custom_call", output_to_operand_aliasing={{0}: (7, {}), {1}: (8, {})} | custom-call | tf_op jit(solution)/shard_map/unpack/pallas_call | solution.py:109
  (69 shorter events, 25.7 us)
Async XLA Ops:
  5.0 5.4 %collective-permute-start = (f32[3,32,16,128]{3,2,1,0:T(8,128)}, f32[3,32,16,128]{3,2,1,0:T(8,128)S(1)}, u32[]{:S(2)}, u32[]{:S(2)}) collective-permute-start(f32[3,32,16,128]{3,2,1,0:T(8,128)} %bitcast.78), channel_id=1, source_target_pairs={{0,4},{4,0},{1,5},{5,1},{2,6},{6,2},{3,7},{7,3},{8,12},{12,8},{9,1... | collective-permute-start | bytes 2359304 | tf_op jit(solution)/shard_map/ppermute | solution.py:487
  10.4 12.9 %copy-start.7 = (f32[1040,128]{1,0:T(8,128)}, f32[1040,128]{1,0:T(8,128)S(1)}, u32[]{:S(2)}) copy-start(f32[1040,128]{1,0:T(8,128)S(1)} %pad_maximum_fusion.1.refs_4_) | copy-start | bytes 1597444
  10.4 35.8 %collective-permute-start.2 = (f32[1040,128]{1,0:T(8,128)S(1)}, f32[1040,128]{1,0:T(8,128)S(1)}, u32[]{:S(2)}, u32[]{:S(2)}) collective-permute-start(f32[1040,128]{1,0:T(8,128)S(1)} %pad_maximum_fusion.1.refs_4_), channel_id=1, source_target_pairs={{0,2},{1,3},{2,32},{3,33},{4,38},{5,39},{6,4},{7,5},{32,34},{33,35... | collective-permute-start | bytes 1597448 | tf_op jit(solution)/shard_map/ppermute | solution.py:479
  15.6 33.1 %collective-permute-start.3 = (f32[1040,128]{1,0:T(8,128)}, f32[1040,128]{1,0:T(8,128)S(1)}, u32[]{:S(2)}, u32[]{:S(2)}) collective-permute-start(f32[1040,128]{1,0:T(8,128)} %pad_maximum_fusion.2.refs_5_), channel_id=1, source_target_pairs={{0,3},{1,32},{2,33},{3,34},{4,37},{5,38},{6,39},{7,4},{32,35},{33,... | collective-permute-start | bytes 1597448 | tf_op jit(solution)/shard_map/ppermute | solution.py:479
  17.2 42.1 %collective-permute-start.1 = (f32[1040,128]{1,0:T(8,128)}, f32[1040,128]{1,0:T(8,128)S(1)}, u32[]{:S(2)}, u32[]{:S(2)}) collective-permute-start(f32[1040,128]{1,0:T(8,128)} %pad_maximum_fusion.refs_3_), channel_id=1, source_target_pairs={{0,1},{1,2},{2,3},{3,32},{4,39},{5,4},{6,5},{7,6},{32,33},{33,34},... | collective-permute-start | bytes 1597448 | tf_op jit(solution)/shard_map/ppermute | solution.py:479
  17.7 28.6 %collective-permute-start.4 = (f32[32,16,128]{2,1,0:T(8,128)S(1)}, f32[32,16,128]{2,1,0:T(8,128)S(1)}, u32[]{:S(2)}, u32[]{:S(2)}) collective-permute-start(f32[32,16,128]{2,1,0:T(8,128)S(1)} %bitcast.79), channel_id=1, source_target_pairs={{0,32},{1,33},{2,34},{3,35},{32,0},{33,1},{34,2},{35,3},{4,36},{5,... | collective-permute-start | bytes 786440 | tf_op jit(solution)/shard_map/ppermute | solution.py:483
  27.1 32.1 %copy-start.2 = (f32[16,2,2,8,128]{4,3,2,1,0:T(8,128)S(1)}, f32[16,2,2,8,128]{4,3,2,1,0:T(8,128)}, u32[]{:S(2)}) copy-start(f32[16,2,2,8,128]{4,3,2,1,0:T(8,128)} %get-tuple-element.28) | copy-start | bytes 786436
  27.1 35.7 %all-to-all-start = ((f32[32,8,16,128]{3,2,1,0:T(8,128)}), f32[32,8,16,128]{3,2,1,0:T(8,128)}, u32[]{:S(2)}, u32[]{:S(2)}) async-start(f32[32,8,16,128]{3,2,1,0:T(8,128)} %bitcast.67), calls=%async_computation | async-start | bytes 4194304 | tf_op jit(solution)/shard_map/all_to_all | solution.py:491
  60.8 10.9 %copy-start.8 = (f32[1,4,128]{2,1,0:T(4,128)S(1)}, f32[1,4,128]{2,1,0:T(4,128)}, u32[]{:S(2)}) copy-start(f32[1,4,128]{2,1,0:T(4,128)} %slice.63) | copy-start | bytes 6148
  65.1 20.5 %collective-permute-start.6 = (f32[2,32,16,128]{3,2,1,0:T(8,128)S(1)}, f32[2,32,16,128]{3,2,1,0:T(8,128)S(1)}, u32[]{:S(2)}, u32[]{:S(2)}) collective-permute-start(f32[2,32,16,128]{3,2,1,0:T(8,128)S(1)} %get-tuple-element.31), channel_id=1, source_target_pairs={{0,1},{1,2},{2,3},{3,32},{4,39},{5,4},{6,5},{7,6},{32,33},{33,34},... | collective-permute-start | bytes 1572872 | tf_op jit(solution)/shard_map/ppermute | solution.py:479
  66.0 33.5 %collective-permute-start.7 = (f32[2,32,16,128]{3,2,1,0:T(8,128)S(1)}, f32[2,32,16,128]{3,2,1,0:T(8,128)S(1)}, u32[]{:S(2)}, u32[]{:S(2)}) collective-permute-start(f32[2,32,16,128]{3,2,1,0:T(8,128)S(1)} %get-tuple-element.32), channel_id=1, source_target_pairs={{0,2},{1,3},{2,32},{3,33},{4,38},{5,39},{6,4},{7,5},{32,34},{33,35... | collective-permute-start | bytes 1572872 | tf_op jit(solution)/shard_map/ppermute | solution.py:479
  70.1 15.5 %collective-permute-start.5 = (f32[32,16,128]{2,1,0:T(8,128)}, f32[32,16,128]{2,1,0:T(8,128)S(1)}, u32[]{:S(2)}, u32[]{:S(2)}) collective-permute-start(f32[32,16,128]{2,1,0:T(8,128)} %get-tuple-element.30), channel_id=1, source_target_pairs={{0,32},{1,33},{2,34},{3,35},{32,0},{33,1},{34,2},{35,3},{4,36},{5,... | collective-permute-start | bytes 786440 | tf_op jit(solution)/shard_map/ppermute | solution.py:483
  71.9 37.7 %all-to-all-start.1 = ((f32[32,8,16,128]{3,2,1,0:T(8,128)}), f32[32,8,16,128]{3,2,1,0:T(8,128)}, u32[]{:S(2)}, u32[]{:S(2)}) async-start(f32[32,8,16,128]{3,2,1,0:T(8,128)} %get-tuple-element.34), calls=%async_computation.1 | async-start | bytes 4194304 | tf_op jit(solution)/shard_map/all_to_all | solution.py:491
  81.3 39.1 %collective-permute-start.8 = (f32[2,32,16,128]{3,2,1,0:T(8,128)}, f32[2,32,16,128]{3,2,1,0:T(8,128)}, u32[]{:S(2)}, u32[]{:S(2)}) collective-permute-start(f32[2,32,16,128]{3,2,1,0:T(8,128)} %get-tuple-element.33), channel_id=1, source_target_pairs={{0,3},{1,32},{2,33},{3,34},{4,37},{5,38},{6,39},{7,4},{32,35},{33,... | collective-permute-start | bytes 1572872 | tf_op jit(solution)/shard_map/ppermute | solution.py:479
  99.5 10.1 %copy-start.3 = (bf16[1408,256]{1,0:T(8,128)(2,1)S(1)}, bf16[1408,256]{1,0:T(8,128)(2,1)}, u32[]{:S(2)}) copy-start(bf16[1408,256]{1,0:T(8,128)(2,1)} %constant.38.clone.refs_3_.refs_9_) | copy-start | bytes 2162692
  99.5 10.1 %copy-start.4 = (f32[64,256]{1,0:T(8,128)S(1)}, f32[64,256]{1,0:T(8,128)}, u32[]{:S(2)}) copy-start(f32[64,256]{1,0:T(8,128)} %constant.39.clone.refs_4_.refs_10_) | copy-start | bytes 196612
  119.5 3.3 %collective-permute-start.11 = (f32[3,32,16,128]{3,2,1,0:T(8,128)S(1)}, f32[3,32,16,128]{3,2,1,0:T(8,128)S(1)}, u32[]{:S(2)}, u32[]{:S(2)}) collective-permute-start(f32[3,32,16,128]{3,2,1,0:T(8,128)S(1)} %get-tuple-element.36), channel_id=1, source_target_pairs={{0,4},{4,0},{1,5},{5,1},{2,6},{6,2},{3,7},{7,3},{8,12},{12,8},{9,1... | collective-permute-start | bytes 2359304 | tf_op jit(solution)/shard_map/ppermute | solution.py:487
  120.3 12.5 %collective-permute-start.9 = (f32[2,32,16,128]{3,2,1,0:T(8,128)S(1)}, f32[2,32,16,128]{3,2,1,0:T(8,128)S(1)}, u32[]{:S(2)}, u32[]{:S(2)}) collective-permute-start(f32[2,32,16,128]{3,2,1,0:T(8,128)S(1)} %give.2.refs_5_), channel_id=1, source_target_pairs={{0,4},{4,0},{1,5},{5,1},{2,6},{6,2},{3,7},{7,3},{8,12},{12,8},{9,1... | collective-permute-start | bytes 1572872 | tf_op jit(solution)/shard_map/ppermute | solution.py:487
  121.3 7.9 %collective-permute-start.10 = (f32[32,16,128]{2,1,0:T(8,128)S(1)}, f32[32,16,128]{2,1,0:T(8,128)S(1)}, u32[]{:S(2)}, u32[]{:S(2)}) collective-permute-start(f32[32,16,128]{2,1,0:T(8,128)S(1)} %slice_bitcast_fusion.3), channel_id=1, source_target_pairs={{0,4},{4,0},{1,5},{5,1},{2,6},{6,2},{3,7},{7,3},{8,12},{12,8},{9,1... | collective-permute-start | bytes 786440 | tf_op jit(solution)/shard_map/ppermute | solution.py:487
  121.9 24.8 %collective-permute-start.12 = (f32[32,16,128]{2,1,0:T(8,128)}, f32[32,16,128]{2,1,0:T(8,128)}, u32[]{:S(2)}, u32[]{:S(2)}) collective-permute-start(f32[32,16,128]{2,1,0:T(8,128)} %get-tuple-element.38), channel_id=1, source_target_pairs={{0,32},{1,33},{2,34},{3,35},{32,0},{33,1},{34,2},{35,3},{4,36},{5,... | collective-permute-start | bytes 786440 | tf_op jit(solution)/shard_map/ppermute | solution.py:483
  123.6 23.1 %collective-permute-start.13 = (f32[64,16,128]{2,1,0:T(8,128)}, f32[64,16,128]{2,1,0:T(8,128)}, u32[]{:S(2)}, u32[]{:S(2)}) collective-permute-start(f32[64,16,128]{2,1,0:T(8,128)} %pad_maximum_fusion.3.refs_11_), channel_id=1, source_target_pairs={{0,1},{1,2},{2,3},{3,32},{4,39},{5,4},{6,5},{7,6},{32,33},{33,34},... | collective-permute-start | bytes 1572872 | tf_op jit(solution)/shard_map/ppermute | solution.py:479
  127.3 28.3 %collective-permute-start.14 = (f32[64,16,128]{2,1,0:T(8,128)}, f32[64,16,128]{2,1,0:T(8,128)}, u32[]{:S(2)}, u32[]{:S(2)}) collective-permute-start(f32[64,16,128]{2,1,0:T(8,128)} %pad_maximum_fusion.4.refs_12_), channel_id=1, source_target_pairs={{0,2},{1,3},{2,32},{3,33},{4,38},{5,39},{6,4},{7,5},{32,34},{33,35... | collective-permute-start | bytes 1572872 | tf_op jit(solution)/shard_map/ppermute | solution.py:479
  129.2 44.3 %collective-permute-start.15 = (f32[64,16,128]{2,1,0:T(8,128)}, f32[64,16,128]{2,1,0:T(8,128)}, u32[]{:S(2)}, u32[]{:S(2)}) collective-permute-start(f32[64,16,128]{2,1,0:T(8,128)} %pad_maximum_fusion.5.refs_13_), channel_id=1, source_target_pairs={{0,3},{1,32},{2,33},{3,34},{4,37},{5,38},{6,39},{7,4},{32,35},{33,... | collective-permute-start | bytes 1572872 | tf_op jit(solution)/shard_map/ppermute | solution.py:479
  142.0 31.6 %copy-start.6 = (f32[32,16,128]{2,1,0:T(8,128)S(1)}, f32[32,16,128]{2,1,0:T(8,128)}, u32[]{:S(2)}) copy-start(f32[32,16,128]{2,1,0:T(8,128)} %copy-done.5) | copy-start | bytes 786436
  142.0 34.0 %all-to-all-start.2 = ((f32[32,8,16,128]{3,2,1,0:T(8,128)}), f32[32,8,16,128]{3,2,1,0:T(8,128)}, u32[]{:S(2)}, u32[]{:S(2)}) async-start(f32[32,8,16,128]{3,2,1,0:T(8,128)} %convolve.3), calls=%async_computation.2 | async-start | bytes 4194304 | tf_op jit(solution)/shard_map/all_to_all | solution.py:491
  177.8 20.7 %collective-permute-start.17 = (f32[2,32,16,128]{3,2,1,0:T(8,128)S(1)}, f32[2,32,16,128]{3,2,1,0:T(8,128)S(1)}, u32[]{:S(2)}, u32[]{:S(2)}) collective-permute-start(f32[2,32,16,128]{3,2,1,0:T(8,128)S(1)} %get-tuple-element.40), channel_id=1, source_target_pairs={{0,1},{1,2},{2,3},{3,32},{4,39},{5,4},{6,5},{7,6},{32,33},{33,34},... | collective-permute-start | bytes 1572872 | tf_op jit(solution)/shard_map/ppermute | solution.py:479
  179.0 22.5 %collective-permute-start.18 = (f32[2,32,16,128]{3,2,1,0:T(8,128)S(1)}, f32[2,32,16,128]{3,2,1,0:T(8,128)S(1)}, u32[]{:S(2)}, u32[]{:S(2)}) collective-permute-start(f32[2,32,16,128]{3,2,1,0:T(8,128)S(1)} %get-tuple-element.41), channel_id=1, source_target_pairs={{0,2},{1,3},{2,32},{3,33},{4,38},{5,39},{6,4},{7,5},{32,34},{33,35... | collective-permute-start | bytes 1572872 | tf_op jit(solution)/shard_map/ppermute | solution.py:479
  180.6 37.4 %collective-permute-start.19 = (f32[2,32,16,128]{3,2,1,0:T(8,128)S(1)}, f32[2,32,16,128]{3,2,1,0:T(8,128)S(1)}, u32[]{:S(2)}, u32[]{:S(2)}) collective-permute-start(f32[2,32,16,128]{3,2,1,0:T(8,128)S(1)} %get-tuple-element.42), channel_id=1, source_target_pairs={{0,3},{1,32},{2,33},{3,34},{4,37},{5,38},{6,39},{7,4},{32,35},{33,... | collective-permute-start | bytes 1572872 | tf_op jit(solution)/shard_map/ppermute | solution.py:479
  181.7 16.7 %collective-permute-start.16 = (f32[32,16,128]{2,1,0:T(8,128)}, f32[32,16,128]{2,1,0:T(8,128)S(1)}, u32[]{:S(2)}, u32[]{:S(2)}) collective-permute-start(f32[32,16,128]{2,1,0:T(8,128)} %get-tuple-element.39), channel_id=1, source_target_pairs={{0,32},{1,33},{2,34},{3,35},{32,0},{33,1},{34,2},{35,3},{4,36},{5,... | collective-permute-start | bytes 786440 | tf_op jit(solution)/shard_map/ppermute | solution.py:483
  186.1 43.8 %all-to-all-start.3 = ((f32[32,8,16,128]{3,2,1,0:T(8,128)}), f32[32,8,16,128]{3,2,1,0:T(8,128)}, u32[]{:S(2)}, u32[]{:S(2)}) async-start(f32[32,8,16,128]{3,2,1,0:T(8,128)} %get-tuple-element.43), calls=%async_computation.3 | async-start | bytes 4194304 | tf_op jit(solution)/shard_map/all_to_all | solution.py:491
  218.0 11.9 %copy-start.1 = (s32[2]{0:T(128)S(1)}, s32[2]{0:T(128)}, u32[]{:S(2)}) copy-start(s32[2]{0:T(128)} %pad_add_fusion.refs_0_) | copy-start | bytes 28
  218.2 15.4 %collective-permute-start.20 = (f32[3,32,16,128]{3,2,1,0:T(8,128)S(1)}, f32[3,32,16,128]{3,2,1,0:T(8,128)S(1)}, u32[]{:S(2)}, u32[]{:S(2)}) collective-permute-start(f32[3,32,16,128]{3,2,1,0:T(8,128)S(1)} %give.3.refs_2_), channel_id=1, source_target_pairs={{0,4},{4,0},{1,5},{5,1},{2,6},{6,2},{3,7},{7,3},{8,12},{12,8},{9,1... | collective-permute-start | bytes 2359304 | tf_op jit(solution)/shard_map/ppermute | solution.py:487
  (3 other events, 18.4 us)

commit v5 on v4

--- a/solution.py
+++ b/solution.py
@@ -18,7 +18,6 @@
 NZ, NU = 8, 32
 NXY = NU // 2
 STEPS = (1, 2, 3)
-PARTS = 1
 BLOCK = (NU, 16, 128)
 NJ, NB = 64, 128
 NE = NJ * NB
@@ -43,18 +42,29 @@
     zh, u = np.meshgrid(np.arange(2), np.arange(NU), indexing="ij")
     j = ((u // 8) * 16 + zh * 8 + u % 8).reshape(-1)
     outer = 2 * math.pi * (j[:, None] * np.arange(NJ)[None, :] % NJ) / NJ
-    inner = 2 * math.pi * (np.arange(NB)[:, None] * np.arange(NB)[None, :] % NB) / NB
+    half = np.arange(NB // 2)
+    evens = 2 * math.pi * (half[:, None] * 2 * half[None, :] % NB) / NB
+    odds = 2 * math.pi * (half[:, None] * (2 * half[None, :] + 1) % NB) / NB
     twist = 2 * math.pi * (np.arange(NJ)[:, None] * np.arange(NB)[None, :]) / NE
-    co, so, ci, si = np.cos(outer), np.sin(outer), np.cos(inner), np.sin(inner)
+    co, so = np.cos(outer), np.sin(outer)
     d1 = np.block([[co.T, so.T], [-so.T, co.T]])
-    d2 = np.block([[ci, -si], [si, ci]])
-    e2 = np.block([[ci, si], [-si, ci]])
+    ce, se, cd, sd = np.cos(evens), np.sin(evens), np.cos(odds), np.sin(odds)
+    inners = [
+        np.block([[ce, -se], [se, ce]]),
+        np.block([[cd, -sd], [-sd, -cd]]),
+        np.block([[ce.T, se.T], [-se.T, ce.T]]),
+        np.block([[cd.T, sd.T], [-sd.T, cd.T]]),
+    ]
     polar_scale, sigma_scale = NE**-1.5, -(float(NE) ** -2)
     e1p = polar_scale * np.block([[-so, -co], [co, -so]])
     e1s = sigma_scale * np.block([[co, -so], [so, co]])
-    products = [np.concatenate(halves(table), axis=1) for table in (d1, e1p, e1s)]
-    for table in (d2, e2):
-        products.extend(halves(table))
+    products = []
+    for table in (d1, e1p, e1s):
+        high, low = halves(table)
+        products.append(np.block([[high, high], [low, np.zeros_like(low)]]))
+    for table in inners:
+        high, low = halves(table)
+        products.append(np.block([[high, low], [high, np.zeros_like(low)]]))
     turns = np.concatenate([np.cos(twist), np.sin(twist)], axis=1).astype(np.float32)
     return np.concatenate(products, axis=0), turns
 
@@ -68,13 +78,10 @@
     return lax.dot_general(a, b, (((1,), (0,)), ((), ())), preferred_element_type=F32)
 
 
-def dot3(a, b):
-    return dot(a[0], b[0]) + (dot(a[0], b[1]) + dot(a[1], b[0]))
-
-
 def dot_pair(table, first, second):
     high, low = split(jnp.concatenate([first, second], axis=1))
-    out = dot(table, jnp.concatenate([high, high], axis=0)) + dot(table[:, :128], low)
+    out = dot(table, jnp.concatenate([high, low], axis=0))
+    out = out[:128] + out[128:]
     return out[:, :NB], out[:, NB:]
 
 
@@ -88,114 +95,135 @@
     return lax.rem(z + (shift + NZ), NZ)
 
 
-def whole(shape):
-    return pl.BlockSpec(shape, lambda i, *_: (0,) * len(shape))
-
-
-def part(shape, dim, at=()):
-    block, fixed = list(shape), [0] * len(shape)
-    block[dim] //= PARTS
-    for where, length, index in at:
-        block[where], fixed[where] = length, index
-    return pl.BlockSpec(
-        tuple(block), lambda i, *_: tuple(i if n == dim else f for n, f in enumerate(fixed))
-    )
-
-
-def local_call(
-    kernel, scalars, ins, in_specs, after, shapes, out_specs, name, aliases=None, work=0, limit=LIMIT
-):
+def staged_call(kernel, scalars, ins, after, shapes, scratch, sems, name, aliases=None, limit=LIMIT):
     count = len(ins)
+
+    def body(*refs):
+        outs = refs[1 + count + len(after) :][: len(shapes)]
+        kernel(refs[0], refs[1 : 1 + count], outs, refs[1 + count + len(after) + len(shapes) :])
+
     return pl.pallas_call(
-        lambda *refs: kernel(refs[:1], refs[1 : 1 + count], refs[1 + count + len(after) :]),
+        body,
         out_shape=[jax.ShapeDtypeStruct(s, F32) for s in shapes],
-        grid_spec=pltpu.PrefetchScalarGridSpec(
-            num_scalar_prefetch=1,
-            grid=(PARTS,),
-            in_specs=list(in_specs) + [HBM] * len(after),
-            out_specs=out_specs,
-        ),
+        in_specs=[SMEM] + [HBM] * (count + len(after)),
+        out_specs=[HBM] * len(shapes),
+        scratch_shapes=[pltpu.VMEM(s, F32) for s in scratch] + [pltpu.SemaphoreType.DMA((n,)) for n in sems],
         input_output_aliases=aliases or {},
         compiler_params=pltpu.CompilerParams(vmem_limit_bytes=limit),
-        cost_estimate=pl.CostEstimate(flops=work, bytes_accessed=0, transcendentals=0),
+        cost_estimate=pl.CostEstimate(flops=0, bytes_accessed=0, transcendentals=0),
         name=name,
     )(scalars, *ins, *after)
 
 
 GRID_IN = (2, 2 * NZ, NXY, 8, 128)
-
-
-def chunk_part(chunk):
-    return part(GRID_IN, 2, [(1, NZ, chunk)])
-
-
-def blocks_of(lesser, greater, zd):
-    for g, ref in enumerate((lesser, greater)):
-        yield g, *interleave(ref[0, zd], ref[1, zd])
-
-
-def pack_ring_kernel(scalars, ins, outs):
+SHIFTS = (-1, -2, -3, 1, 2, 3, 4, 0)
+
+
+def pull_all(pairs, sem):
+    copies = [pltpu.make_async_copy(s, t, sem.at[n]) for n, (s, t) in enumerate(pairs)]
+    for copy in copies:
+        copy.start()
+    return copies
+
+
+def pack_blocks(scalars, lesser, greater, held, built, in_sem, chunk, unit, done):
+    z = scalars[0]
+    places = [around(z, unit * shift) for shift in SHIFTS]
+    pairs = [
+        (ref.at[:, chunk * NZ + zd], held.at[n, g])
+        for n, zd in enumerate(places)
+        for g, ref in enumerate((lesser, greater))
+    ]
+    copies = pull_all(pairs, in_sem)
+    for n in range(NZ):
+        for g in range(2):
+            copies[2 * n + g].wait()
+            even, odd = interleave(held[n, g, 0], held[n, g, 1])
+            built[n, :, 0, 8 * g : 8 * g + 8] = even
+            built[n, :, 1, 8 * g : 8 * g + 8] = odd
+        done(n, SHIFTS[n])
+
+
+def pack_ring_kernel(scalars, ins, outs, scratch):
     lesser, greater, screen, couple = ins
-    own, far, keep, give, gains = outs
-    z, sign = scalars[0][0], scalars[0][1]
-    targets = [(own, 0), (far, 4)]
-    targets += [(keep.at[d - 1], sign * d) for d in STEPS]
-    targets += [(give.at[d - 1], -sign * d) for d in STEPS]
-    for dest, shift in targets:
-        for g, even, odd in blocks_of(lesser, greater, around(z, shift)):
-            dest[:, 0, g] = even
-            dest[:, 1, g] = odd
+    own, far, keep, give, own_gains, sent_gains = outs
+    held, built, small, gains, in_sem, out_sem, small_sem = scratch
+    z, sign = scalars[0], scalars[1]
+    small_in = [pltpu.make_async_copy(r, small.at[i], small_sem.at[i]) for i, r in enumerate((screen, couple))]
+    for copy in small_in:
+        copy.start()
+    pushes = []
+
+    def push(n, shift):
+        dest = own if shift == 0 else far if shift == 4 else keep.at[shift - 1] if shift > 0 else give.at[-shift - 1]
+        pushes.append(pltpu.make_async_copy(built.at[n], dest, out_sem.at[n]))
+        pushes[-1].start()
+
+    pack_blocks(scalars, lesser, greater, held, built, in_sem, 0, sign, push)
+    for copy in small_in:
+        copy.wait()
     for d in range(4):
         zd = around(z, sign * d)
-        rows = [ref[pl.ds(zd + q * NZ, 1), :] for ref in (screen, couple) for q in range(2)]
+        rows = [small[i, pl.ds(zd + q * NZ, 1), :] for i in range(2) for q in range(2)]
         gains[d] = jnp.concatenate(rows * 4, axis=0)
+    last = [
+        pltpu.make_async_copy(gains.at[0], own_gains, small_sem.at[2]),
+        pltpu.make_async_copy(gains.at[1:], sent_gains, small_sem.at[3]),
+    ]
+    for copy in last:
+        copy.start()
+    for copy in pushes + last:
+        copy.wait()
+
+
+PACKED = (NXY, 2, 16, 128)
+PACK_SCRATCH = [(NZ, 2, 2, NXY, 8, 128), (NZ, *PACKED)]
 
 
 def pack_ring(scalars, lesser, greater, screen, couple):
-    small = whole((16, 128))
-    one = (NXY, 2, 2, 8, 128)
-    shapes = [one, one, (3, *one), (3, *one), (4, 16, 128)]
-    own, far, keep, give, gains = local_call(
+    shapes = [PACKED, PACKED, (3, *PACKED), (3, *PACKED), (16, 128), (3, 16, 128)]
+    own, far, keep, give, own_gains, gains = staged_call(
         pack_ring_kernel,
         scalars,
         [lesser.reshape(GRID_IN), greater.reshape(GRID_IN), screen.reshape(16, 128), couple.reshape(16, 128)],
-        [chunk_part(0), chunk_part(0), small, small],
         [],
         shapes,
-        [part(one, 0), part(one, 0), part((3, *one), 1), part((3, *one), 1), whole((4, 16, 128))],
+        PACK_SCRATCH + [(2, 16, 128), (4, 16, 128)],
+        [2 * NZ, NZ, 4],
         "pack_ring",
         limit=FULL,
     )
-    return own.reshape(BLOCK), far.reshape(BLOCK), keep.reshape(3, *BLOCK), give.reshape(3, *BLOCK), gains
-
-
-def pack_plane_kernel(scalars, ins, outs):
+    keep, give = keep.reshape(3, *BLOCK), give.reshape(3, *BLOCK)
+    return own.reshape(BLOCK), far.reshape(BLOCK), keep, give, own_gains, gains
+
+
+def pack_plane_kernel(scalars, ins, outs, scratch):
     lesser, greater = ins
-    out = outs[0]
-    z = scalars[0][0]
-    for shift in range(-3, 5):
-        for g, even, odd in blocks_of(lesser, greater, around(z, shift)):
-            if shift in (0, 4):
-                out[:, 0, shift // 4, g] = even
-                out[:, 1, shift // 4, g] = odd
-            elif shift > 0:
-                out[:, 0, 2 * shift, g] = even
-                out[:, 0, 2 * shift + 1, g] = odd
-            else:
-                out[:, 1, -2 * shift, g] = odd
-                out[:, 1, -2 * shift + 1, g] = even
+    held, built, in_sem, out_sem = scratch
+    pushes = []
+
+    def push(n, shift):
+        for c in range(2):
+            core, slot = (c, shift // 4) if shift in (0, 4) else (0, 2 * shift + c)
+            if shift < 0:
+                core, slot = 1, -2 * shift + 1 - c
+            pushes.append(pltpu.make_async_copy(built.at[n, :, c], outs[0].at[:, core, slot], out_sem.at[2 * n + c]))
+            pushes[-1].start()
+
+    pack_blocks(scalars, lesser, greater, held, built, in_sem, 1, 1, push)
+    for copy in pushes:
+        copy.wait()
 
 
 def pack_plane(scalars, lesser, greater, after):
-    shape = (NXY, 2, NZ, 2, 8, 128)
-    (out,) = local_call(
+    (out,) = staged_call(
         pack_plane_kernel,
         scalars,
         [lesser.reshape(GRID_IN), greater.reshape(GRID_IN)],
-        [chunk_part(1), chunk_part(1)],
         after,
-        [shape],
-        [part(shape, 0)],
+        [(NXY, 2, NZ, 16, 128)],
+        PACK_SCRATCH,
+        [2 * NZ, 2 * NZ],
         "pack_plane",
         limit=FULL,
     )
@@ -267,7 +295,7 @@
 
 
 def convolve_kernel(joined_in, joined_out, chunk, n_after, *refs):
-    n_in = 1 if joined_in else 7
+    n_in = 1 if joined_in else 8
     n_out = 1 if joined_out else 4
     refs = list(refs)
     scalars, weights = refs[:2]
@@ -298,7 +326,7 @@
             pairs.append((source.at[:, c, slot], x_at.at[zs, :, core]))
     else:
         own, far = ins[:2]
-        got = [ins[5].at[0], ins[5].at[1], ins[6]]
+        got = [ins[5].at[0], ins[6], ins[7]]
         pairs.append((own.at[:, 0], xin.at[pl.ds(z * NU, NU)]))
         pairs.append((far, xin.at[pl.ds(around(z, 4) * NU, NU)]))
         for d in STEPS:
@@ -311,16 +339,25 @@
         copy.wait()
 
     products, turns = held
-    d1, e1p, e1s = [products[i * 128 : i * 128 + 128] for i in range(3)]
-    d2, e2 = [
-        (products[i * 512 + 384 : i * 512 + 640], products[i * 512 + 640 : i * 512 + 896]) for i in range(2)
-    ]
+    d1, e1p, e1s = [products[i * 256 : i * 256 + 256] for i in range(3)]
+    evens, odds, evens_back, odds_back = [products[768 + i * 256 : 1024 + i * 256] for i in range(4)]
     cos, sin = turns[:, :NB], turns[:, NB:]
+
+    def swap(x):
+        return pltpu.roll(x, NB // 2, 1)
+
+    def pick(first, second):
+        lane = lax.broadcasted_iota(jnp.int32, first.shape, 1)
+        return jnp.where(lane < NB // 2, first, second)
+
+    def dot_terms(x, table):
+        out = dot(jnp.concatenate(split(x), axis=1), table)
+        return out[:, :NB] + out[:, NB:]
     rows_in = xin.reshape((NZ * NU + 1) * 16, 128)
     rows_out = yout.reshape((NZ * NU + 1) * 16, 128)
 
     def step(kk, carry):
-        turned = []
+        sums, differences = [], []
         for g in range(2):
             for r in (0, 2):
                 sides = []
@@ -333,10 +370,15 @@
                     sides.append(jnp.concatenate(parts, axis=0))
                 for y in dot_pair(d1, *sides):
                     yr, yi = y[:NJ], y[NJ:]
-                    turned.append(jnp.concatenate([yr * cos + yi * sin, yi * cos - yr * sin], axis=1))
-        spec = dot3(split(jnp.concatenate(turned, axis=0)), d2)
-        lr, li = spec[:256, :NB], spec[:256, NB:]
-        gr, gi = spec[256:, :NB], spec[256:, NB:]
+                    tr, ti = yr * cos + yi * sin, yi * cos - yr * sin
+                    sr, si = swap(tr), swap(ti)
+                    sums.append(pick(tr + sr, ti + si))
+                    differences.append(pick(tr - sr, ti - si))
+        even = dot_terms(jnp.concatenate(sums, axis=0), evens)
+        odd = dot_terms(jnp.concatenate(differences, axis=0), odds)
+        real, imag = pick(even, swap(odd)), pick(swap(even), odd)
+        lr, gr = real[:256], real[256:]
+        li, gi = imag[:256], imag[256:]
         cr = lr * gr + li * gi
         ci = li * gr - lr * gi
         wr, wi = [], []
@@ -351,16 +393,18 @@
         wr, wi = jnp.concatenate(wr, axis=0), jnp.concatenate(wi, axis=0)
         vr = lr * wr - li * wi
         vi = lr * wi + li * wr
-        both = jnp.concatenate(
-            [jnp.concatenate([cr, ci], axis=1), jnp.concatenate([vr, vi], axis=1)], axis=0
-        )
-        back = dot3(split(both), e2)
+        real = jnp.concatenate([cr, vr], axis=0)
+        imag = jnp.concatenate([ci, vi], axis=0)
+        even = dot_terms(pick(real, swap(imag)), evens_back)
+        odd = dot_terms(pick(swap(real), imag), odds_back)
+        near, away = even + odd, even - odd
+        back_real, back_imag = pick(near, swap(away)), pick(swap(near), away)
         for o in range(2):
             for r in (0, 2):
                 sides = []
                 for row in (r, r + 1):
-                    part = back[(o * 4 + row) * NJ : (o * 4 + row + 1) * NJ]
-                    ar, ai = part[:, :NB], part[:, NB:]
+                    at = (o * 4 + row) * NJ
+                    ar, ai = back_real[at : at + NJ], back_imag[at : at + NJ]
                     sides.append(jnp.concatenate([ar * cos - ai * sin, ai * cos + ar * sin], axis=0))
                 for row, done in zip((r, r + 1), dot_pair((e1p, e1s)[o], *sides)):
                     for c in range(2):
@@ -415,55 +459,61 @@
     )(scalars, weights, *ins, *consts, *after)
 
 
-def unpack_kernel(joined, scalars, ins, outs):
-    z, sign = scalars[0][0], scalars[0][1]
-
-    def put(shift, even, odd):
-        for o in range(2):
-            real, imag = interleave(even[o], odd[o])
-            outs[o][0, around(z, shift)] = real
-            outs[o][1, around(z, shift)] = imag
-
+def unpack_kernel(joined, chunk, scalars, ins, outs, scratch):
+    held, built, in_sem, out_sem = scratch
+    z, sign = scalars[0], scalars[1]
+    pairs, places = [], []
     if joined:
-        v = ins[0]
-        for shift in range(-3, 5):
-            if shift in (0, 4):
-                even, odd = (0, shift // 4), (1, shift // 4)
-            elif shift < 0:
-                even, odd = (0, -2 * shift), (0, -2 * shift + 1)
-            else:
-                even, odd = (1, 2 * shift + 1), (1, 2 * shift)
-            put(shift, [v[:, *even, o] for o in range(2)], [v[:, *odd, o] for o in range(2)])
+        for n, shift in enumerate(SHIFTS):
+            places.append(around(z, shift))
+            for c in range(2):
+                core, slot = (c, shift // 4) if shift in (0, 4) else (0, -2 * shift + c)
+                if 0 < shift < 4:
+                    core, slot = 1, 2 * shift + 1 - c
+                pairs.append((ins[0].at[:, core, slot], held.at[n, :, c]))
     else:
         own, far, *paid, got = ins
-        put(0, *[[own[:, c, 0, o] for o in range(2)] for c in range(2)])
-        put(4, *[[far[:, c, o] for o in range(2)] for c in range(2)])
-        for d in STEPS:
-            put(-sign * d, *[[paid[d - 1][0, :, c, o] for o in range(2)] for c in range(2)])
-            put(sign * d, *[[got[d - 1, :, c, o] for o in range(2)] for c in range(2)])
+        sources = [(0, own.at[:, :, 0]), (4, far)]
+        sources += [(-sign * d, paid[d - 1].at[0]) for d in STEPS]
+        sources += [(sign * d, got.at[d - 1]) for d in STEPS]
+        for n, (shift, source) in enumerate(sources):
+            places.append(around(z, shift))
+            pairs.append((source, held.at[n]))
+    copies = pull_all(pairs, in_sem)
+    per = len(pairs) // NZ
+    pushes = []
+    for n in range(NZ):
+        for copy in copies[per * n : per * n + per]:
+            copy.wait()
+        for o in range(2):
+            real, imag = interleave(held[n, :, 0, 8 * o : 8 * o + 8], held[n, :, 1, 8 * o : 8 * o + 8])
+            built[n, o, 0] = real
+            built[n, o, 1] = imag
+            dest = outs[o].at[:, chunk * NZ + places[n]]
+            pushes.append(pltpu.make_async_copy(built.at[n, o], dest, out_sem.at[2 * n + o]))
+            pushes[-1].start()
+    for copy in pushes:
+        copy.wait()
 
 
 def unpack(scalars, ins, chunk, old, after):
     joined = len(ins) == 1
-    wide, one = (NXY, 2, NZ, 2, 8, 128), (NXY, 2, 2, 8, 128)
+    wide = (NXY, 2, NZ, 16, 128)
     if joined:
         ins = [ins[0].reshape(wide)]
-        specs = [part(wide, 0)]
     else:
         own, far, *paid, got = ins
-        ins = [own.reshape(wide), far.reshape(one)]
-        ins += [x.reshape(2, *one) for x in paid]
-        ins.append(got.reshape(3, *one))
-        specs = [part(wide, 0, [(2, 1, 0)]), part(one, 0)]
-        specs += [part((2, *one), 1, [(0, 1, 0)])] * 3 + [part((3, *one), 1)]
-    return local_call(
-        functools.partial(unpack_kernel, joined),
+        ins = [own.reshape(wide), far.reshape(PACKED)]
+        ins += [x.reshape(2, *PACKED) for x in paid]
+        ins.append(got.reshape(3, *PACKED))
+    return staged_call(
+        functools.partial(unpack_kernel, joined, chunk),
         scalars,
         ins,
-        specs,
         list(old) + after,
         [GRID_IN] * 2,
-        [chunk_part(chunk)] * 2,
+        [(NZ, *PACKED), (NZ, 2, 2, NXY, 8, 128)],
+        [2 * NZ, 2 * NZ],
         "unpack",
         {1 + len(ins) + i: i for i in range(len(old))},
     )
@@ -495,11 +545,11 @@
     z = lax.axis_index(RING).astype(jnp.int32)
     u = lax.axis_index(PLANE).astype(jnp.int32)
     scalars = jnp.stack([z, 1 - 2 * lax.rem(u, 2)])
-    own, far, keep, give, gains = pack_ring(scalars, green_lesser, green_greater, screen, couple)
+    own, far, keep, give, own_gains, gains = pack_ring(scalars, green_lesser, green_greater, screen, couple)
     far = to_far(far)
     got = to_core(give)
     rows = [
-        jnp.concatenate([keep[d - 1].reshape(512, 128), got[d - 1].reshape(512, 128), gains[d]], axis=0)
+        jnp.concatenate([keep[d - 1].reshape(512, 128), got[d - 1].reshape(512, 128), gains[d - 1]], axis=0)
         for d in STEPS
     ]
     second = over_plane(pack_plane(scalars, green_lesser, green_greater, rows))
@@ -510,13 +560,14 @@
     first = over_plane(first)
     far2 = to_far(far2)
     paid2 = [to_ring(x, d) for d, x in zip(STEPS, paid2)]
-    gains = jnp.stack([gains[0, :4]] + [x[1024:1028] for x in rows])
-    weights = lax.dynamic_slice(gains, (0, 0, u * KK), (4, 4, KK)).reshape(-1)
-    give2 = give_back(paid2[:2], far2)
+    weights = [lax.dynamic_slice(own_gains, (0, u * KK), (4, KK))]
+    weights += [lax.dynamic_slice(x, (x.shape[0] - 16, u * KK), (4, KK)) for x in rows]
+    weights = jnp.stack(weights).reshape(-1)
+    give2 = give_back(paid2[:1], far2)
 
     own, far, keep, give = convolve(scalars, weights, [first], False, 0, [give2])
     got = to_core(give)
-    got2 = [to_core(give2), to_core(paid2[2][1])]
+    got2 = [to_core(x) for x in (give2, paid2[1][1], paid2[2][1])]
     paid = [jnp.concatenate([keep[d - 1], got[d - 1]], axis=0) for d in STEPS]
     order = list(paid)
     far = to_far(far)

time: 237 us -> 236 us (level)
    all_to_all x4, waiting for transfers between devices: 12 us -> 24.5 us  [over_plane(): return lax.all_to_all(x, PLANE, split_axis=0, concat_axis=0, tiled=True)]
    ppermute x12, waiting for transfers between devices: 73.3 us -> 63.8 us  [to_ring(): return lax.ppermute(x, ('zh', 'c', 'zl'), moves)]
    ppermute x5 -> x6, starting transfers between devices: 16.4 us -> 12.5 us  [to_core(): return lax.ppermute(x, 'c', [(0, 1), (1, 0)])]
    ppermute x4, starting transfers between devices: 11.1 us -> 14.6 us  [to_far(): return lax.ppermute(x, RING, [(i, (i + 4) % NZ) for i in range(NZ)])]
  transfers between devices with their start and end apart: 25 -> 26, of which waited for: 13 -> 12; matrix products, arithmetic and copies ran while one was open for 4% -> 4% of each run, Pallas kernels for 13% -> 12%
where the time goes in v5:
time: 236 us; the launch traced here: 235 us
  waiting for transfers between devices  109 us (46%)
  starting transfers between devices  77.5 us (33%)
  Pallas kernels  38.3 us (16%)
  local copies, waits for them, and re-layouts  5.07 us (2%)
  other arithmetic  4.05 us (2%)
    ppermute x12, waiting for transfers between devices, to_ring(): return lax.ppermute(x, ('zh', 'c', 'zl'), moves)  63.8 us
    all_to_all x4, starting transfers between devices, over_plane(): return lax.all_to_all(x, PLANE, split_axis=0, concat_axis=0, tiled=True)  27 us
    all_to_all x4, waiting for transfers between devices, over_plane(): return lax.all_to_all(x, PLANE, split_axis=0, concat_axis=0, tiled=True)  24.5 us
    ppermute x12, starting transfers between devices, to_ring(): return lax.ppermute(x, ('zh', 'c', 'zl'), moves)  23.4 us
    ppermute x4, waiting for transfers between devices, to_far(): return lax.ppermute(x, RING, [(i, (i + 4) % NZ) for i in range(NZ)])  20.8 us
    pallas_call x2, Pallas kernels, convolve(): pl.pallas_call(functools.partial(convolve_kernel, len(ins) == 1, joined_o...  17.2 us
    ppermute x4, starting transfers between devices, to_far(): return lax.ppermute(x, RING, [(i, (i + 4) % NZ) for i in range(NZ)])  14.6 us
    pallas_call x4, Pallas kernels, staged_call(): pl.pallas_call(body, out_shape=[jax.ShapeDtypeStruct(s, F32) for s in sha...  12.8 us
  transfers between devices with their start and end apart: 26, of which 12 were waited for; matrix products, arithmetic and copies ran while one was open for 4% of the time, Pallas kernels for 12%

profile of v5, /device:TPU:1, one launch (start us, length us, event | category | flops | bytes accessed | tf_op | source)
XLA Modules:
  0.0 235.4 jit_solution(6012237229269473543)
XLA Ops:
  1.3 3.3 %pack_ring.1 = (f32[16,2,16,128]{3,2,1,0:T(8,128)}, f32[16,2,16,128]{3,2,1,0:T(8,128)}, f32[3,16,2,16,128]{4,3,2,1,0:T(8,128)}, f32[3,16,2,16,128]{4,3,2,1,0:T(8...) custom-call(s32[2]{0:T(128)} %pad_add_fusion.refs_0_, f32[2,16,16,8,128]{4,3,2,1,0:T(8,128)} %bitcast.67, ...), custom_call_target="tpu_custom_call" | custom-call | tf_op jit(solution)/shard_map/pack_ring/pallas_call | solution.py:105
  4.6 3.3 %collective-permute-start = (f32[3,32,16,128]{3,2,1,0:T(8,128)}, f32[3,32,16,128]{3,2,1,0:T(8,128)S(1)}, u32[]{:S(2)}, u32[]{:S(2)}) collective-permute-start(f32[3,32,16,128]{3,2,1,0:T(8,128)} %bitcast.82), channel_id=1, source_target_pairs={{0,4},{4,0},{1,5},{5,1},{2,6},{6,2},{3,7},{7,3},{8,12},{12,8},{9,1... | collective-permute-start | bytes 2359304 | tf_op jit(solution)/shard_map/ppermute | solution.py:537
  10.1 4.4 %collective-permute-start.2 = (f32[1040,128]{1,0:T(8,128)S(1)}, f32[1040,128]{1,0:T(8,128)S(1)}, u32[]{:S(2)}, u32[]{:S(2)}) collective-permute-start(f32[1040,128]{1,0:T(8,128)S(1)} %pad_maximum_fusion.1.refs_4_), channel_id=1, source_target_pairs={{0,2},{1,3},{2,32},{3,33},{4,38},{5,39},{6,4},{7,5},{32,34},{33,35... | collective-permute-start | bytes 1597448 | tf_op jit(solution)/shard_map/ppermute | solution.py:529
  16.6 4.5 %collective-permute-start.4 = (f32[32,16,128]{2,1,0:T(8,128)S(1)}, f32[32,16,128]{2,1,0:T(8,128)S(1)}, u32[]{:S(2)}, u32[]{:S(2)}) collective-permute-start(f32[32,16,128]{2,1,0:T(8,128)S(1)} %bitcast.83), channel_id=1, source_target_pairs={{0,32},{1,33},{2,34},{3,35},{32,0},{33,1},{34,2},{35,3},{4,36},{5,... | collective-permute-start | bytes 786440 | tf_op jit(solution)/shard_map/ppermute | solution.py:533
  21.1 3.3 %pack_plane.1 = f32[16,2,8,16,128]{4,3,2,1,0:T(8,128)} custom-call(s32[2]{0:T(128)} %pad_add_fusion.refs_0_, f32[2,16,16,8,128]{4,3,2,1,0:T(8,128)} %bitcast.68, f32[2,16,16,8,128]{4,3,2,1,0:T(8,128)} %bitcast.70, f32[1040,128]{1,0:T(8,128)} %pad_maximum_fusion.refs_3_, f32[1040,128]{1,0:T(8,128)} %copy-done.5, f32[1040,128]{1,0:T(8,128)} %copy-done.6), custom_call_target="tpu_custom_call" | custom-call | tf_op jit(solution)/shard_map/pack_plane/pallas_call | solution.py:105
  24.4 7.4 %all-to-all-start = ((f32[32,8,16,128]{3,2,1,0:T(8,128)}), f32[32,8,16,128]{3,2,1,0:T(8,128)}, u32[]{:S(2)}, u32[]{:S(2)}) async-start(f32[32,8,16,128]{3,2,1,0:T(8,128)} %bitcast.71), calls=%async_computation | async-start | bytes 4194304 | tf_op jit(solution)/shard_map/all_to_all | solution.py:541
  31.8 13.1 %collective-permute-done.4.refs_1_ = f32[32,16,128]{2,1,0:T(8,128)S(1)} collective-permute-done((f32[32,16,128]{2,1,0:T(8,128)S(1)}, f32[32,16,128]{2,1,0:T(8,128)S(1)}, u32[]{:S(2)}, u32[]{:S(2)}) %collective-permute-start.4) | collective-permute-done | bytes 262176 | tf_op jit(solution)/shard_map/ppermute | solution.py:533
  44.9 3.5 %collective-permute-done.3 = f32[1040,128]{1,0:T(8,128)S(1)} collective-permute-done((f32[1040,128]{1,0:T(8,128)S(1)}, f32[1040,128]{1,0:T(8,128)S(1)}, u32[]{:S(2)}, u32[]{:S(2)}) %collective-permute-start.3) | collective-permute-done | bytes 532512 | tf_op jit(solution)/shard_map/ppermute | solution.py:529
  48.4 10.5 %collective-permute-done.1 = f32[1040,128]{1,0:T(8,128)S(1)} collective-permute-done((f32[1040,128]{1,0:T(8,128)}, f32[1040,128]{1,0:T(8,128)S(1)}, u32[]{:S(2)}, u32[]{:S(2)}) %collective-permute-start.1) | collective-permute-done | bytes 532512 | tf_op jit(solution)/shard_map/ppermute | solution.py:529
  60.5 2.3 fan.2
  65.6 3.7 %collective-permute-start.5 = (f32[32,16,128]{2,1,0:T(8,128)S(1)}, f32[32,16,128]{2,1,0:T(8,128)S(1)}, u32[]{:S(2)}, u32[]{:S(2)}) collective-permute-start(f32[32,16,128]{2,1,0:T(8,128)S(1)} %get-tuple-element.32), channel_id=1, source_target_pairs={{0,32},{1,33},{2,34},{3,35},{32,0},{33,1},{34,2},{35,3},{4,36},{5,... | collective-permute-start | bytes 786440 | tf_op jit(solution)/shard_map/ppermute | solution.py:533
  69.5 7.7 %all-to-all-start.1 = ((f32[32,8,16,128]{3,2,1,0:T(8,128)}), f32[32,8,16,128]{3,2,1,0:T(8,128)}, u32[]{:S(2)}, u32[]{:S(2)}) async-start(f32[32,8,16,128]{3,2,1,0:T(8,128)} %get-tuple-element.36), calls=%async_computation.1 | async-start | bytes 4194304 | tf_op jit(solution)/shard_map/all_to_all | solution.py:541
  77.2 3.0 %collective-permute-start.7 = (f32[2,32,16,128]{3,2,1,0:T(8,128)}, f32[2,32,16,128]{3,2,1,0:T(8,128)}, u32[]{:S(2)}, u32[]{:S(2)}) collective-permute-start(f32[2,32,16,128]{3,2,1,0:T(8,128)} %get-tuple-element.34), channel_id=1, source_target_pairs={{0,2},{1,3},{2,32},{3,33},{4,38},{5,39},{6,4},{7,5},{32,34},{33,35... | collective-permute-start | bytes 1572872 | tf_op jit(solution)/shard_map/ppermute | solution.py:529
  80.2 2.6 %collective-permute-start.8 = (f32[2,32,16,128]{3,2,1,0:T(8,128)}, f32[2,32,16,128]{3,2,1,0:T(8,128)}, u32[]{:S(2)}, u32[]{:S(2)}) collective-permute-start(f32[2,32,16,128]{3,2,1,0:T(8,128)} %get-tuple-element.35), channel_id=1, source_target_pairs={{0,3},{1,32},{2,33},{3,34},{4,37},{5,38},{6,39},{7,4},{32,35},{33,... | collective-permute-start | bytes 1572872 | tf_op jit(solution)/shard_map/ppermute | solution.py:529
  83.0 22.6 %all-to-all-done.1.refs_2_ = f32[32,8,16,128]{3,2,1,0:T(8,128)} async-done(((f32[32,8,16,128]{3,2,1,0:T(8,128)}), f32[32,8,16,128]{3,2,1,0:T(8,128)}, u32[]{:S(2)}, u32[]{:S(2)}) %all-to-all-start.1) | async-done | bytes 2097184 | tf_op jit(solution)/shard_map/all_to_all | solution.py:541
  105.6 8.5 %convolve.2 = (f32[32,16,128]{2,1,0:T(8,128)S(1)}, f32[32,16,128]{2,1,0:T(8,128)}, f32[3,32,16,128]{3,2,1,0:T(8,128)S(1)}, f32[3,32,16,128]{3,2,1,0:T(8,128)S(1)}) custom-call(s32[2]{0:T(128)S(1)} %copy-done, f32[64]{0:T(128)S(1)} %reshape.81.refs_1_, f32[32,8,16,128]{3,2,1,0:T(8,128)} %all-to-all-done.1.refs_2_, bf16[1792,256]{1,0:T(8,128)(2,1)S(1)} %copy-done.3, ...), custom_call_target="tpu_custom_call" | custom-call | flops 199999995904 | tf_op jit(solution)/shard_map/convolve/pallas_call | solution.py:444
  119.6 2.2 collective-permute-start.13
  126.0 3.7 %collective-permute-start.15 = (f32[64,16,128]{2,1,0:T(8,128)}, f32[64,16,128]{2,1,0:T(8,128)}, u32[]{:S(2)}, u32[]{:S(2)}) collective-permute-start(f32[64,16,128]{2,1,0:T(8,128)} %pad_maximum_fusion.4.refs_13_), channel_id=1, source_target_pairs={{0,2},{1,3},{2,32},{3,33},{4,38},{5,39},{6,4},{7,5},{32,34},{33,35... | collective-permute-start | bytes 1572872 | tf_op jit(solution)/shard_map/ppermute | solution.py:529
  129.7 8.6 %convolve.3 = f32[32,8,16,128]{3,2,1,0:T(8,128)} custom-call(s32[2]{0:T(128)S(1)} %copy-done, f32[64]{0:T(128)S(1)} %reshape.81.refs_1_, f32[32,8,16,128]{3,2,1,0:T(8,128)} %all-to-all-done.refs_0_.refs_2_, f32[32,16,128]{2,1,0:T(8,128)S(1)} %collective-permute-done.5.refs_1_.refs_3_, f32[2,32,16,128]{3,2,1,0:T(8,128)S(1)} %collective-permute-done.6.refs_0_.refs_4_, ...), custom_call_target="tpu_custom_call" | custom-call | flops 199999995904 | tf_op jit(solution)/shard_map/convolve/pallas_call | solution.py:444
  138.4 7.3 %all-to-all-start.2 = ((f32[32,8,16,128]{3,2,1,0:T(8,128)}), f32[32,8,16,128]{3,2,1,0:T(8,128)}, u32[]{:S(2)}, u32[]{:S(2)}) async-start(f32[32,8,16,128]{3,2,1,0:T(8,128)} %convolve.3), calls=%async_computation.2 | async-start | bytes 4194304 | tf_op jit(solution)/shard_map/all_to_all | solution.py:541
  145.7 10.0 %collective-permute-done.15.refs_3_ = f32[64,16,128]{2,1,0:T(8,128)} collective-permute-done((f32[64,16,128]{2,1,0:T(8,128)}, f32[64,16,128]{2,1,0:T(8,128)}, u32[]{:S(2)}, u32[]{:S(2)}) %collective-permute-start.15) | collective-permute-done | bytes 524320 | tf_op jit(solution)/shard_map/ppermute | solution.py:529
  155.7 14.0 %collective-permute-done.16.refs_4_ = f32[64,16,128]{2,1,0:T(8,128)} collective-permute-done((f32[64,16,128]{2,1,0:T(8,128)}, f32[64,16,128]{2,1,0:T(8,128)}, u32[]{:S(2)}, u32[]{:S(2)}) %collective-permute-start.16) | collective-permute-done | bytes 524320 | tf_op jit(solution)/shard_map/ppermute | solution.py:529
  169.8 2.4 %merge.3.refs_1_ = f32[32,8,16,128]{3,2,1,0:T(8,128)} custom-call(f32[32,16,128]{2,1,0:T(8,128)S(1)} %get-tuple-element.39.refs_0_, f32[32,16,128]{2,1,0:T(8,128)} %collective-permute-done.13.refs_1_, f32[64,16,128]{2,1,0:T(8,128)} %collective-permute-done.14.refs_2_, f32[64,16,128]{2,1,0:T(8,128)} %collective-permute-done.15.refs_3_, ...), custom_call_target="tpu_custom_call" | custom-call | flops 199999995904 | tf_op jit(solution)/shard_map/merge/pallas_call | solution.py:254
  175.8 2.3 collective-permute-start.18
  180.9 4.2 %collective-permute-start.17 = (f32[32,16,128]{2,1,0:T(8,128)}, f32[32,16,128]{2,1,0:T(8,128)S(1)}, u32[]{:S(2)}, u32[]{:S(2)}) collective-permute-start(f32[32,16,128]{2,1,0:T(8,128)} %get-tuple-element.41), channel_id=1, source_target_pairs={{0,32},{1,33},{2,34},{3,35},{32,0},{33,1},{34,2},{35,3},{4,36},{5,... | collective-permute-start | bytes 786440 | tf_op jit(solution)/shard_map/ppermute | solution.py:533
  185.1 4.5 %all-to-all-start.3 = ((f32[32,8,16,128]{3,2,1,0:T(8,128)}), f32[32,8,16,128]{3,2,1,0:T(8,128)}, u32[]{:S(2)}, u32[]{:S(2)}) async-start(f32[32,8,16,128]{3,2,1,0:T(8,128)} %get-tuple-element.45), calls=%async_computation.3 | async-start | bytes 4194304 | tf_op jit(solution)/shard_map/all_to_all | solution.py:541
  189.7 7.7 %collective-permute-done.17.refs_3_ = f32[32,16,128]{2,1,0:T(8,128)S(1)} collective-permute-done((f32[32,16,128]{2,1,0:T(8,128)}, f32[32,16,128]{2,1,0:T(8,128)S(1)}, u32[]{:S(2)}, u32[]{:S(2)}) %collective-permute-start.17) | collective-permute-done | bytes 262176 | tf_op jit(solution)/shard_map/ppermute | solution.py:533
  197.4 4.8 %collective-permute-done.19.refs_1_ = f32[2,32,16,128]{3,2,1,0:T(8,128)S(1)} collective-permute-done((f32[2,32,16,128]{3,2,1,0:T(8,128)S(1)}, f32[2,32,16,128]{3,2,1,0:T(8,128)S(1)}, u32[]{:S(2)}, u32[]{:S(2)}) %collective-permute-start.19) | collective-permute-done | bytes 524320 | tf_op jit(solution)/shard_map/ppermute | solution.py:529
  202.2 20.7 %collective-permute-done.20.refs_2_ = f32[2,32,16,128]{3,2,1,0:T(8,128)S(1)} collective-permute-done((f32[2,32,16,128]{3,2,1,0:T(8,128)S(1)}, f32[2,32,16,128]{3,2,1,0:T(8,128)S(1)}, u32[]{:S(2)}, u32[]{:S(2)}) %collective-permute-start.20) | collective-permute-done | bytes 524320 | tf_op jit(solution)/shard_map/ppermute | solution.py:529
  223.1 5.8 %collective-permute-start.21 = (f32[3,32,16,128]{3,2,1,0:T(8,128)S(1)}, f32[3,32,16,128]{3,2,1,0:T(8,128)S(1)}, u32[]{:S(2)}, u32[]{:S(2)}) collective-permute-start(f32[3,32,16,128]{3,2,1,0:T(8,128)S(1)} %give.3.refs_2_), channel_id=1, source_target_pairs={{0,4},{4,0},{1,5},{5,1},{2,6},{6,2},{3,7},{7,3},{8,12},{12,8},{9,1... | collective-permute-start | bytes 2359304 | tf_op jit(solution)/shard_map/ppermute | solution.py:537
  228.9 3.2 %unpack.2 = (f32[2,16,16,8,128]{4,3,2,1,0:T(8,128)}, f32[2,16,16,8,128]{4,3,2,1,0:T(8,128)}) custom-call(s32[2]{0:T(128)S(1)} %copy-done.1, f32[16,2,8,16,128]{4,3,2,1,0:T(8,128)} %bitcast.40.refs_1_, f32[3,32,16,128]{3,2,1,0:T(8,128)S(1)} %give.3.refs_2_), custom_call_target="tpu_custom_call" | custom-call | tf_op jit(solution)/shard_map/unpack/pallas_call | solution.py:105
  232.1 3.1 %unpack.3 = (f32[2,16,16,8,128]{4,3,2,1,0:T(8,128)}, f32[2,16,16,8,128]{4,3,2,1,0:T(8,128)}) custom-call(s32[2]{0:T(128)S(1)} %copy-done.1, f32[16,2,8,16,128]{4,3,2,1,0:T(8,128)} %bitcast.34.refs_1_, f32[16,2,16,128]{3,2,1,0:T(8,128)S(1)} %bitcast.62, f32[2,16,2,16,128]{4,3,2,1,0:T(8,128)S(1)} %bitcast.59, ...), custom_call_target="tpu_custom_call", output_to_operand_aliasing={{0}: (7, {}), {1}: (8, {})} | custom-call | tf_op jit(solution)/shard_map/unpack/pallas_call | solution.py:105
  (68 shorter events, 25.8 us)
Async XLA Ops:
  4.6 5.5 %collective-permute-start = (f32[3,32,16,128]{3,2,1,0:T(8,128)}, f32[3,32,16,128]{3,2,1,0:T(8,128)S(1)}, u32[]{:S(2)}, u32[]{:S(2)}) collective-permute-start(f32[3,32,16,128]{3,2,1,0:T(8,128)} %bitcast.82), channel_id=1, source_target_pairs={{0,4},{4,0},{1,5},{5,1},{2,6},{6,2},{3,7},{7,3},{8,12},{12,8},{9,1... | collective-permute-start | bytes 2359304 | tf_op jit(solution)/shard_map/ppermute | solution.py:537
  9.8 6.9 %copy-start.7 = (f32[16,2,16,128]{3,2,1,0:T(8,128)S(1)}, f32[16,2,16,128]{3,2,1,0:T(8,128)}, u32[]{:S(2)}) copy-start(f32[16,2,16,128]{3,2,1,0:T(8,128)} %get-tuple-element.31) | copy-start | bytes 786436
  10.1 11.0 %copy-start.5 = (f32[1040,128]{1,0:T(8,128)}, f32[1040,128]{1,0:T(8,128)S(1)}, u32[]{:S(2)}) copy-start(f32[1040,128]{1,0:T(8,128)S(1)} %pad_maximum_fusion.1.refs_4_) | copy-start | bytes 1597444
  10.1 34.8 %collective-permute-start.2 = (f32[1040,128]{1,0:T(8,128)S(1)}, f32[1040,128]{1,0:T(8,128)S(1)}, u32[]{:S(2)}, u32[]{:S(2)}) collective-permute-start(f32[1040,128]{1,0:T(8,128)S(1)} %pad_maximum_fusion.1.refs_4_), channel_id=1, source_target_pairs={{0,2},{1,3},{2,32},{3,33},{4,38},{5,39},{6,4},{7,5},{32,34},{33,35... | collective-permute-start | bytes 1597448 | tf_op jit(solution)/shard_map/ppermute | solution.py:529
  14.5 33.9 %collective-permute-start.3 = (f32[1040,128]{1,0:T(8,128)S(1)}, f32[1040,128]{1,0:T(8,128)S(1)}, u32[]{:S(2)}, u32[]{:S(2)}) collective-permute-start(f32[1040,128]{1,0:T(8,128)S(1)} %pad_maximum_fusion.2.refs_5_), channel_id=1, source_target_pairs={{0,3},{1,32},{2,33},{3,34},{4,37},{5,38},{6,39},{7,4},{32,35},{33,... | collective-permute-start | bytes 1597448 | tf_op jit(solution)/shard_map/ppermute | solution.py:529
  16.2 42.8 %collective-permute-start.1 = (f32[1040,128]{1,0:T(8,128)}, f32[1040,128]{1,0:T(8,128)S(1)}, u32[]{:S(2)}, u32[]{:S(2)}) collective-permute-start(f32[1040,128]{1,0:T(8,128)} %pad_maximum_fusion.refs_3_), channel_id=1, source_target_pairs={{0,1},{1,2},{2,3},{3,32},{4,39},{5,4},{6,5},{7,6},{32,33},{33,34},... | collective-permute-start | bytes 1597448 | tf_op jit(solution)/shard_map/ppermute | solution.py:529
  16.6 28.3 %collective-permute-start.4 = (f32[32,16,128]{2,1,0:T(8,128)S(1)}, f32[32,16,128]{2,1,0:T(8,128)S(1)}, u32[]{:S(2)}, u32[]{:S(2)}) collective-permute-start(f32[32,16,128]{2,1,0:T(8,128)S(1)} %bitcast.83), channel_id=1, source_target_pairs={{0,32},{1,33},{2,34},{3,35},{32,0},{33,1},{34,2},{35,3},{4,36},{5,... | collective-permute-start | bytes 786440 | tf_op jit(solution)/shard_map/ppermute | solution.py:533
  24.4 34.5 %copy-start.2 = (f32[16,2,16,128]{3,2,1,0:T(8,128)S(1)}, f32[16,2,16,128]{3,2,1,0:T(8,128)}, u32[]{:S(2)}) copy-start(f32[16,2,16,128]{3,2,1,0:T(8,128)} %get-tuple-element.30) | copy-start | bytes 786436
  24.4 36.1 %all-to-all-start = ((f32[32,8,16,128]{3,2,1,0:T(8,128)}), f32[32,8,16,128]{3,2,1,0:T(8,128)}, u32[]{:S(2)}, u32[]{:S(2)}) async-start(f32[32,8,16,128]{3,2,1,0:T(8,128)} %bitcast.71), calls=%async_computation | async-start | bytes 4194304 | tf_op jit(solution)/shard_map/all_to_all | solution.py:541
  62.8 20.0 %collective-permute-start.6 = (f32[2,32,16,128]{3,2,1,0:T(8,128)S(1)}, f32[2,32,16,128]{3,2,1,0:T(8,128)S(1)}, u32[]{:S(2)}, u32[]{:S(2)}) collective-permute-start(f32[2,32,16,128]{3,2,1,0:T(8,128)S(1)} %get-tuple-element.33), channel_id=1, source_target_pairs={{0,1},{1,2},{2,3},{3,32},{4,39},{5,4},{6,5},{7,6},{32,33},{33,34},... | collective-permute-start | bytes 1572872 | tf_op jit(solution)/shard_map/ppermute | solution.py:529
  65.6 17.3 %collective-permute-start.5 = (f32[32,16,128]{2,1,0:T(8,128)S(1)}, f32[32,16,128]{2,1,0:T(8,128)S(1)}, u32[]{:S(2)}, u32[]{:S(2)}) collective-permute-start(f32[32,16,128]{2,1,0:T(8,128)S(1)} %get-tuple-element.32), channel_id=1, source_target_pairs={{0,32},{1,33},{2,34},{3,35},{32,0},{33,1},{34,2},{35,3},{4,36},{5,... | collective-permute-start | bytes 786440 | tf_op jit(solution)/shard_map/ppermute | solution.py:533
  69.5 36.1 %all-to-all-start.1 = ((f32[32,8,16,128]{3,2,1,0:T(8,128)}), f32[32,8,16,128]{3,2,1,0:T(8,128)}, u32[]{:S(2)}, u32[]{:S(2)}) async-start(f32[32,8,16,128]{3,2,1,0:T(8,128)} %get-tuple-element.36), calls=%async_computation.1 | async-start | bytes 4194304 | tf_op jit(solution)/shard_map/all_to_all | solution.py:541
  77.2 38.0 %collective-permute-start.7 = (f32[2,32,16,128]{3,2,1,0:T(8,128)}, f32[2,32,16,128]{3,2,1,0:T(8,128)}, u32[]{:S(2)}, u32[]{:S(2)}) collective-permute-start(f32[2,32,16,128]{3,2,1,0:T(8,128)} %get-tuple-element.34), channel_id=1, source_target_pairs={{0,2},{1,3},{2,32},{3,33},{4,38},{5,39},{6,4},{7,5},{32,34},{33,35... | collective-permute-start | bytes 1572872 | tf_op jit(solution)/shard_map/ppermute | solution.py:529
  80.2 36.6 %collective-permute-start.8 = (f32[2,32,16,128]{3,2,1,0:T(8,128)}, f32[2,32,16,128]{3,2,1,0:T(8,128)}, u32[]{:S(2)}, u32[]{:S(2)}) collective-permute-start(f32[2,32,16,128]{3,2,1,0:T(8,128)} %get-tuple-element.35), channel_id=1, source_target_pairs={{0,3},{1,32},{2,33},{3,34},{4,37},{5,38},{6,39},{7,4},{32,35},{33,... | collective-permute-start | bytes 1572872 | tf_op jit(solution)/shard_map/ppermute | solution.py:529
  82.9 22.7 %copy-start = (s32[2]{0:T(128)S(1)}, s32[2]{0:T(128)}, u32[]{:S(2)}) copy-start(s32[2]{0:T(128)} %pad_add_fusion.refs_0_) | copy-start | bytes 28
  82.9 22.7 %copy-start.3 = (bf16[1792,256]{1,0:T(8,128)(2,1)S(1)}, bf16[1792,256]{1,0:T(8,128)(2,1)}, u32[]{:S(2)}) copy-start(bf16[1792,256]{1,0:T(8,128)(2,1)} %constant.40.clone.refs_3_.refs_10_) | copy-start | bytes 2752516
  82.9 22.7 %copy-start.4 = (f32[64,256]{1,0:T(8,128)S(1)}, f32[64,256]{1,0:T(8,128)}, u32[]{:S(2)}) copy-start(f32[64,256]{1,0:T(8,128)} %constant.41.clone.refs_4_.refs_11_) | copy-start | bytes 196612
  114.1 7.8 %collective-permute-start.12 = (f32[3,32,16,128]{3,2,1,0:T(8,128)S(1)}, f32[3,32,16,128]{3,2,1,0:T(8,128)S(1)}, u32[]{:S(2)}, u32[]{:S(2)}) collective-permute-start(f32[3,32,16,128]{3,2,1,0:T(8,128)S(1)} %get-tuple-element.38), channel_id=1, source_target_pairs={{0,4},{4,0},{1,5},{5,1},{2,6},{6,2},{3,7},{7,3},{8,12},{12,8},{9,1... | collective-permute-start | bytes 2359304 | tf_op jit(solution)/shard_map/ppermute | solution.py:537
  115.1 10.9 %collective-permute-start.9 = (f32[1,32,16,128]{3,2,1,0:T(8,128)S(1)}, f32[1,32,16,128]{3,2,1,0:T(8,128)S(1)}, u32[]{:S(2)}, u32[]{:S(2)}) collective-permute-start(f32[1,32,16,128]{3,2,1,0:T(8,128)S(1)} %give.2.refs_5_), channel_id=1, source_target_pairs={{0,4},{4,0},{1,5},{5,1},{2,6},{6,2},{3,7},{7,3},{8,12},{12,8},{9,1... | collective-permute-start | bytes 786440 | tf_op jit(solution)/shard_map/ppermute | solution.py:537
  116.2 13.5 %collective-permute-start.10 = (f32[32,16,128]{2,1,0:T(8,128)S(1)}, f32[32,16,128]{2,1,0:T(8,128)S(1)}, u32[]{:S(2)}, u32[]{:S(2)}) collective-permute-start(f32[32,16,128]{2,1,0:T(8,128)S(1)} %slice_bitcast_fusion.4), channel_id=1, source_target_pairs={{0,4},{4,0},{1,5},{5,1},{2,6},{6,2},{3,7},{7,3},{8,12},{12,8},{9,1... | collective-permute-start | bytes 786440 | tf_op jit(solution)/shard_map/ppermute | solution.py:537
  117.8 12.0 %collective-permute-start.11 = (f32[32,16,128]{2,1,0:T(8,128)S(1)}, f32[32,16,128]{2,1,0:T(8,128)S(1)}, u32[]{:S(2)}, u32[]{:S(2)}) collective-permute-start(f32[32,16,128]{2,1,0:T(8,128)S(1)} %slice_bitcast_fusion.3), channel_id=1, source_target_pairs={{0,4},{4,0},{1,5},{5,1},{2,6},{6,2},{3,7},{7,3},{8,12},{12,8},{9,1... | collective-permute-start | bytes 786440 | tf_op jit(solution)/shard_map/ppermute | solution.py:537
  119.6 26.1 %collective-permute-start.13 = (f32[32,16,128]{2,1,0:T(8,128)}, f32[32,16,128]{2,1,0:T(8,128)}, u32[]{:S(2)}, u32[]{:S(2)}) collective-permute-start(f32[32,16,128]{2,1,0:T(8,128)} %get-tuple-element.40), channel_id=1, source_target_pairs={{0,32},{1,33},{2,34},{3,35},{32,0},{33,1},{34,2},{35,3},{4,36},{5,... | collective-permute-start | bytes 786440 | tf_op jit(solution)/shard_map/ppermute | solution.py:533
  122.8 22.9 %collective-permute-start.14 = (f32[64,16,128]{2,1,0:T(8,128)}, f32[64,16,128]{2,1,0:T(8,128)}, u32[]{:S(2)}, u32[]{:S(2)}) collective-permute-start(f32[64,16,128]{2,1,0:T(8,128)} %pad_maximum_fusion.3.refs_12_), channel_id=1, source_target_pairs={{0,1},{1,2},{2,3},{3,32},{4,39},{5,4},{6,5},{7,6},{32,33},{33,34},... | collective-permute-start | bytes 1572872 | tf_op jit(solution)/shard_map/ppermute | solution.py:529
  126.0 29.7 %collective-permute-start.15 = (f32[64,16,128]{2,1,0:T(8,128)}, f32[64,16,128]{2,1,0:T(8,128)}, u32[]{:S(2)}, u32[]{:S(2)}) collective-permute-start(f32[64,16,128]{2,1,0:T(8,128)} %pad_maximum_fusion.4.refs_13_), channel_id=1, source_target_pairs={{0,2},{1,3},{2,32},{3,33},{4,38},{5,39},{6,4},{7,5},{32,34},{33,35... | collective-permute-start | bytes 1572872 | tf_op jit(solution)/shard_map/ppermute | solution.py:529
  129.7 40.0 %collective-permute-start.16 = (f32[64,16,128]{2,1,0:T(8,128)}, f32[64,16,128]{2,1,0:T(8,128)}, u32[]{:S(2)}, u32[]{:S(2)}) collective-permute-start(f32[64,16,128]{2,1,0:T(8,128)} %pad_maximum_fusion.5.refs_14_), channel_id=1, source_target_pairs={{0,3},{1,32},{2,33},{3,34},{4,37},{5,38},{6,39},{7,4},{32,35},{33,... | collective-permute-start | bytes 1572872 | tf_op jit(solution)/shard_map/ppermute | solution.py:529
  138.4 35.6 %all-to-all-start.2 = ((f32[32,8,16,128]{3,2,1,0:T(8,128)}), f32[32,8,16,128]{3,2,1,0:T(8,128)}, u32[]{:S(2)}, u32[]{:S(2)}) async-start(f32[32,8,16,128]{3,2,1,0:T(8,128)} %convolve.3), calls=%async_computation.2 | async-start | bytes 4194304 | tf_op jit(solution)/shard_map/all_to_all | solution.py:541
  175.8 21.5 %collective-permute-start.18 = (f32[2,32,16,128]{3,2,1,0:T(8,128)S(1)}, f32[2,32,16,128]{3,2,1,0:T(8,128)S(1)}, u32[]{:S(2)}, u32[]{:S(2)}) collective-permute-start(f32[2,32,16,128]{3,2,1,0:T(8,128)S(1)} %get-tuple-element.42), channel_id=1, source_target_pairs={{0,1},{1,2},{2,3},{3,32},{4,39},{5,4},{6,5},{7,6},{32,33},{33,34},... | collective-permute-start | bytes 1572872 | tf_op jit(solution)/shard_map/ppermute | solution.py:529
  178.2 24.1 %collective-permute-start.19 = (f32[2,32,16,128]{3,2,1,0:T(8,128)S(1)}, f32[2,32,16,128]{3,2,1,0:T(8,128)S(1)}, u32[]{:S(2)}, u32[]{:S(2)}) collective-permute-start(f32[2,32,16,128]{3,2,1,0:T(8,128)S(1)} %get-tuple-element.43), channel_id=1, source_target_pairs={{0,2},{1,3},{2,32},{3,33},{4,38},{5,39},{6,4},{7,5},{32,34},{33,35... | collective-permute-start | bytes 1572872 | tf_op jit(solution)/shard_map/ppermute | solution.py:529
  179.6 43.4 %collective-permute-start.20 = (f32[2,32,16,128]{3,2,1,0:T(8,128)S(1)}, f32[2,32,16,128]{3,2,1,0:T(8,128)S(1)}, u32[]{:S(2)}, u32[]{:S(2)}) collective-permute-start(f32[2,32,16,128]{3,2,1,0:T(8,128)S(1)} %get-tuple-element.44), channel_id=1, source_target_pairs={{0,3},{1,32},{2,33},{3,34},{4,37},{5,38},{6,39},{7,4},{32,35},{33,... | collective-permute-start | bytes 1572872 | tf_op jit(solution)/shard_map/ppermute | solution.py:529
  180.9 16.5 %collective-permute-start.17 = (f32[32,16,128]{2,1,0:T(8,128)}, f32[32,16,128]{2,1,0:T(8,128)S(1)}, u32[]{:S(2)}, u32[]{:S(2)}) collective-permute-start(f32[32,16,128]{2,1,0:T(8,128)} %get-tuple-element.41), channel_id=1, source_target_pairs={{0,32},{1,33},{2,34},{3,35},{32,0},{33,1},{34,2},{35,3},{4,36},{5,... | collective-permute-start | bytes 786440 | tf_op jit(solution)/shard_map/ppermute | solution.py:533
  185.1 43.8 %all-to-all-start.3 = ((f32[32,8,16,128]{3,2,1,0:T(8,128)}), f32[32,8,16,128]{3,2,1,0:T(8,128)}, u32[]{:S(2)}, u32[]{:S(2)}) async-start(f32[32,8,16,128]{3,2,1,0:T(8,128)} %get-tuple-element.45), calls=%async_computation.3 | async-start | bytes 4194304 | tf_op jit(solution)/shard_map/all_to_all | solution.py:541
  223.1 9.0 %collective-permute-start.21 = (f32[3,32,16,128]{3,2,1,0:T(8,128)S(1)}, f32[3,32,16,128]{3,2,1,0:T(8,128)S(1)}, u32[]{:S(2)}, u32[]{:S(2)}) collective-permute-start(f32[3,32,16,128]{3,2,1,0:T(8,128)S(1)} %give.3.refs_2_), channel_id=1, source_target_pairs={{0,4},{4,0},{1,5},{5,1},{2,6},{6,2},{3,7},{7,3},{8,12},{12,8},{9,1... | collective-permute-start | bytes 2359304 | tf_op jit(solution)/shard_map/ppermute | solution.py:537
  (2 other events, 12.6 us)

commit v6 on v5

--- a/solution.py
+++ b/solution.py
@@ -126,27 +126,59 @@
     return copies
 
 
-def pack_blocks(scalars, lesser, greater, held, built, in_sem, chunk, unit, done):
+def pack_blocks(scalars, lesser, greater, held, built, in_sem, chunk, unit, done, shifts=SHIFTS):
     z = scalars[0]
-    places = [around(z, unit * shift) for shift in SHIFTS]
+    places = [around(z, unit * shift) for shift in shifts]
     pairs = [
         (ref.at[:, chunk * NZ + zd], held.at[n, g])
         for n, zd in enumerate(places)
         for g, ref in enumerate((lesser, greater))
     ]
     copies = pull_all(pairs, in_sem)
-    for n in range(NZ):
+    for n in range(len(shifts)):
         for g in range(2):
             copies[2 * n + g].wait()
             even, odd = interleave(held[n, g, 0], held[n, g, 1])
             built[n, :, 0, 8 * g : 8 * g + 8] = even
             built[n, :, 1, 8 * g : 8 * g + 8] = odd
-        done(n, SHIFTS[n])
+        done(n, shifts[n])
+
+
+PACKED = (NXY, 2, 16, 128)
+PACK_SCRATCH = [(NZ, 2, 2, NXY, 8, 128), (NZ, *PACKED)]
+
+
+def pack_give_kernel(scalars, ins, outs, scratch):
+    held, built, in_sem, out_sem = scratch
+    pushes = []
+
+    def push(n, shift):
+        pushes.append(pltpu.make_async_copy(built.at[n], outs[0].at[-shift - 1], out_sem.at[n]))
+        pushes[-1].start()
+
+    pack_blocks(scalars, *ins, held, built, in_sem, 0, scalars[1], push, SHIFTS[:3])
+    for copy in pushes:
+        copy.wait()
+
+
+def pack_give(scalars, lesser, greater):
+    (give,) = staged_call(
+        pack_give_kernel,
+        scalars,
+        [lesser.reshape(GRID_IN), greater.reshape(GRID_IN)],
+        [],
+        [(3, *PACKED)],
+        PACK_SCRATCH,
+        [2 * NZ, NZ],
+        "pack_give",
+        limit=FULL,
+    )
+    return give
 
 
 def pack_ring_kernel(scalars, ins, outs, scratch):
     lesser, greater, screen, couple = ins
-    own, far, keep, give, own_gains, sent_gains = outs
+    own, far, keep, own_gains, sent_gains = outs
     held, built, small, gains, in_sem, out_sem, small_sem = scratch
     z, sign = scalars[0], scalars[1]
     small_in = [pltpu.make_async_copy(r, small.at[i], small_sem.at[i]) for i, r in enumerate((screen, couple))]
@@ -155,11 +187,11 @@
     pushes = []
 
     def push(n, shift):
-        dest = own if shift == 0 else far if shift == 4 else keep.at[shift - 1] if shift > 0 else give.at[-shift - 1]
+        dest = own if shift == 0 else far if shift == 4 else keep.at[shift - 1]
         pushes.append(pltpu.make_async_copy(built.at[n], dest, out_sem.at[n]))
         pushes[-1].start()
 
-    pack_blocks(scalars, lesser, greater, held, built, in_sem, 0, sign, push)
+    pack_blocks(scalars, lesser, greater, held, built, in_sem, 0, sign, push, SHIFTS[3:])
     for copy in small_in:
         copy.wait()
     for d in range(4):
@@ -176,17 +208,14 @@
         copy.wait()
 
 
-PACKED = (NXY, 2, 16, 128)
-PACK_SCRATCH = [(NZ, 2, 2, NXY, 8, 128), (NZ, *PACKED)]
-
-
 def pack_ring(scalars, lesser, greater, screen, couple):
-    shapes = [PACKED, PACKED, (3, *PACKED), (3, *PACKED), (16, 128), (3, 16, 128)]
-    own, far, keep, give, own_gains, gains = staged_call(
+    give = pack_give(scalars, lesser, greater)
+    shapes = [PACKED, PACKED, (3, *PACKED), (16, 128), (3, 16, 128)]
+    own, far, keep, own_gains, gains = staged_call(
         pack_ring_kernel,
         scalars,
         [lesser.reshape(GRID_IN), greater.reshape(GRID_IN), screen.reshape(16, 128), couple.reshape(16, 128)],
-        [],
+        [give],
         shapes,
         PACK_SCRATCH + [(2, 16, 128), (4, 16, 128)],
         [2 * NZ, NZ, 4],

time: 236 us -> 238 us (level)
  Pallas kernels: 38.3 us -> 40.9 us
    pallas_call x4 -> x5, Pallas kernels: 12.8 us -> 15.4 us  [staged_call(): pl.pallas_call(body, out_shape=[jax.ShapeDtypeStruct(s, F32) for s in sha...]
  transfers between devices with their start and end apart: 26 -> 26, of which waited for: 12 -> 11; matrix products, arithmetic and copies ran while one was open for 4% -> 4% of each run, Pallas kernels for 12% -> 13%
where the time goes in v6:
time: 238 us; the launch traced here: 237 us
  waiting for transfers between devices  109 us (46%)
  starting transfers between devices  77.1 us (32%)
  Pallas kernels  40.9 us (17%)
  local copies, waits for them, and re-layouts  5.08 us (2%)
  other arithmetic  4.05 us (2%)
    ppermute x12, waiting for transfers between devices, to_ring(): return lax.ppermute(x, ('zh', 'c', 'zl'), moves)  63.7 us
    all_to_all x4, starting transfers between devices, over_plane(): return lax.all_to_all(x, PLANE, split_axis=0, concat_axis=0, tiled=True)  26.6 us
    all_to_all x4, waiting for transfers between devices, over_plane(): return lax.all_to_all(x, PLANE, split_axis=0, concat_axis=0, tiled=True)  24.5 us
    ppermute x12, starting transfers between devices, to_ring(): return lax.ppermute(x, ('zh', 'c', 'zl'), moves)  23.1 us
    ppermute x4, waiting for transfers between devices, to_far(): return lax.ppermute(x, RING, [(i, (i + 4) % NZ) for i in range(NZ)])  21 us
    pallas_call x2, Pallas kernels, convolve(): pl.pallas_call(functools.partial(convolve_kernel, len(ins) == 1, joined_o...  17.2 us
    pallas_call x5, Pallas kernels, staged_call(): pl.pallas_call(body, out_shape=[jax.ShapeDtypeStruct(s, F32) for s in sha...  15.4 us
    ppermute x4, starting transfers between devices, to_far(): return lax.ppermute(x, RING, [(i, (i + 4) % NZ) for i in range(NZ)])  14.8 us
  transfers between devices with their start and end apart: 26, of which 11 were waited for; matrix products, arithmetic and copies ran while one was open for 4% of the time, Pallas kernels for 13%

profile of v6, /device:TPU:1, one launch (start us, length us, event | category | flops | bytes accessed | tf_op | source)
XLA Modules:
  0.0 237.4 jit_solution(8378761055643030557)
XLA Ops:
  1.3 2.8 %pack_give.1.refs_5_ = f32[3,16,2,16,128]{4,3,2,1,0:T(8,128)} custom-call(s32[2]{0:T(128)} %pad_add_fusion.refs_0_, f32[2,16,16,8,128]{4,3,2,1,0:T(8,128)} %bitcast.67, f32[2,16,16,8,128]{4,3,2,1,0:T(8,128)} %bitcast.70), custom_call_target="tpu_custom_call" | custom-call | tf_op jit(solution)/shard_map/pack_give/pallas_call | solution.py:105
  4.1 3.3 %collective-permute-start = (f32[3,32,16,128]{3,2,1,0:T(8,128)}, f32[3,32,16,128]{3,2,1,0:T(8,128)S(1)}, u32[]{:S(2)}, u32[]{:S(2)}) collective-permute-start(f32[3,32,16,128]{3,2,1,0:T(8,128)} %bitcast.74), channel_id=1, source_target_pairs={{0,4},{4,0},{1,5},{5,1},{2,6},{6,2},{3,7},{7,3},{8,12},{12,8},{9,1... | collective-permute-start | bytes 2359304 | tf_op jit(solution)/shard_map/ppermute | solution.py:566
  7.4 3.0 %pack_ring.1 = (f32[16,2,16,128]{3,2,1,0:T(8,128)}, f32[16,2,16,128]{3,2,1,0:T(8,128)}, f32[3,16,2,16,128]{4,3,2,1,0:T(8,128)}, f32[16,128]{1,0:T(8,128)}, f32[3,16,128]{2,1,0:T(8,128)}) custom-call(s32[2]{0:T(128)} %pad_add_fusion.refs_0_, f32[2,16,16,8,128]{4,3,2,1,0:T(8,128)} %bitcast.68, f32[2,16,16,8,128]{4,3,2,1,0:T(8,128)} %bitcast.71, ...), custom_call_target="tpu_custom_call" | custom-call | tf_op jit(solution)/shard_map/pack_ring/pallas_call | solution.py:105
  12.5 4.4 %collective-permute-start.2 = (f32[1040,128]{1,0:T(8,128)S(1)}, f32[1040,128]{1,0:T(8,128)S(1)}, u32[]{:S(2)}, u32[]{:S(2)}) collective-permute-start(f32[1040,128]{1,0:T(8,128)S(1)} %pad_maximum_fusion.1.refs_4_), channel_id=1, source_target_pairs={{0,2},{1,3},{2,32},{3,33},{4,38},{5,39},{6,4},{7,5},{32,34},{33,35... | collective-permute-start | bytes 1597448 | tf_op jit(solution)/shard_map/ppermute | solution.py:558
  19.0 4.5 %collective-permute-start.4 = (f32[32,16,128]{2,1,0:T(8,128)S(1)}, f32[32,16,128]{2,1,0:T(8,128)S(1)}, u32[]{:S(2)}, u32[]{:S(2)}) collective-permute-start(f32[32,16,128]{2,1,0:T(8,128)S(1)} %bitcast.85), channel_id=1, source_target_pairs={{0,32},{1,33},{2,34},{3,35},{32,0},{33,1},{34,2},{35,3},{4,36},{5,... | collective-permute-start | bytes 786440 | tf_op jit(solution)/shard_map/ppermute | solution.py:562
  23.5 3.3 %pack_plane.1 = f32[16,2,8,16,128]{4,3,2,1,0:T(8,128)} custom-call(s32[2]{0:T(128)} %pad_add_fusion.refs_0_, f32[2,16,16,8,128]{4,3,2,1,0:T(8,128)} %bitcast.69, f32[2,16,16,8,128]{4,3,2,1,0:T(8,128)} %bitcast.72, f32[1040,128]{1,0:T(8,128)} %pad_maximum_fusion.refs_3_, f32[1040,128]{1,0:T(8,128)} %copy-done.5, f32[1040,128]{1,0:T(8,128)} %copy-done.6), custom_call_target="tpu_custom_call" | custom-call | tf_op jit(solution)/shard_map/pack_plane/pallas_call | solution.py:105
  26.8 7.4 %all-to-all-start = ((f32[32,8,16,128]{3,2,1,0:T(8,128)}), f32[32,8,16,128]{3,2,1,0:T(8,128)}, u32[]{:S(2)}, u32[]{:S(2)}) async-start(f32[32,8,16,128]{3,2,1,0:T(8,128)} %bitcast.73), calls=%async_computation | async-start | bytes 4194304 | tf_op jit(solution)/shard_map/all_to_all | solution.py:570
  34.2 13.3 %collective-permute-done.4.refs_1_ = f32[32,16,128]{2,1,0:T(8,128)S(1)} collective-permute-done((f32[32,16,128]{2,1,0:T(8,128)S(1)}, f32[32,16,128]{2,1,0:T(8,128)S(1)}, u32[]{:S(2)}, u32[]{:S(2)}) %collective-permute-start.4) | collective-permute-done | bytes 262176 | tf_op jit(solution)/shard_map/ppermute | solution.py:562
  47.5 3.2 %collective-permute-done.3 = f32[1040,128]{1,0:T(8,128)S(1)} collective-permute-done((f32[1040,128]{1,0:T(8,128)S(1)}, f32[1040,128]{1,0:T(8,128)S(1)}, u32[]{:S(2)}, u32[]{:S(2)}) %collective-permute-start.3) | collective-permute-done | bytes 532512 | tf_op jit(solution)/shard_map/ppermute | solution.py:558
  50.7 10.6 %collective-permute-done.1 = f32[1040,128]{1,0:T(8,128)S(1)} collective-permute-done((f32[1040,128]{1,0:T(8,128)}, f32[1040,128]{1,0:T(8,128)S(1)}, u32[]{:S(2)}, u32[]{:S(2)}) %collective-permute-start.1) | collective-permute-done | bytes 532512 | tf_op jit(solution)/shard_map/ppermute | solution.py:558
  67.9 3.7 %collective-permute-start.5 = (f32[32,16,128]{2,1,0:T(8,128)S(1)}, f32[32,16,128]{2,1,0:T(8,128)S(1)}, u32[]{:S(2)}, u32[]{:S(2)}) collective-permute-start(f32[32,16,128]{2,1,0:T(8,128)S(1)} %get-tuple-element.30), channel_id=1, source_target_pairs={{0,32},{1,33},{2,34},{3,35},{32,0},{33,1},{34,2},{35,3},{4,36},{5,... | collective-permute-start | bytes 786440 | tf_op jit(solution)/shard_map/ppermute | solution.py:562
  71.9 7.4 %all-to-all-start.1 = ((f32[32,8,16,128]{3,2,1,0:T(8,128)}), f32[32,8,16,128]{3,2,1,0:T(8,128)}, u32[]{:S(2)}, u32[]{:S(2)}) async-start(f32[32,8,16,128]{3,2,1,0:T(8,128)} %get-tuple-element.34), calls=%async_computation.1 | async-start | bytes 4194304 | tf_op jit(solution)/shard_map/all_to_all | solution.py:570
  79.2 3.0 %collective-permute-start.7 = (f32[2,32,16,128]{3,2,1,0:T(8,128)}, f32[2,32,16,128]{3,2,1,0:T(8,128)}, u32[]{:S(2)}, u32[]{:S(2)}) collective-permute-start(f32[2,32,16,128]{3,2,1,0:T(8,128)} %get-tuple-element.32), channel_id=1, source_target_pairs={{0,2},{1,3},{2,32},{3,33},{4,38},{5,39},{6,4},{7,5},{32,34},{33,35... | collective-permute-start | bytes 1572872 | tf_op jit(solution)/shard_map/ppermute | solution.py:558
  82.2 2.6 %collective-permute-start.8 = (f32[2,32,16,128]{3,2,1,0:T(8,128)}, f32[2,32,16,128]{3,2,1,0:T(8,128)}, u32[]{:S(2)}, u32[]{:S(2)}) collective-permute-start(f32[2,32,16,128]{3,2,1,0:T(8,128)} %get-tuple-element.33), channel_id=1, source_target_pairs={{0,3},{1,32},{2,33},{3,34},{4,37},{5,38},{6,39},{7,4},{32,35},{33,... | collective-permute-start | bytes 1572872 | tf_op jit(solution)/shard_map/ppermute | solution.py:558
  85.0 22.6 %all-to-all-done.1.refs_2_ = f32[32,8,16,128]{3,2,1,0:T(8,128)} async-done(((f32[32,8,16,128]{3,2,1,0:T(8,128)}), f32[32,8,16,128]{3,2,1,0:T(8,128)}, u32[]{:S(2)}, u32[]{:S(2)}) %all-to-all-start.1) | async-done | bytes 2097184 | tf_op jit(solution)/shard_map/all_to_all | solution.py:570
  107.6 8.5 %convolve.2 = (f32[32,16,128]{2,1,0:T(8,128)S(1)}, f32[32,16,128]{2,1,0:T(8,128)}, f32[3,32,16,128]{3,2,1,0:T(8,128)S(1)}, f32[3,32,16,128]{3,2,1,0:T(8,128)S(1)}) custom-call(s32[2]{0:T(128)S(1)} %copy-done, f32[64]{0:T(128)S(1)} %reshape.83.refs_1_, f32[32,8,16,128]{3,2,1,0:T(8,128)} %all-to-all-done.1.refs_2_, bf16[1792,256]{1,0:T(8,128)(2,1)S(1)} %copy-done.3, ...), custom_call_target="tpu_custom_call" | custom-call | flops 199999995904 | tf_op jit(solution)/shard_map/convolve/pallas_call | solution.py:473
  121.9 2.4 collective-permute-start.13
  128.0 3.7 %collective-permute-start.15 = (f32[64,16,128]{2,1,0:T(8,128)}, f32[64,16,128]{2,1,0:T(8,128)}, u32[]{:S(2)}, u32[]{:S(2)}) collective-permute-start(f32[64,16,128]{2,1,0:T(8,128)} %pad_maximum_fusion.4.refs_13_), channel_id=1, source_target_pairs={{0,2},{1,3},{2,32},{3,33},{4,38},{5,39},{6,4},{7,5},{32,34},{33,35... | collective-permute-start | bytes 1572872 | tf_op jit(solution)/shard_map/ppermute | solution.py:558
  131.7 8.6 %convolve.3 = f32[32,8,16,128]{3,2,1,0:T(8,128)} custom-call(s32[2]{0:T(128)S(1)} %copy-done, f32[64]{0:T(128)S(1)} %reshape.83.refs_1_, f32[32,8,16,128]{3,2,1,0:T(8,128)} %all-to-all-done.refs_0_.refs_2_, f32[32,16,128]{2,1,0:T(8,128)S(1)} %collective-permute-done.5.refs_1_.refs_3_, f32[2,32,16,128]{3,2,1,0:T(8,128)S(1)} %collective-permute-done.6.refs_0_.refs_4_, ...), custom_call_target="tpu_custom_call" | custom-call | flops 199999995904 | tf_op jit(solution)/shard_map/convolve/pallas_call | solution.py:473
  140.4 7.3 %all-to-all-start.2 = ((f32[32,8,16,128]{3,2,1,0:T(8,128)}), f32[32,8,16,128]{3,2,1,0:T(8,128)}, u32[]{:S(2)}, u32[]{:S(2)}) async-start(f32[32,8,16,128]{3,2,1,0:T(8,128)} %convolve.3), calls=%async_computation.2 | async-start | bytes 4194304 | tf_op jit(solution)/shard_map/all_to_all | solution.py:570
  147.7 10.0 %collective-permute-done.15.refs_3_ = f32[64,16,128]{2,1,0:T(8,128)} collective-permute-done((f32[64,16,128]{2,1,0:T(8,128)}, f32[64,16,128]{2,1,0:T(8,128)}, u32[]{:S(2)}, u32[]{:S(2)}) %collective-permute-start.15) | collective-permute-done | bytes 524320 | tf_op jit(solution)/shard_map/ppermute | solution.py:558
  157.7 14.0 %collective-permute-done.16.refs_4_ = f32[64,16,128]{2,1,0:T(8,128)} collective-permute-done((f32[64,16,128]{2,1,0:T(8,128)}, f32[64,16,128]{2,1,0:T(8,128)}, u32[]{:S(2)}, u32[]{:S(2)}) %collective-permute-start.16) | collective-permute-done | bytes 524320 | tf_op jit(solution)/shard_map/ppermute | solution.py:558
  171.7 2.4 %merge.3.refs_1_ = f32[32,8,16,128]{3,2,1,0:T(8,128)} custom-call(f32[32,16,128]{2,1,0:T(8,128)S(1)} %get-tuple-element.37.refs_0_, f32[32,16,128]{2,1,0:T(8,128)} %collective-permute-done.13.refs_1_, f32[64,16,128]{2,1,0:T(8,128)} %collective-permute-done.14.refs_2_, f32[64,16,128]{2,1,0:T(8,128)} %collective-permute-done.15.refs_3_, ...), custom_call_target="tpu_custom_call" | custom-call | flops 199999995904 | tf_op jit(solution)/shard_map/merge/pallas_call | solution.py:283
  177.8 2.3 collective-permute-start.18
  182.9 4.3 %collective-permute-start.17 = (f32[32,16,128]{2,1,0:T(8,128)}, f32[32,16,128]{2,1,0:T(8,128)S(1)}, u32[]{:S(2)}, u32[]{:S(2)}) collective-permute-start(f32[32,16,128]{2,1,0:T(8,128)} %get-tuple-element.39), channel_id=1, source_target_pairs={{0,32},{1,33},{2,34},{3,35},{32,0},{33,1},{34,2},{35,3},{4,36},{5,... | collective-permute-start | bytes 786440 | tf_op jit(solution)/shard_map/ppermute | solution.py:562
  187.1 4.5 %all-to-all-start.3 = ((f32[32,8,16,128]{3,2,1,0:T(8,128)}), f32[32,8,16,128]{3,2,1,0:T(8,128)}, u32[]{:S(2)}, u32[]{:S(2)}) async-start(f32[32,8,16,128]{3,2,1,0:T(8,128)} %get-tuple-element.43), calls=%async_computation.3 | async-start | bytes 4194304 | tf_op jit(solution)/shard_map/all_to_all | solution.py:570
  191.7 7.7 %collective-permute-done.17.refs_3_ = f32[32,16,128]{2,1,0:T(8,128)S(1)} collective-permute-done((f32[32,16,128]{2,1,0:T(8,128)}, f32[32,16,128]{2,1,0:T(8,128)S(1)}, u32[]{:S(2)}, u32[]{:S(2)}) %collective-permute-start.17) | collective-permute-done | bytes 262176 | tf_op jit(solution)/shard_map/ppermute | solution.py:562
  199.4 4.8 %collective-permute-done.19.refs_1_ = f32[2,32,16,128]{3,2,1,0:T(8,128)S(1)} collective-permute-done((f32[2,32,16,128]{3,2,1,0:T(8,128)S(1)}, f32[2,32,16,128]{3,2,1,0:T(8,128)S(1)}, u32[]{:S(2)}, u32[]{:S(2)}) %collective-permute-start.19) | collective-permute-done | bytes 524320 | tf_op jit(solution)/shard_map/ppermute | solution.py:558
  204.2 20.8 %collective-permute-done.20.refs_2_ = f32[2,32,16,128]{3,2,1,0:T(8,128)S(1)} collective-permute-done((f32[2,32,16,128]{3,2,1,0:T(8,128)S(1)}, f32[2,32,16,128]{3,2,1,0:T(8,128)S(1)}, u32[]{:S(2)}, u32[]{:S(2)}) %collective-permute-start.20) | collective-permute-done | bytes 524320 | tf_op jit(solution)/shard_map/ppermute | solution.py:558
  225.1 5.8 %collective-permute-start.21 = (f32[3,32,16,128]{3,2,1,0:T(8,128)S(1)}, f32[3,32,16,128]{3,2,1,0:T(8,128)S(1)}, u32[]{:S(2)}, u32[]{:S(2)}) collective-permute-start(f32[3,32,16,128]{3,2,1,0:T(8,128)S(1)} %give.3.refs_2_), channel_id=1, source_target_pairs={{0,4},{4,0},{1,5},{5,1},{2,6},{6,2},{3,7},{7,3},{8,12},{12,8},{9,1... | collective-permute-start | bytes 2359304 | tf_op jit(solution)/shard_map/ppermute | solution.py:566
  231.0 3.2 %unpack.2 = (f32[2,16,16,8,128]{4,3,2,1,0:T(8,128)}, f32[2,16,16,8,128]{4,3,2,1,0:T(8,128)}) custom-call(s32[2]{0:T(128)S(1)} %copy-done.1, f32[16,2,8,16,128]{4,3,2,1,0:T(8,128)} %bitcast.40.refs_1_, f32[3,32,16,128]{3,2,1,0:T(8,128)S(1)} %give.3.refs_2_), custom_call_target="tpu_custom_call" | custom-call | tf_op jit(solution)/shard_map/unpack/pallas_call | solution.py:105
  234.2 3.1 %unpack.3 = (f32[2,16,16,8,128]{4,3,2,1,0:T(8,128)}, f32[2,16,16,8,128]{4,3,2,1,0:T(8,128)}) custom-call(s32[2]{0:T(128)S(1)} %copy-done.1, f32[16,2,8,16,128]{4,3,2,1,0:T(8,128)} %bitcast.34.refs_1_, f32[16,2,16,128]{3,2,1,0:T(8,128)S(1)} %bitcast.62, f32[2,16,2,16,128]{4,3,2,1,0:T(8,128)S(1)} %bitcast.59, ...), custom_call_target="tpu_custom_call", output_to_operand_aliasing={{0}: (7, {}), {1}: (8, {})} | custom-call | tf_op jit(solution)/shard_map/unpack/pallas_call | solution.py:105
  (69 shorter events, 27.8 us)
Async XLA Ops:
  4.1 8.3 %collective-permute-start = (f32[3,32,16,128]{3,2,1,0:T(8,128)}, f32[3,32,16,128]{3,2,1,0:T(8,128)S(1)}, u32[]{:S(2)}, u32[]{:S(2)}) collective-permute-start(f32[3,32,16,128]{3,2,1,0:T(8,128)} %bitcast.74), channel_id=1, source_target_pairs={{0,4},{4,0},{1,5},{5,1},{2,6},{6,2},{3,7},{7,3},{8,12},{12,8},{9,1... | collective-permute-start | bytes 2359304 | tf_op jit(solution)/shard_map/ppermute | solution.py:566
  12.3 6.7 %copy-start.7 = (f32[16,2,16,128]{3,2,1,0:T(8,128)S(1)}, f32[16,2,16,128]{3,2,1,0:T(8,128)}, u32[]{:S(2)}) copy-start(f32[16,2,16,128]{3,2,1,0:T(8,128)} %get-tuple-element.29) | copy-start | bytes 786436
  12.5 11.0 %copy-start.5 = (f32[1040,128]{1,0:T(8,128)}, f32[1040,128]{1,0:T(8,128)S(1)}, u32[]{:S(2)}) copy-start(f32[1040,128]{1,0:T(8,128)S(1)} %pad_maximum_fusion.1.refs_4_) | copy-start | bytes 1597444
  12.5 35.0 %collective-permute-start.2 = (f32[1040,128]{1,0:T(8,128)S(1)}, f32[1040,128]{1,0:T(8,128)S(1)}, u32[]{:S(2)}, u32[]{:S(2)}) collective-permute-start(f32[1040,128]{1,0:T(8,128)S(1)} %pad_maximum_fusion.1.refs_4_), channel_id=1, source_target_pairs={{0,2},{1,3},{2,32},{3,33},{4,38},{5,39},{6,4},{7,5},{32,34},{33,35... | collective-permute-start | bytes 1597448 | tf_op jit(solution)/shard_map/ppermute | solution.py:558
  16.9 33.8 %collective-permute-start.3 = (f32[1040,128]{1,0:T(8,128)S(1)}, f32[1040,128]{1,0:T(8,128)S(1)}, u32[]{:S(2)}, u32[]{:S(2)}) collective-permute-start(f32[1040,128]{1,0:T(8,128)S(1)} %pad_maximum_fusion.2.refs_5_), channel_id=1, source_target_pairs={{0,3},{1,32},{2,33},{3,34},{4,37},{5,38},{6,39},{7,4},{32,35},{33,... | collective-permute-start | bytes 1597448 | tf_op jit(solution)/shard_map/ppermute | solution.py:558
  18.5 42.8 %collective-permute-start.1 = (f32[1040,128]{1,0:T(8,128)}, f32[1040,128]{1,0:T(8,128)S(1)}, u32[]{:S(2)}, u32[]{:S(2)}) collective-permute-start(f32[1040,128]{1,0:T(8,128)} %pad_maximum_fusion.refs_3_), channel_id=1, source_target_pairs={{0,1},{1,2},{2,3},{3,32},{4,39},{5,4},{6,5},{7,6},{32,33},{33,34},... | collective-permute-start | bytes 1597448 | tf_op jit(solution)/shard_map/ppermute | solution.py:558
  19.0 28.5 %collective-permute-start.4 = (f32[32,16,128]{2,1,0:T(8,128)S(1)}, f32[32,16,128]{2,1,0:T(8,128)S(1)}, u32[]{:S(2)}, u32[]{:S(2)}) collective-permute-start(f32[32,16,128]{2,1,0:T(8,128)S(1)} %bitcast.85), channel_id=1, source_target_pairs={{0,32},{1,33},{2,34},{3,35},{32,0},{33,1},{34,2},{35,3},{4,36},{5,... | collective-permute-start | bytes 786440 | tf_op jit(solution)/shard_map/ppermute | solution.py:562
  26.8 34.5 %copy-start.2 = (f32[16,2,16,128]{3,2,1,0:T(8,128)S(1)}, f32[16,2,16,128]{3,2,1,0:T(8,128)}, u32[]{:S(2)}) copy-start(f32[16,2,16,128]{3,2,1,0:T(8,128)} %get-tuple-element.28) | copy-start | bytes 786436
  26.8 36.1 %all-to-all-start = ((f32[32,8,16,128]{3,2,1,0:T(8,128)}), f32[32,8,16,128]{3,2,1,0:T(8,128)}, u32[]{:S(2)}, u32[]{:S(2)}) async-start(f32[32,8,16,128]{3,2,1,0:T(8,128)} %bitcast.73), calls=%async_computation | async-start | bytes 4194304 | tf_op jit(solution)/shard_map/all_to_all | solution.py:570
  65.2 19.7 %collective-permute-start.6 = (f32[2,32,16,128]{3,2,1,0:T(8,128)S(1)}, f32[2,32,16,128]{3,2,1,0:T(8,128)S(1)}, u32[]{:S(2)}, u32[]{:S(2)}) collective-permute-start(f32[2,32,16,128]{3,2,1,0:T(8,128)S(1)} %get-tuple-element.31), channel_id=1, source_target_pairs={{0,1},{1,2},{2,3},{3,32},{4,39},{5,4},{6,5},{7,6},{32,33},{33,34},... | collective-permute-start | bytes 1572872 | tf_op jit(solution)/shard_map/ppermute | solution.py:558
  67.9 16.9 %collective-permute-start.5 = (f32[32,16,128]{2,1,0:T(8,128)S(1)}, f32[32,16,128]{2,1,0:T(8,128)S(1)}, u32[]{:S(2)}, u32[]{:S(2)}) collective-permute-start(f32[32,16,128]{2,1,0:T(8,128)S(1)} %get-tuple-element.30), channel_id=1, source_target_pairs={{0,32},{1,33},{2,34},{3,35},{32,0},{33,1},{34,2},{35,3},{4,36},{5,... | collective-permute-start | bytes 786440 | tf_op jit(solution)/shard_map/ppermute | solution.py:562
  71.9 35.7 %all-to-all-start.1 = ((f32[32,8,16,128]{3,2,1,0:T(8,128)}), f32[32,8,16,128]{3,2,1,0:T(8,128)}, u32[]{:S(2)}, u32[]{:S(2)}) async-start(f32[32,8,16,128]{3,2,1,0:T(8,128)} %get-tuple-element.34), calls=%async_computation.1 | async-start | bytes 4194304 | tf_op jit(solution)/shard_map/all_to_all | solution.py:570
  79.2 38.0 %collective-permute-start.7 = (f32[2,32,16,128]{3,2,1,0:T(8,128)}, f32[2,32,16,128]{3,2,1,0:T(8,128)}, u32[]{:S(2)}, u32[]{:S(2)}) collective-permute-start(f32[2,32,16,128]{3,2,1,0:T(8,128)} %get-tuple-element.32), channel_id=1, source_target_pairs={{0,2},{1,3},{2,32},{3,33},{4,38},{5,39},{6,4},{7,5},{32,34},{33,35... | collective-permute-start | bytes 1572872 | tf_op jit(solution)/shard_map/ppermute | solution.py:558
  82.2 36.7 %collective-permute-start.8 = (f32[2,32,16,128]{3,2,1,0:T(8,128)}, f32[2,32,16,128]{3,2,1,0:T(8,128)}, u32[]{:S(2)}, u32[]{:S(2)}) collective-permute-start(f32[2,32,16,128]{3,2,1,0:T(8,128)} %get-tuple-element.33), channel_id=1, source_target_pairs={{0,3},{1,32},{2,33},{3,34},{4,37},{5,38},{6,39},{7,4},{32,35},{33,... | collective-permute-start | bytes 1572872 | tf_op jit(solution)/shard_map/ppermute | solution.py:558
  84.9 22.7 %copy-start = (s32[2]{0:T(128)S(1)}, s32[2]{0:T(128)}, u32[]{:S(2)}) copy-start(s32[2]{0:T(128)} %pad_add_fusion.refs_0_) | copy-start | bytes 28
  84.9 22.7 %copy-start.3 = (bf16[1792,256]{1,0:T(8,128)(2,1)S(1)}, bf16[1792,256]{1,0:T(8,128)(2,1)}, u32[]{:S(2)}) copy-start(bf16[1792,256]{1,0:T(8,128)(2,1)} %constant.40.clone.refs_3_.refs_10_) | copy-start | bytes 2752516
  84.9 22.7 %copy-start.4 = (f32[64,256]{1,0:T(8,128)S(1)}, f32[64,256]{1,0:T(8,128)}, u32[]{:S(2)}) copy-start(f32[64,256]{1,0:T(8,128)} %constant.41.clone.refs_4_.refs_11_) | copy-start | bytes 196612
  116.1 8.1 %collective-permute-start.12 = (f32[3,32,16,128]{3,2,1,0:T(8,128)S(1)}, f32[3,32,16,128]{3,2,1,0:T(8,128)S(1)}, u32[]{:S(2)}, u32[]{:S(2)}) collective-permute-start(f32[3,32,16,128]{3,2,1,0:T(8,128)S(1)} %get-tuple-element.36), channel_id=1, source_target_pairs={{0,4},{4,0},{1,5},{5,1},{2,6},{6,2},{3,7},{7,3},{8,12},{12,8},{9,1... | collective-permute-start | bytes 2359304 | tf_op jit(solution)/shard_map/ppermute | solution.py:566
  117.1 10.9 %collective-permute-start.9 = (f32[1,32,16,128]{3,2,1,0:T(8,128)S(1)}, f32[1,32,16,128]{3,2,1,0:T(8,128)S(1)}, u32[]{:S(2)}, u32[]{:S(2)}) collective-permute-start(f32[1,32,16,128]{3,2,1,0:T(8,128)S(1)} %give.2.refs_5_), channel_id=1, source_target_pairs={{0,4},{4,0},{1,5},{5,1},{2,6},{6,2},{3,7},{7,3},{8,12},{12,8},{9,1... | collective-permute-start | bytes 786440 | tf_op jit(solution)/shard_map/ppermute | solution.py:566
  118.2 13.6 %collective-permute-start.10 = (f32[32,16,128]{2,1,0:T(8,128)S(1)}, f32[32,16,128]{2,1,0:T(8,128)S(1)}, u32[]{:S(2)}, u32[]{:S(2)}) collective-permute-start(f32[32,16,128]{2,1,0:T(8,128)S(1)} %slice_bitcast_fusion.4), channel_id=1, source_target_pairs={{0,4},{4,0},{1,5},{5,1},{2,6},{6,2},{3,7},{7,3},{8,12},{12,8},{9,1... | collective-permute-start | bytes 786440 | tf_op jit(solution)/shard_map/ppermute | solution.py:566
  120.0 11.8 %collective-permute-start.11 = (f32[32,16,128]{2,1,0:T(8,128)S(1)}, f32[32,16,128]{2,1,0:T(8,128)S(1)}, u32[]{:S(2)}, u32[]{:S(2)}) collective-permute-start(f32[32,16,128]{2,1,0:T(8,128)S(1)} %slice_bitcast_fusion.3), channel_id=1, source_target_pairs={{0,4},{4,0},{1,5},{5,1},{2,6},{6,2},{3,7},{7,3},{8,12},{12,8},{9,1... | collective-permute-start | bytes 786440 | tf_op jit(solution)/shard_map/ppermute | solution.py:566
  121.9 25.8 %collective-permute-start.13 = (f32[32,16,128]{2,1,0:T(8,128)}, f32[32,16,128]{2,1,0:T(8,128)}, u32[]{:S(2)}, u32[]{:S(2)}) collective-permute-start(f32[32,16,128]{2,1,0:T(8,128)} %get-tuple-element.38), channel_id=1, source_target_pairs={{0,32},{1,33},{2,34},{3,35},{32,0},{33,1},{34,2},{35,3},{4,36},{5,... | collective-permute-start | bytes 786440 | tf_op jit(solution)/shard_map/ppermute | solution.py:562
  125.2 22.5 %collective-permute-start.14 = (f32[64,16,128]{2,1,0:T(8,128)}, f32[64,16,128]{2,1,0:T(8,128)}, u32[]{:S(2)}, u32[]{:S(2)}) collective-permute-start(f32[64,16,128]{2,1,0:T(8,128)} %pad_maximum_fusion.3.refs_12_), channel_id=1, source_target_pairs={{0,1},{1,2},{2,3},{3,32},{4,39},{5,4},{6,5},{7,6},{32,33},{33,34},... | collective-permute-start | bytes 1572872 | tf_op jit(solution)/shard_map/ppermute | solution.py:558
  128.0 29.7 %collective-permute-start.15 = (f32[64,16,128]{2,1,0:T(8,128)}, f32[64,16,128]{2,1,0:T(8,128)}, u32[]{:S(2)}, u32[]{:S(2)}) collective-permute-start(f32[64,16,128]{2,1,0:T(8,128)} %pad_maximum_fusion.4.refs_13_), channel_id=1, source_target_pairs={{0,2},{1,3},{2,32},{3,33},{4,38},{5,39},{6,4},{7,5},{32,34},{33,35... | collective-permute-start | bytes 1572872 | tf_op jit(solution)/shard_map/ppermute | solution.py:558
  131.7 40.0 %collective-permute-start.16 = (f32[64,16,128]{2,1,0:T(8,128)}, f32[64,16,128]{2,1,0:T(8,128)}, u32[]{:S(2)}, u32[]{:S(2)}) collective-permute-start(f32[64,16,128]{2,1,0:T(8,128)} %pad_maximum_fusion.5.refs_14_), channel_id=1, source_target_pairs={{0,3},{1,32},{2,33},{3,34},{4,37},{5,38},{6,39},{7,4},{32,35},{33,... | collective-permute-start | bytes 1572872 | tf_op jit(solution)/shard_map/ppermute | solution.py:558
  140.4 35.7 %all-to-all-start.2 = ((f32[32,8,16,128]{3,2,1,0:T(8,128)}), f32[32,8,16,128]{3,2,1,0:T(8,128)}, u32[]{:S(2)}, u32[]{:S(2)}) async-start(f32[32,8,16,128]{3,2,1,0:T(8,128)} %convolve.3), calls=%async_computation.2 | async-start | bytes 4194304 | tf_op jit(solution)/shard_map/all_to_all | solution.py:570
  177.8 21.5 %collective-permute-start.18 = (f32[2,32,16,128]{3,2,1,0:T(8,128)S(1)}, f32[2,32,16,128]{3,2,1,0:T(8,128)S(1)}, u32[]{:S(2)}, u32[]{:S(2)}) collective-permute-start(f32[2,32,16,128]{3,2,1,0:T(8,128)S(1)} %get-tuple-element.40), channel_id=1, source_target_pairs={{0,1},{1,2},{2,3},{3,32},{4,39},{5,4},{6,5},{7,6},{32,33},{33,34},... | collective-permute-start | bytes 1572872 | tf_op jit(solution)/shard_map/ppermute | solution.py:558
  180.1 24.0 %collective-permute-start.19 = (f32[2,32,16,128]{3,2,1,0:T(8,128)S(1)}, f32[2,32,16,128]{3,2,1,0:T(8,128)S(1)}, u32[]{:S(2)}, u32[]{:S(2)}) collective-permute-start(f32[2,32,16,128]{3,2,1,0:T(8,128)S(1)} %get-tuple-element.41), channel_id=1, source_target_pairs={{0,2},{1,3},{2,32},{3,33},{4,38},{5,39},{6,4},{7,5},{32,34},{33,35... | collective-permute-start | bytes 1572872 | tf_op jit(solution)/shard_map/ppermute | solution.py:558
  181.6 43.4 %collective-permute-start.20 = (f32[2,32,16,128]{3,2,1,0:T(8,128)S(1)}, f32[2,32,16,128]{3,2,1,0:T(8,128)S(1)}, u32[]{:S(2)}, u32[]{:S(2)}) collective-permute-start(f32[2,32,16,128]{3,2,1,0:T(8,128)S(1)} %get-tuple-element.42), channel_id=1, source_target_pairs={{0,3},{1,32},{2,33},{3,34},{4,37},{5,38},{6,39},{7,4},{32,35},{33,... | collective-permute-start | bytes 1572872 | tf_op jit(solution)/shard_map/ppermute | solution.py:558
  182.9 16.5 %collective-permute-start.17 = (f32[32,16,128]{2,1,0:T(8,128)}, f32[32,16,128]{2,1,0:T(8,128)S(1)}, u32[]{:S(2)}, u32[]{:S(2)}) collective-permute-start(f32[32,16,128]{2,1,0:T(8,128)} %get-tuple-element.39), channel_id=1, source_target_pairs={{0,32},{1,33},{2,34},{3,35},{32,0},{33,1},{34,2},{35,3},{4,36},{5,... | collective-permute-start | bytes 786440 | tf_op jit(solution)/shard_map/ppermute | solution.py:562
  187.1 43.8 %all-to-all-start.3 = ((f32[32,8,16,128]{3,2,1,0:T(8,128)}), f32[32,8,16,128]{3,2,1,0:T(8,128)}, u32[]{:S(2)}, u32[]{:S(2)}) async-start(f32[32,8,16,128]{3,2,1,0:T(8,128)} %get-tuple-element.43), calls=%async_computation.3 | async-start | bytes 4194304 | tf_op jit(solution)/shard_map/all_to_all | solution.py:570
  225.1 9.0 %collective-permute-start.21 = (f32[3,32,16,128]{3,2,1,0:T(8,128)S(1)}, f32[3,32,16,128]{3,2,1,0:T(8,128)S(1)}, u32[]{:S(2)}, u32[]{:S(2)}) collective-permute-start(f32[3,32,16,128]{3,2,1,0:T(8,128)S(1)} %give.3.refs_2_), channel_id=1, source_target_pairs={{0,4},{4,0},{1,5},{5,1},{2,6},{6,2},{3,7},{7,3},{8,12},{12,8},{9,1... | collective-permute-start | bytes 2359304 | tf_op jit(solution)/shard_map/ppermute | solution.py:566
  (2 other events, 12.6 us)
